TPU v7x, 512 devices: a whole 4x8x8 slice. The times are simulated.
512 devices in a mesh: clip: 8 (over x, z_lo), frame: 4 (over z_hi), head: 16 (over y, core).
Axes of the slice: x: 4, y: 8, z: 8 (z_hi: 4, z_lo: 2; z = z_hi * 2 + z_lo), core: 2. Of those that a mesh axis runs over, the one named last changes fastest.
Arguments:
- residual: bfloat16 [8, 16, 32, 5120], P('clip', 'frame', None, 'head'), may hold values from -6 to 6
- projections: bfloat16 [8, 16, 32, 3, 4096], P('clip', 'frame', None, None, 'head'), may hold values from -8 to 8
- out_weight: bfloat16 [4096, 5120], P('head', 'frame'), may hold values from -0.1875 to 0.1875
- out_grad: bfloat16 [8, 16, 32, 5120], P('clip', 'frame', None, 'head'), may hold values from -6 to 6
Outputs:
- block_out: bfloat16 [8, 16, 32, 5120], P('clip', 'frame', None, 'head')
- qkv_grad: bfloat16 [8, 16, 32, 3, 4096], P('clip', 'frame', None, None, 'head')
- weight_grad: bfloat16 [4096, 5120], P('head', 'frame')
All inputs are finite; a program needn't handle non-finite values.
Results may differ from a plain program's by a relative error of at most 0.02.
Values may be sent and summed in bfloat16 or wider, within the bound.
No kernel may reach another device: no remote copies, remote signals or barrier semaphores. Data moves between devices by JAX's collectives and lax.ppermute only.
A program may use at most 64 MiB of HBM per device.

v0:
```python
import jax
import jax.numpy as jnp
from jax import lax
from jax.sharding import PartitionSpec as P

HEAD_DIM = 128


def attend(queries, key_rows, values):
    score_scale = queries.shape[-1] ** (-0.5)
    scores = (
        jnp.einsum("cfphe,cgphe->cphfg", queries, key_rows, preferred_element_type=jnp.float32)
        * score_scale
    )
    frame_index = jnp.arange(queries.shape[1])
    allowed = frame_index[:, None] >= frame_index[None, :]
    scores = jnp.where(allowed, scores, -jnp.inf)
    row_max = jnp.max(scores, axis=-1, keepdims=True)
    shifted = jnp.exp(scores - row_max)
    probability = shifted / jnp.sum(shifted, axis=-1, keepdims=True)
    weights = probability.astype(jnp.bfloat16)
    attended = jnp.einsum(
        "cphfg,cgphe->cfphe", weights, values, preferred_element_type=jnp.float32
    ).astype(jnp.bfloat16)
    return (probability, weights, attended)


def attend_back(queries, key_rows, values, probability, weights, grad_rows):
    score_scale = queries.shape[-1] ** (-0.5)
    prob_grad = jnp.einsum(
        "cfphe,cgphe->cphfg", grad_rows, values, preferred_element_type=jnp.float32
    )
    row_dot = jnp.sum(probability * prob_grad, axis=-1, keepdims=True)
    score_grad = (probability * (prob_grad - row_dot)).astype(jnp.bfloat16)
    query_grad = (
        jnp.einsum("cphfg,cgphe->cfphe", score_grad, key_rows, preferred_element_type=jnp.float32)
        * score_scale
    ).astype(jnp.bfloat16)
    key_grad = (
        jnp.einsum("cphfg,cfphe->cgphe", score_grad, queries, preferred_element_type=jnp.float32)
        * score_scale
    ).astype(jnp.bfloat16)
    value_grad = jnp.einsum(
        "cphfg,cfphe->cgphe", weights, grad_rows, preferred_element_type=jnp.float32
    ).astype(jnp.bfloat16)
    return (query_grad, key_grad, value_grad)


def local(residual, projections, out_weight, out_grad):
    patch_rows = lax.all_to_all(projections, "frame", split_axis=2, concat_axis=1, tiled=True)
    clip_count, frames, patches, _, inner_width = patch_rows.shape
    head_count = inner_width // HEAD_DIM
    heads_view = patch_rows.reshape(clip_count, frames, patches, 3, head_count, HEAD_DIM)
    queries = heads_view[:, :, :, 0]
    key_rows = heads_view[:, :, :, 1]
    values = heads_view[:, :, :, 2]
    probability, weights, attended = attend(queries, key_rows, values)
    attended_home = lax.all_to_all(
        attended.reshape(clip_count, frames, patches, inner_width),
        "frame",
        split_axis=1,
        concat_axis=2,
        tiled=True,
    )
    flat_rows = attended_home.reshape(-1, inner_width)
    weight_full = lax.all_gather(out_weight, "frame", axis=1, tiled=True)
    partial_out = jnp.dot(flat_rows, weight_full, preferred_element_type=jnp.float32)
    projected = lax.psum_scatter(
        partial_out.astype(jnp.bfloat16), "head", scatter_dimension=1, tiled=True
    ).astype(jnp.float32)
    block_out = (
        (residual.reshape(projected.shape).astype(jnp.float32) + projected)
        .astype(jnp.bfloat16)
        .reshape(residual.shape)
    )
    grad_full = lax.all_gather(out_grad, "head", axis=3, tiled=True)
    grad_flat = grad_full.reshape(flat_rows.shape[0], -1)
    attended_grad = lax.dot_general(
        grad_flat, weight_full, (((1,), (1,)), ((), ())), preferred_element_type=jnp.float32
    ).astype(jnp.bfloat16)
    grad_part = lax.dot_general(
        flat_rows, grad_flat, (((0,), (0,)), ((), ())), preferred_element_type=jnp.float32
    )
    frame_share = lax.psum_scatter(
        grad_part.astype(jnp.bfloat16), "frame", scatter_dimension=1, tiled=True
    )
    weight_grad = lax.psum(frame_share, "clip")
    grad_home = lax.all_to_all(
        attended_grad.reshape(attended_home.shape), "frame", split_axis=2, concat_axis=1, tiled=True
    )
    grad_rows = grad_home.reshape(clip_count, frames, patches, head_count, HEAD_DIM)
    query_grad, key_grad, value_grad = attend_back(
        queries, key_rows, values, probability, weights, grad_rows
    )
    stacked = jnp.stack([query_grad, key_grad, value_grad], axis=3).reshape(
        clip_count, frames, patches, 3, inner_width
    )
    qkv_grad = lax.all_to_all(stacked, "frame", split_axis=1, concat_axis=2, tiled=True)
    return (block_out, qkv_grad, weight_grad)


def solution(mesh):
    in_specs = (
        P("clip", "frame", None, "head"),
        P("clip", "frame", None, None, "head"),
        P("head", "frame"),
        P("clip", "frame", None, "head"),
    )
    out_specs = (
        P("clip", "frame", None, "head"),
        P("clip", "frame", None, None, "head"),
        P("head", "frame"),
    )
    return jax.shard_map(local, mesh=mesh, in_specs=in_specs, out_specs=out_specs, check_vma=False)
```

profile of v0, /device:TPU:16, one launch (start us, length us, event | category | flops | bytes accessed | tf_op | source)
XLA Modules:
  0.0 347.7 jit_solution(10752715296655188290)
XLA Ops:
  7.2 0.0 all-gather.5.cloned.1.call-start
  7.2 1.8 copy.102
  9.0 0.0 all-gather.5.cloned.1.call-update
  9.1 0.0 all-gather.3.cloned.1.call-start
  9.1 0.7 all-gather.3.cloned.1.call-update
  9.8 1.8 copy.91
  11.6 10.3 %all-to-all-start = ((bf16[1,4,32,3,256]{4,1,3,0,2:T(4,128)(2,1)}), bf16[1,4,32,3,256]{4,1,3,0,2:T(4,128)(2,1)S(1)}, u32[]{:S(2)}, u32[]{:S(2)}) async-start(bf16[1,4,32,3,256]{4,1,3,0,2:T(4,128)(2,1)} %copy.91), calls=%async_computation | async-start | bytes 393216 | tf_op jit(solution)/shard_map/all_to_all | solution.py:50
  21.9 0.0 reduce-scatter.5.cloned.1.call-start
  21.9 9.9 %all-to-all-done = bf16[1,4,32,3,256]{4,1,3,0,2:T(4,128)(2,1)S(1)} async-done(((bf16[1,4,32,3,256]{4,1,3,0,2:T(4,128)(2,1)}), bf16[1,4,32,3,256]{4,1,3,0,2:T(4,128)(2,1)S(1)}, u32[]{:S(2)}, u32[]{:S(2)}) %all-to-all-start) | async-done | bytes 196640 | tf_op jit(solution)/shard_map/all_to_all | solution.py:50
  31.8 0.1 reshape.109
  31.9 0.1 fusion.15
  32.0 0.2 fusion.16
  32.3 0.2 fusion.6
  32.5 10.8 %all_to_all.63 = bf16[1,16,8,256]{3,2,0,1:T(8,128)(2,1)S(1)} all-to-all(bf16[1,16,8,256]{3,2,0,1:T(8,128)(2,1)S(1)} %bitcast.98), channel_id=1, replica_groups=mesh['clip'=8,'frame'=4,'head'=16] {'frame'}, dimensions={1} | all-to-all | bytes 131072 | tf_op jit(solution)/shard_map/all_to_all | solution.py:58
  43.3 17.1 %all-gather.5.cloned.1.call-done = bf16[1,4,32,5120]{2,1,0,3:T(4,128)(2,1)} async-done(((bf16[1,4,32,320]{2,1,0,3:T(4,128)(2,1)}), bf16[1,4,32,5120]{2,1,0,3:T(4,128)(2,1)}) %all-gather.5.cloned.1.call-update) | async-done | bytes 1310736 | tf_op jit(solution)/shard_map/all_gather | solution.py:76
  60.4 6.0 %copy.103 = bf16[1,4,32,5120]{3,2,1,0:T(8,128)(2,1)S(1)} copy(bf16[1,4,32,5120]{2,1,0,3:T(4,128)(2,1)} %all-gather.5.cloned.1.call-done) | data formatting | bytes 2621440 | tf_op jit(solution)/shard_map/all_gather | solution.py:76
  66.4 2.4 convolution_convert_fusion
  68.8 0.0 reduce-scatter.5.cloned.1.call-update
  68.8 0.0 reduce-scatter.3.cloned.1.call-start
  68.9 56.7 %all-gather.3.cloned.1.call-done = bf16[256,5120]{1,0:T(8,128)(2,1)} async-done(((bf16[256,1280]{1,0:T(8,128)(2,1)}), bf16[256,5120]{1,0:T(8,128)(2,1)}) %all-gather.3.cloned.1.call-update) | async-done | bytes 2621456 | tf_op jit(solution)/shard_map/all_gather | solution.py:66
  125.6 4.0 %convolution_convert_fusion.1 = bf16[128,5120]{0,1:T(8,128)(2,1)} fusion(bf16[128,256]{1,0:T(8,128)(2,1)S(1)} %bitcast.96, bf16[256,5120]{1,0:T(8,128)(2,1)} %all-gather.3.cloned.1.call-done), kind=kOutput, calls=%fused_computation.2 | convolution fusion | flops 336199680 | bytes 3997696 | tf_op jit(solution)/shard_map/dot_general | solution.py:67
  129.6 0.0 reduce-scatter.3.cloned.1.call-update
  129.6 0.0 all-reduce.2.cloned.1.call-start
  129.7 2.7 convolution_convert_fusion.2
  132.4 0.0 copy-start
  132.4 0.1 copy.104
  132.5 12.2 %all_to_all.64 = bf16[1,4,32,256]{3,1,0,2:T(4,128)(2,1)S(1)} all-to-all(bf16[1,4,32,256]{3,1,0,2:T(4,128)(2,1)S(1)} %copy.104), channel_id=1, replica_groups=mesh['clip'=8,'frame'=4,'head'=16] {'frame'}, dimensions={2} | all-to-all | bytes 131072 | tf_op jit(solution)/shard_map/all_to_all | solution.py:88
  144.7 0.2 multiply_reduce_fusion
  144.9 0.2 fusion.9
  145.1 0.2 fusion.8
  145.4 41.9 %reduce-scatter.5.cloned.1.call-done = bf16[256,1280]{1,0:T(8,128)(2,1)} async-done(((bf16[256,5120]{1,0:T(8,128)(2,1)}), bf16[256,1280]{1,0:T(8,128)(2,1)}) %reduce-scatter.5.cloned.1.call-update) | async-done | bytes 655376 | tf_op jit(solution)/shard_map/reduce_scatter | solution.py:84
  187.3 0.0 all-reduce.2.cloned.1.call-update
  187.3 0.2 fusion.7
  187.5 0.7 copy.113
  188.2 5.6 %all-to-all-start.3 = ((bf16[1,16,8,3,256]{4,2,3,0,1:T(8,128)(2,1)}), bf16[1,16,8,3,256]{4,2,3,0,1:T(8,128)(2,1)S(1)}, u32[]{:S(2)}, u32[]{:S(2)}) async-start(bf16[1,16,8,3,256]{4,2,3,0,1:T(8,128)(2,1)} %copy.113), calls=%async_computation.4 | async-start | bytes 393216 | tf_op jit(solution)/shard_map/all_to_all | solution.py:98
  193.8 0.0 copy-done
  193.8 0.1 copy.100
  193.9 10.0 %all-to-all-done.3 = bf16[1,16,8,3,256]{4,2,3,0,1:T(8,128)(2,1)S(1)} async-done(((bf16[1,16,8,3,256]{4,2,3,0,1:T(8,128)(2,1)}), bf16[1,16,8,3,256]{4,2,3,0,1:T(8,128)(2,1)S(1)}, u32[]{:S(2)}, u32[]{:S(2)}) %all-to-all-start.3) | async-done | bytes 196640 | tf_op jit(solution)/shard_map/all_to_all | solution.py:98
  204.0 0.7 copy.148
  204.7 40.5 %reduce-scatter.3.cloned.1.call-done = bf16[128,320]{0,1:T(8,128)(2,1)} async-done(((bf16[128,5120]{0,1:T(8,128)(2,1)}), bf16[128,320]{0,1:T(8,128)(2,1)}) %reduce-scatter.3.cloned.1.call-update) | async-done | bytes 81936 | tf_op jit(solution)/shard_map/reduce_scatter | solution.py:68
  245.1 0.9 add_convert_fusion
  246.0 0.8 copy.101
  246.8 92.5 %all-reduce.2.cloned.1.call-done = bf16[256,1280]{1,0:T(8,128)(2,1)} async-done(((bf16[256,1280]{1,0:T(8,128)(2,1)}), bf16[256,1280]{1,0:T(8,128)(2,1)}) %all-reduce.2.cloned.1.call-update) | async-done | bytes 655376 | tf_op jit(solution)/shard_map/psum | solution.py:87
  339.2 2.0 copy.154
  (11 shorter events, 0.2 us)
Async XLA Ops:
  7.2 53.2 %all-gather.5.cloned.1.call-start = ((), (), s32[]{:S(2)}) async-start(), calls=%async_computation.8 | async-start | bytes 5570560 | tf_op jit(solution)/shard_map/all_gather | solution.py:76
  9.1 116.6 %all-gather.3.cloned.1.call-start = ((), (), s32[]{:S(2)}) async-start(), calls=%async_computation.6 | async-start | bytes 3276800 | tf_op jit(solution)/shard_map/all_gather | solution.py:66
  11.6 20.2 %all-to-all-start = ((bf16[1,4,32,3,256]{4,1,3,0,2:T(4,128)(2,1)}), bf16[1,4,32,3,256]{4,1,3,0,2:T(4,128)(2,1)S(1)}, u32[]{:S(2)}, u32[]{:S(2)}) async-start(bf16[1,4,32,3,256]{4,1,3,0,2:T(4,128)(2,1)} %copy.91), calls=%async_computation | async-start | bytes 393216 | tf_op jit(solution)/shard_map/all_to_all | solution.py:50
  21.9 165.4 %reduce-scatter.5.cloned.1.call-start = ((), (), s32[]{:S(2)}) async-start(), calls=%async_computation.9 | async-start | bytes 3276800 | tf_op jit(solution)/shard_map/reduce_scatter | solution.py:84
  68.8 176.3 %reduce-scatter.3.cloned.1.call-start = ((), (), s32[]{:S(2)}) async-start(), calls=%async_computation.7 | async-start | bytes 1392640 | tf_op jit(solution)/shard_map/reduce_scatter | solution.py:68
  129.6 209.6 %all-reduce.2.cloned.1.call-start = ((), (), s32[]{:S(2)}) async-start(), calls=%async_computation.10 | async-start | bytes 1310720 | tf_op jit(solution)/shard_map/psum | solution.py:87
  132.4 61.4 %copy-start = (bf16[1,4,32,320]{3,2,1,0:T(8,128)(2,1)S(1)}, bf16[1,4,32,320]{3,2,1,0:T(8,128)(2,1)}, u32[]{:S(2)}) copy-start(bf16[1,4,32,320]{3,2,1,0:T(8,128)(2,1)} %param.4) | copy-start | bytes 245764
  188.2 15.7 %all-to-all-start.3 = ((bf16[1,16,8,3,256]{4,2,3,0,1:T(8,128)(2,1)}), bf16[1,16,8,3,256]{4,2,3,0,1:T(8,128)(2,1)S(1)}, u32[]{:S(2)}, u32[]{:S(2)}) async-start(bf16[1,16,8,3,256]{4,2,3,0,1:T(8,128)(2,1)} %copy.113), calls=%async_computation.4 | async-start | bytes 393216 | tf_op jit(solution)/shard_map/all_to_all | solution.py:98
Sparse Core Ops, SparseCore 0:
  10.7 49.6 all-gather.4
  62.5 63.0 all-gather.2
  128.5 58.7 reduce-scatter.4
  190.0 55.1 reduce-scatter.2
  247.9 91.2 all-reduce.1
where the time goes:
time: 349 us; the launch traced here: 348 us
  waiting for transfers between devices  269 us (77%)
  blocking collectives  23 us (7%)
  starting transfers between devices  16 us (5%)
  local copies, waits for them, and re-layouts  14.2 us (4%)
  between operations  13.9 us (4%)
  matrix products  10.3 us (3%)
    psum x1, waiting for transfers between devices, local(): weight_grad = lax.psum(frame_share, 'clip')  92.5 us
    all_gather x1, waiting for transfers between devices, local(): weight_full = lax.all_gather(out_weight, 'frame', axis=1, tiled=True)  56.7 us
    reduce_scatter x1, waiting for transfers between devices, local(): lax.psum_scatter(grad_part.astype(jnp.bfloat16), 'frame', scatter_dimensi...  41.9 us
    reduce_scatter x1, waiting for transfers between devices, local(): lax.psum_scatter(partial_out.astype(jnp.bfloat16), 'head', scatter_dimens...  40.5 us
    all_gather x1, waiting for transfers between devices, local(): grad_full = lax.all_gather(out_grad, 'head', axis=3, tiled=True)  17.1 us
    all_to_all x1, blocking collectives, local(): lax.all_to_all(attended_grad.reshape(attended_home.shape), 'frame', split...  12.2 us
    all_to_all x1, blocking collectives, local(): lax.all_to_all(attended.reshape(clip_count, frames, patches, inner_width)...  10.8 us
    all_to_all x1, starting transfers between devices, local(): lax.all_to_all(projections, 'frame', split_axis=2, concat_axis=1, tiled=T...  10.3 us
  transfers between devices with their start and end apart: 7, of which 7 were waited for; matrix products, arithmetic and copies ran while one was open for 6% of the time, Pallas kernels for 0%

commit v1 on v0

v1 whole, which is shorter than its diff:
```python
import jax
import jax.numpy as jnp
from jax import lax
from jax.experimental import pallas as pl
from jax.experimental.pallas import tpu as pltpu
from jax.sharding import Mesh, PartitionSpec as P

HEAD_DIM = 128
AXES = ("x", "zl", "frame", "y", "core")
CLIP = ("x", "zl")
SWAP = ((0, 1), (1, 0))
F32 = jnp.float32
BF16 = jnp.bfloat16


def probabilities(queries, key_rows, patches):
    rows = queries.shape[0]
    scores = lax.dot_general(
        queries, key_rows, (((1,), (1,)), ((), ())), preferred_element_type=F32
    ) * (HEAD_DIM ** (-0.5))
    at = lax.broadcasted_iota(jnp.int32, (rows, rows), 0)
    to = lax.broadcasted_iota(jnp.int32, (rows, rows), 1)
    allowed = (at % patches == to % patches) & (at >= to)
    scores = jnp.where(allowed, scores, -jnp.inf)
    shifted = jnp.exp(scores - jnp.max(scores, axis=-1, keepdims=True))
    return shifted / jnp.sum(shifted, axis=-1, keepdims=True)


def attend_kernel(patches, qkv_ref, attended_ref):
    width = attended_ref.shape[1]
    for at in range(0, width, HEAD_DIM):
        queries = qkv_ref[:, at : at + HEAD_DIM]
        key_rows = qkv_ref[:, width + at : width + at + HEAD_DIM]
        values = qkv_ref[:, 2 * width + at : 2 * width + at + HEAD_DIM]
        weights = probabilities(queries, key_rows, patches).astype(BF16)
        attended_ref[:, at : at + HEAD_DIM] = jnp.dot(
            weights, values, preferred_element_type=F32
        ).astype(BF16)


def attend_back_kernel(patches, qkv_ref, shares_ref, grads_ref):
    width = shares_ref.shape[2]
    grad_rows = jnp.sum(shares_ref[...].astype(F32), axis=0).astype(BF16)
    score_scale = HEAD_DIM ** (-0.5)
    for at in range(0, width, HEAD_DIM):
        queries = qkv_ref[:, at : at + HEAD_DIM]
        key_rows = qkv_ref[:, width + at : width + at + HEAD_DIM]
        values = qkv_ref[:, 2 * width + at : 2 * width + at + HEAD_DIM]
        grad = grad_rows[:, at : at + HEAD_DIM]
        probability = probabilities(queries, key_rows, patches)
        prob_grad = lax.dot_general(
            grad, values, (((1,), (1,)), ((), ())), preferred_element_type=F32
        )
        row_dot = jnp.sum(probability * prob_grad, axis=-1, keepdims=True)
        score_grad = (probability * (prob_grad - row_dot)).astype(BF16)
        query_grad = jnp.dot(score_grad, key_rows, preferred_element_type=F32) * score_scale
        key_grad = (
            lax.dot_general(
                score_grad, queries, (((0,), (0,)), ((), ())), preferred_element_type=F32
            )
            * score_scale
        )
        value_grad = lax.dot_general(
            probability.astype(BF16), grad, (((0,), (0,)), ((), ())), preferred_element_type=F32
        )
        for part, value in enumerate((query_grad, key_grad, value_grad)):
            start = part * width + at
            grads_ref[:, start : start + HEAD_DIM] = value.astype(BF16)


def whole(kernel, out_shape, *operands):
    return pl.pallas_call(
        kernel,
        out_shape=out_shape,
        compiler_params=pltpu.CompilerParams(vmem_limit_bytes=32 * 1024 * 1024),
    )(*operands)


def local(residual, projections, out_weight, out_grad):
    n_frame, n_y = lax.axis_size("frame"), lax.axis_size("y")
    n_clip = lax.axis_size("x") * lax.axis_size("zl")
    core = lax.axis_index("core")
    _, steps, patches, _, inner = projections.shape
    width = out_grad.shape[-1]
    own_patches = patches // n_frame
    rows = steps * n_frame * own_patches
    tokens = steps * patches
    halves = n_y // n_frame

    weight_t = out_weight.T.reshape(halves, 2, width, inner)
    weight_keep = lax.dynamic_index_in_dim(weight_t, core, 1, keepdims=False)
    weight_give = lax.dynamic_index_in_dim(weight_t, 1 - core, 1, keepdims=False)
    weight_got = lax.ppermute(weight_give, "core", SWAP)
    first = jnp.where(core == 0, weight_keep, weight_got)
    second = jnp.where(core == 0, weight_got, weight_keep)
    weight_rows = jnp.concatenate([first, second], axis=-1).reshape(halves * width, 2 * inner)

    there = [
        (f * n_y + y, (y // halves) * n_y + halves * f + y % halves)
        for f in range(n_frame)
        for y in range(n_y)
    ]
    back = [(b, a) for a, b in there]

    grad_t = (
        out_grad.reshape(steps, n_frame, own_patches, width)
        .transpose(3, 1, 0, 2)
        .reshape(width, tokens)
    )
    grad_moved = lax.ppermute(grad_t, ("frame", "y"), back)
    grad_all = lax.all_gather(grad_moved, ("y", "core"))
    grad_all = grad_all.reshape(n_frame, halves, 2, width, tokens)

    sent = (
        projections.reshape(steps, n_frame, own_patches, 3 * inner)
        .transpose(1, 0, 2, 3)
    )
    qkv = lax.all_to_all(sent, "frame", 0, 0, tiled=True).reshape(rows, 3 * inner)
    attended = whole(
        lambda *refs: attend_kernel(own_patches, *refs),
        jax.ShapeDtypeStruct((rows, inner), BF16),
        qkv,
    )
    attended_all = lax.all_gather(attended, ("frame", "core"))
    group = tokens // n_frame
    attended_all = attended_all.reshape(n_frame, 2, n_frame, group, inner)
    feature_rows = attended_all.transpose(2, 0, 3, 1, 4).reshape(n_frame * tokens, 2 * inner)

    partial = lax.dot_general(
        weight_rows, feature_rows, (((1,), (1,)), ((), ())), preferred_element_type=F32
    ).astype(BF16)
    pieces = (
        partial.reshape(halves, width, n_frame, tokens)
        .transpose(2, 0, 1, 3)
        .reshape(n_y, width, tokens)
    )
    pieces = lax.all_to_all(pieces, "y", 0, 0, tiled=True)
    projected = jnp.sum(pieces.astype(F32), axis=0).astype(BF16)
    projected = lax.ppermute(projected, ("frame", "y"), there)
    projected = (
        projected.reshape(width, n_frame, steps, own_patches)
        .transpose(2, 1, 3, 0)
        .reshape(residual.shape)
    )
    block_out = (residual.astype(F32) + projected.astype(F32)).astype(BF16)

    grad_own = lax.dynamic_index_in_dim(grad_all, core, 2, keepdims=False)
    grad_own = grad_own.transpose(1, 2, 0, 3).reshape(halves * width, n_frame * tokens)
    share = lax.dot_general(
        grad_own, weight_rows, (((0,), (0,)), ((), ())), preferred_element_type=F32
    ).astype(BF16)
    share = (
        share.reshape(n_frame, n_frame, group, 2, inner)
        .transpose(1, 3, 0, 2, 4)
        .reshape(2 * n_frame, rows, inner)
    )
    shares = lax.all_to_all(share, ("frame", "core"), 0, 0, tiled=True)

    own_rows = lax.dynamic_index_in_dim(
        feature_rows.reshape(n_frame * tokens, 2, inner), core, 1, keepdims=False
    )
    grad_rows = grad_all.transpose(0, 4, 1, 2, 3).reshape(n_frame * tokens, -1)
    weight_part = lax.dot_general(
        own_rows, grad_rows, (((0,), (0,)), ((), ())), preferred_element_type=F32
    ).astype(BF16)
    weight_part = weight_part.reshape(n_clip, inner // n_clip, -1)
    weight_part = lax.all_to_all(weight_part, CLIP, 0, 0, tiled=True)
    weight_sum = jnp.sum(weight_part.astype(F32), axis=0).astype(BF16)
    weight_sum = jnp.broadcast_to(weight_sum[None], (n_clip, *weight_sum.shape))
    weight_grad = lax.all_to_all(weight_sum, CLIP, 0, 0, tiled=True).reshape(out_weight.shape)

    grads = whole(
        lambda *refs: attend_back_kernel(own_patches, *refs),
        jax.ShapeDtypeStruct((rows, 3 * inner), BF16),
        qkv,
        shares,
    )
    grads = grads.reshape(n_frame, steps, own_patches, 3 * inner)
    grads = lax.all_to_all(grads, "frame", 0, 0, tiled=True)
    qkv_grad = grads.transpose(1, 0, 2, 3).reshape(projections.shape)
    return (block_out, qkv_grad, weight_grad)


def solution(mesh):
    n_clip, n_frame, n_head = mesh.devices.shape
    fine = Mesh(mesh.devices.reshape(n_clip // 2, 2, n_frame, n_head // 2, 2), AXES)
    head = ("y", "core")
    in_specs = (
        P(CLIP, "frame", None, head),
        P(CLIP, "frame", None, None, head),
        P(head, "frame"),
        P(CLIP, "frame", None, head),
    )
    out_specs = (
        P(CLIP, "frame", None, head),
        P(CLIP, "frame", None, None, head),
        P(head, "frame"),
    )
    return jax.shard_map(local, mesh=fine, in_specs=in_specs, out_specs=out_specs, check_vma=False)
```

time: 349 us -> 166 us (0.48)
  the two profiles are of different devices: /device:TPU:16 before, /device:TPU:42 now
where the time goes in v1:
time: 166 us
  waiting for transfers between devices  63.1 us (38%)
  starting transfers between devices  55.2 us (33%)
  blocking collectives  14.9 us (9%)
  between operations  14.2 us (9%)
  local copies, waits for them, and re-layouts  12.1 us (7%)
  matrix products  2.54 us (2%)
  Pallas kernels  2.47 us (1%)
    all_gather x1, blocking collectives, local(): attended_all = lax.all_gather(attended, ('frame', 'core'))  14.9 us
    all_to_all x1, waiting for transfers between devices, local(): shares = lax.all_to_all(share, ('frame', 'core'), 0, 0, tiled=True)  14 us
    all_to_all x1, waiting for transfers between devices, local(): pieces = lax.all_to_all(pieces, 'y', 0, 0, tiled=True)  13.7 us
    all_to_all x1, starting transfers between devices, local(): pieces = lax.all_to_all(pieces, 'y', 0, 0, tiled=True)  11.8 us
    ppermute x1, starting transfers between devices, local(): grad_moved = lax.ppermute(grad_t, ('frame', 'y'), back)  11.4 us
    ppermute x1, waiting for transfers between devices, local(): projected = lax.ppermute(projected, ('frame', 'y'), there)  9.12 us
    all_to_all x1, waiting for transfers between devices, local(): grads = lax.all_to_all(grads, 'frame', 0, 0, tiled=True)  9.1 us
    all_to_all x1, waiting for transfers between devices, local(): lax.all_to_all(sent, 'frame', 0, 0, tiled=True).reshape(rows, 3 * inner)  6.84 us
  transfers between devices with their start and end apart: 10, of which 7 were waited for; matrix products, arithmetic and copies ran while one was open for 7% of the time, Pallas kernels for 1%

profile of v1, /device:TPU:42, one launch (start us, length us, event | category | flops | bytes accessed | tf_op | source)
XLA Modules:
  0.0 165.5 jit_solution(4202269671006108538)
XLA Ops:
  7.2 0.0 all-gather.4.cloned.1.call-start
  7.2 1.0 copy.55
  8.2 11.4 %collective-permute-start.2 = (bf16[320,128]{0,1:T(8,128)(2,1)S(1)}, bf16[320,128]{0,1:T(8,128)(2,1)S(1)}, u32[]{:S(2)}, u32[]{:S(2)}) collective-permute-start(bf16[320,128]{0,1:T(8,128)(2,1)S(1)} %bitcast.89), channel_id=1, source_target_pairs={{0,0},{2,2},{16,4},{18,6},{32,8},{34,10},{48,12},{50,14},{4,16},{6... | collective-permute-start | bytes 245768 | tf_op jit(solution)/shard_map/ppermute | solution.py:110
  19.6 3.9 %collective-permute-done.2 = bf16[320,128]{0,1:T(8,128)(2,1)S(1)} collective-permute-done((bf16[320,128]{0,1:T(8,128)(2,1)S(1)}, bf16[320,128]{0,1:T(8,128)(2,1)S(1)}, u32[]{:S(2)}, u32[]{:S(2)}) %collective-permute-start.2) | collective-permute-done | bytes 81952 | tf_op jit(solution)/shard_map/ppermute | solution.py:110
  23.4 0.7 copy.56
  24.2 0.0 all-gather.4.cloned.1.call-update
  24.2 1.1 copy.48
  25.3 0.2 reshape.84
  25.5 0.7 copy.49
  26.2 6.0 %all-to-all-start = ((bf16[4,4,8,768]{3,2,1,0:T(8,128)(2,1)}), bf16[4,4,8,768]{3,2,1,0:T(8,128)(2,1)S(1)}, u32[]{:S(2)}, u32[]{:S(2)}) async-start(bf16[4,4,8,768]{3,2,1,0:T(8,128)(2,1)} %copy.49), calls=%async_computation | async-start | bytes 393216 | tf_op jit(solution)/shard_map/all_to_all | solution.py:118
  32.2 0.2 copy.47
  32.5 1.9 %collective-permute-start = (bf16[2,320,256]{2,1,0:T(8,128)(2,1)S(1)}, bf16[2,320,256]{2,1,0:T(8,128)(2,1)S(1)}, u32[]{:S(2)}, u32[]{:S(2)}) collective-permute-start(bf16[2,320,256]{2,1,0:T(8,128)(2,1)S(1)} %dynamic-slice_bitcast_fusion.1), channel_id=1, source_target_pairs={{0,1},{1,0},{2,3},{3,2},{4,5},{5,4},{6,7},{7,6},{8,9},{9,8},{10,11... | collective-permute-start | bytes 983048 | tf_op jit(solution)/shard_map/ppermute | solution.py:93
  34.4 6.8 %all-to-all-done = bf16[4,4,8,768]{3,2,1,0:T(8,128)(2,1)S(1)} async-done(((bf16[4,4,8,768]{3,2,1,0:T(8,128)(2,1)}), bf16[4,4,8,768]{3,2,1,0:T(8,128)(2,1)S(1)}, u32[]{:S(2)}, u32[]{:S(2)}) %all-to-all-start) | async-done | bytes 196640 | tf_op jit(solution)/shard_map/all_to_all | solution.py:118
  41.2 0.8 shard_map.67
  42.0 14.9 %all-gather = bf16[1024,256]{1,0:T(8,128)(2,1)S(1)} all-gather(bf16[128,256]{1,0:T(8,128)(2,1)S(1)} %shard_map.67), channel_id=2, replica_groups=mesh['x'=4,'zl'=2,'frame'=4,'y'=8,'core'=2] {'frame','core'}, dimensions={0}, use_global_device_ids=true | all-gather | bytes 589824 | tf_op jit(solution)/shard_map/all_gather | solution.py:124
  56.9 0.5 copy.51
  57.5 0.1 copy.63
  57.6 0.1 bitcast_select_fusion.1
  57.7 0.5 convolution_convert_fusion.1
  58.3 0.2 reshape.88
  58.4 0.9 copy.52
  59.4 11.8 %all-to-all-start.1 = ((bf16[8,320,128]{2,1,0:T(8,128)(2,1)}), bf16[8,320,128]{2,1,0:T(8,128)(2,1)S(1)}, u32[]{:S(2)}, u32[]{:S(2)}) async-start(bf16[8,320,128]{2,1,0:T(8,128)(2,1)} %bitcast.12), calls=%async_computation.1 | async-start | bytes 1310720 | tf_op jit(solution)/shard_map/all_to_all | solution.py:137
  71.2 1.1 dynamic-slice_bitcast_fusion
  72.3 0.5 copy.57
  72.8 0.6 convolution_convert_fusion.2
  73.4 0.1 reshape.94
  73.6 0.9 copy.58
  74.5 13.7 %all-to-all-done.1 = bf16[8,320,128]{2,1,0:T(8,128)(2,1)S(1)} async-done(((bf16[8,320,128]{2,1,0:T(8,128)(2,1)}), bf16[8,320,128]{2,1,0:T(8,128)(2,1)S(1)}, u32[]{:S(2)}, u32[]{:S(2)}) %all-to-all-start.1) | async-done | bytes 655392 | tf_op jit(solution)/shard_map/all_to_all | solution.py:137
  88.2 3.6 %all-to-all-start.2 = ((bf16[8,128,256]{2,1,0:T(8,128)(2,1)}), bf16[8,128,256]{2,1,0:T(8,128)(2,1)S(1)}, u32[]{:S(2)}, u32[]{:S(2)}) async-start(bf16[8,128,256]{2,1,0:T(8,128)(2,1)} %bitcast.77), calls=%async_computation.2 | async-start | bytes 1048576 | tf_op jit(solution)/shard_map/all_to_all | solution.py:157
  91.9 1.0 copy.60
  92.9 1.4 convolution_convert_fusion
  94.3 14.0 %all-to-all-done.2.refs_1_ = bf16[8,128,256]{2,1,0:T(8,128)(2,1)S(1)} async-done(((bf16[8,128,256]{2,1,0:T(8,128)(2,1)}), bf16[8,128,256]{2,1,0:T(8,128)(2,1)S(1)}, u32[]{:S(2)}, u32[]{:S(2)}) %all-to-all-start.2) | async-done | bytes 524320 | tf_op jit(solution)/shard_map/all_to_all | solution.py:157
  108.3 6.0 %all-to-all-start.4 = ((bf16[8,32,1280]{2,1,0:T(8,128)(2,1)}), bf16[8,32,1280]{2,1,0:T(8,128)(2,1)S(1)}, u32[]{:S(2)}, u32[]{:S(2)}) async-start(bf16[8,32,1280]{2,1,0:T(8,128)(2,1)} %bitcast.29), calls=%async_computation.4 | async-start | bytes 1310720 | tf_op jit(solution)/shard_map/all_to_all | solution.py:167
  114.3 1.7 %shard_map.68 = bf16[128,768]{1,0:T(8,128)(2,1)} custom-call(bf16[128,768]{1,0:T(8,128)(2,1)S(1)} %bitcast.69, bf16[8,128,256]{2,1,0:T(8,128)(2,1)S(1)} %all-to-all-done.2.refs_1_), custom_call_target="tpu_custom_call" | custom-call | tf_op jit(solution)/shard_map/pallas_call | solution.py:72
  116.1 6.4 %all-to-all-done.4 = bf16[8,32,1280]{2,1,0:T(8,128)(2,1)S(1)} async-done(((bf16[8,32,1280]{2,1,0:T(8,128)(2,1)}), bf16[8,32,1280]{2,1,0:T(8,128)(2,1)S(1)}, u32[]{:S(2)}, u32[]{:S(2)}) %all-to-all-start.4) | async-done | bytes 655392 | tf_op jit(solution)/shard_map/all_to_all | solution.py:167
  122.5 3.4 %all-to-all-start.3 = ((bf16[4,4,8,768]{3,2,1,0:T(8,128)(2,1)}), bf16[4,4,8,768]{3,2,1,0:T(8,128)(2,1)S(1)}, u32[]{:S(2)}, u32[]{:S(2)}) async-start(bf16[4,4,8,768]{3,2,1,0:T(8,128)(2,1)} %bitcast.24), calls=%async_computation.3 | async-start | bytes 393216 | tf_op jit(solution)/shard_map/all_to_all | solution.py:179
  125.8 0.1 reduce_sum.25
  125.9 9.1 %all-to-all-done.3 = bf16[4,4,8,768]{3,2,1,0:T(8,128)(2,1)S(1)} async-done(((bf16[4,4,8,768]{3,2,1,0:T(8,128)(2,1)}), bf16[4,4,8,768]{3,2,1,0:T(8,128)(2,1)S(1)}, u32[]{:S(2)}, u32[]{:S(2)}) %all-to-all-start.3) | async-done | bytes 196640 | tf_op jit(solution)/shard_map/all_to_all | solution.py:179
  135.0 0.9 broadcast_in_dim.2
  135.9 5.2 %all-to-all-start.5 = ((bf16[8,32,1280]{2,1,0:T(8,128)(2,1)}), bf16[8,32,1280]{2,1,0:T(8,128)(2,1)S(1)}, u32[]{:S(2)}, u32[]{:S(2)}) async-start(bf16[8,32,1280]{2,1,0:T(8,128)(2,1)} %broadcast_in_dim.2), calls=%async_computation.5 | async-start | bytes 1310720 | tf_op jit(solution)/shard_map/all_to_all | solution.py:170
  141.1 0.1 reduce_sum.24
  141.2 5.9 %collective-permute-start.1 = (bf16[320,128]{1,0:T(8,128)(2,1)S(1)}, bf16[320,128]{1,0:T(8,128)(2,1)S(1)}, u32[]{:S(2)}, u32[]{:S(2)}) collective-permute-start(bf16[320,128]{1,0:T(8,128)(2,1)S(1)} %reduce_sum.24), channel_id=1, source_target_pairs={{0,0},{2,2},{4,16},{6,18},{8,32},{10,34},{12,48},{14,50},{16,4},{1... | collective-permute-start | bytes 245768 | tf_op jit(solution)/shard_map/ppermute | solution.py:139
  147.1 9.1 %collective-permute-done.1 = bf16[320,128]{1,0:T(8,128)(2,1)S(1)} collective-permute-done((bf16[320,128]{1,0:T(8,128)(2,1)S(1)}, bf16[320,128]{1,0:T(8,128)(2,1)S(1)}, u32[]{:S(2)}, u32[]{:S(2)}) %collective-permute-start.1) | collective-permute-done | bytes 81952 | tf_op jit(solution)/shard_map/ppermute | solution.py:139
  156.3 0.1 copy.53
  156.4 0.7 fusion.6
  157.1 0.1 reshape.97
  157.2 0.7 copy.61
  157.9 0.8 copy.76
  (13 shorter events, 0.1 us)
Async XLA Ops:
  7.2 25.0 %copy-start.1 = (bf16[256,1280]{1,0:T(8,128)(2,1)S(1)}, bf16[256,1280]{1,0:T(8,128)(2,1)}, u32[]{:S(2)}) copy-start(bf16[256,1280]{1,0:T(8,128)(2,1)} %param.6) | copy-start | bytes 1966084
  7.2 64.0 %all-gather.4.cloned.1.call-start = ((), (), s32[]{:S(2)}) async-start(), calls=%async_computation.6 | async-start | bytes 1392640 | tf_op jit(solution)/shard_map/all_gather | solution.py:111
  8.2 15.2 %collective-permute-start.2 = (bf16[320,128]{0,1:T(8,128)(2,1)S(1)}, bf16[320,128]{0,1:T(8,128)(2,1)S(1)}, u32[]{:S(2)}, u32[]{:S(2)}) collective-permute-start(bf16[320,128]{0,1:T(8,128)(2,1)S(1)} %bitcast.89), channel_id=1, source_target_pairs={{0,0},{2,2},{16,4},{18,6},{32,8},{34,10},{48,12},{50,14},{4,16},{6... | collective-permute-start | bytes 245768 | tf_op jit(solution)/shard_map/ppermute | solution.py:110
  26.2 15.0 %all-to-all-start = ((bf16[4,4,8,768]{3,2,1,0:T(8,128)(2,1)}), bf16[4,4,8,768]{3,2,1,0:T(8,128)(2,1)S(1)}, u32[]{:S(2)}, u32[]{:S(2)}) async-start(bf16[4,4,8,768]{3,2,1,0:T(8,128)(2,1)} %copy.49), calls=%async_computation | async-start | bytes 393216 | tf_op jit(solution)/shard_map/all_to_all | solution.py:118
  32.5 25.1 %collective-permute-start = (bf16[2,320,256]{2,1,0:T(8,128)(2,1)S(1)}, bf16[2,320,256]{2,1,0:T(8,128)(2,1)S(1)}, u32[]{:S(2)}, u32[]{:S(2)}) collective-permute-start(bf16[2,320,256]{2,1,0:T(8,128)(2,1)S(1)} %dynamic-slice_bitcast_fusion.1), channel_id=1, source_target_pairs={{0,1},{1,0},{2,3},{3,2},{4,5},{5,4},{6,7},{7,6},{8,9},{9,8},{10,11... | collective-permute-start | bytes 983048 | tf_op jit(solution)/shard_map/ppermute | solution.py:93
  59.4 28.9 %all-to-all-start.1 = ((bf16[8,320,128]{2,1,0:T(8,128)(2,1)}), bf16[8,320,128]{2,1,0:T(8,128)(2,1)S(1)}, u32[]{:S(2)}, u32[]{:S(2)}) async-start(bf16[8,320,128]{2,1,0:T(8,128)(2,1)} %bitcast.12), calls=%async_computation.1 | async-start | bytes 1310720 | tf_op jit(solution)/shard_map/all_to_all | solution.py:137
  74.5 17.4 %copy-start = (bf16[5120,128]{1,0:T(8,128)(2,1)S(1)}, bf16[5120,128]{1,0:T(8,128)(2,1)}, u32[]{:S(2)}) copy-start(bf16[5120,128]{1,0:T(8,128)(2,1)} %all-gather.4.cloned.1.call-done) | copy-start | bytes 3932164
  88.2 20.1 %all-to-all-start.2 = ((bf16[8,128,256]{2,1,0:T(8,128)(2,1)}), bf16[8,128,256]{2,1,0:T(8,128)(2,1)S(1)}, u32[]{:S(2)}, u32[]{:S(2)}) async-start(bf16[8,128,256]{2,1,0:T(8,128)(2,1)} %bitcast.77), calls=%async_computation.2 | async-start | bytes 1048576 | tf_op jit(solution)/shard_map/all_to_all | solution.py:157
  108.3 14.1 %all-to-all-start.4 = ((bf16[8,32,1280]{2,1,0:T(8,128)(2,1)}), bf16[8,32,1280]{2,1,0:T(8,128)(2,1)S(1)}, u32[]{:S(2)}, u32[]{:S(2)}) async-start(bf16[8,32,1280]{2,1,0:T(8,128)(2,1)} %bitcast.29), calls=%async_computation.4 | async-start | bytes 1310720 | tf_op jit(solution)/shard_map/all_to_all | solution.py:167
  122.5 12.6 %all-to-all-start.3 = ((bf16[4,4,8,768]{3,2,1,0:T(8,128)(2,1)}), bf16[4,4,8,768]{3,2,1,0:T(8,128)(2,1)S(1)}, u32[]{:S(2)}, u32[]{:S(2)}) async-start(bf16[4,4,8,768]{3,2,1,0:T(8,128)(2,1)} %bitcast.24), calls=%async_computation.3 | async-start | bytes 393216 | tf_op jit(solution)/shard_map/all_to_all | solution.py:179
  135.9 20.5 %copy-start.2 = (bf16[1,4,32,320]{3,2,1,0:T(8,128)(2,1)S(1)}, bf16[1,4,32,320]{3,2,1,0:T(8,128)(2,1)}, u32[]{:S(2)}) copy-start(bf16[1,4,32,320]{3,2,1,0:T(8,128)(2,1)} %param.4) | copy-start | bytes 245764
  135.9 22.0 %all-to-all-start.5 = ((bf16[8,32,1280]{2,1,0:T(8,128)(2,1)}), bf16[8,32,1280]{2,1,0:T(8,128)(2,1)S(1)}, u32[]{:S(2)}, u32[]{:S(2)}) async-start(bf16[8,32,1280]{2,1,0:T(8,128)(2,1)} %broadcast_in_dim.2), calls=%async_computation.5 | async-start | bytes 1310720 | tf_op jit(solution)/shard_map/all_to_all | solution.py:170
  141.2 15.0 %collective-permute-start.1 = (bf16[320,128]{1,0:T(8,128)(2,1)S(1)}, bf16[320,128]{1,0:T(8,128)(2,1)S(1)}, u32[]{:S(2)}, u32[]{:S(2)}) collective-permute-start(bf16[320,128]{1,0:T(8,128)(2,1)S(1)} %reduce_sum.24), channel_id=1, source_target_pairs={{0,0},{2,2},{4,16},{6,18},{8,32},{10,34},{12,48},{14,50},{16,4},{1... | collective-permute-start | bytes 245768 | tf_op jit(solution)/shard_map/ppermute | solution.py:139
Sparse Core Ops, SparseCore 0:
  24.3 42.2 all-gather.3

commit v2 on v1

v2 whole, which is shorter than its diff:
```python
import functools

import jax
import jax.numpy as jnp
from jax import lax
from jax.experimental import pallas as pl
from jax.experimental.pallas import tpu as pltpu
from jax.sharding import Mesh, PartitionSpec as P

HEAD_DIM = 128
AXES = ("x", "zl", "frame", "y", "core")
CLIP = ("x", "zl")
SWAP = ((0, 1), (1, 0))
F32 = jnp.float32
BF16 = jnp.bfloat16


def probabilities(queries, key_rows, patches):
    rows = queries.shape[0]
    scores = lax.dot_general(
        queries, key_rows, (((1,), (1,)), ((), ())), preferred_element_type=F32
    ) * (HEAD_DIM ** (-0.5))
    at = lax.broadcasted_iota(jnp.int32, (rows, rows), 0)
    to = lax.broadcasted_iota(jnp.int32, (rows, rows), 1)
    allowed = (at % patches == to % patches) & (at >= to)
    scores = jnp.where(allowed, scores, -jnp.inf)
    shifted = jnp.exp(scores - jnp.max(scores, axis=-1, keepdims=True))
    return shifted / jnp.sum(shifted, axis=-1, keepdims=True)


def attend_kernel(place_ref, all_ref, rows_ref, own_ref, sums_ref):
    n, tokens = rows_ref.shape[0], rows_ref.shape[1]
    frames, _, patches, width = all_ref.shape
    group = patches // n
    for at in range(0, width, HEAD_DIM):
        features = slice(at, at + HEAD_DIM)
        whole_parts = [all_ref[:, part, :, features].astype(F32) for part in range(3)]
        for index in range(n):
            span = slice(index * group, (index + 1) * group)
            blocks = [
                part[:, span].reshape(frames * group, HEAD_DIM).astype(BF16)
                for part in whole_parts
            ]
            queries, key_rows, values = blocks

            @pl.when(place_ref[0] == index)
            def _():
                for part, block in enumerate(blocks):
                    own_ref[part, :, features] = block

            weights = probabilities(queries, key_rows, group).astype(BF16)
            attended = jnp.dot(weights, values, preferred_element_type=F32)
            sums_ref[:, span, features] = attended.reshape(frames, group, HEAD_DIM)
    rows_ref[...] = sums_ref[...].reshape(n, tokens, width).astype(BF16)


def project_block(weight, rows):
    flat = rows.reshape(-1, rows.shape[-1])
    return lax.dot_general(weight, flat, (((1,), (1,)), ((), ())), preferred_element_type=F32)


def project_other_kernel(place_ref, weight_ref, rows_ref, pieces_ref):
    n, tokens = rows_ref.shape[0], rows_ref.shape[1]
    halves = weight_ref.shape[0]
    for half in range(halves):
        block = project_block(weight_ref[half, 1 - place_ref[1]], rows_ref[...]).astype(BF16)
        for frame in range(n):
            pieces_ref[frame * halves + half] = block[:, frame * tokens : (frame + 1) * tokens]


def project_own_kernel(place_ref, weight_ref, rows_ref, got_ref, pieces_ref):
    n, tokens = rows_ref.shape[0], rows_ref.shape[1]
    halves = weight_ref.shape[0]
    for half in range(halves):
        block = project_block(weight_ref[half, place_ref[1]], rows_ref[...])
        for frame in range(n):
            at = frame * halves + half
            piece = block[:, frame * tokens : (frame + 1) * tokens] + got_ref[at].astype(F32)
            pieces_ref[at] = piece.astype(BF16)


def attended_grad_kernel(place_ref, weight_ref, own_ref, other_ref, shares_ref, sums_ref):
    n, step = shares_ref.shape[0], shares_ref.shape[1] // shares_ref.shape[0]
    halves = weight_ref.shape[0]
    core = place_ref[1]
    frames, patches, width = sums_ref.shape
    group = patches // n
    for frame in range(n):
        total = None
        for half in range(halves):
            for grads, at in ((own_ref, core), (other_ref, 1 - core)):
                term = lax.dot_general(
                    grads[frame * halves + half],
                    weight_ref[half, at],
                    (((0,), (0,)), ((), ())),
                    preferred_element_type=F32,
                )
                total = term if total is None else total + term
        sums_ref[...] = total.reshape(sums_ref.shape)
        for j in range(n):
            start = pl.multiple_of(lax.rem(place_ref[0] + j, n) * group, group)
            share = sums_ref[:, pl.ds(start, group), :].reshape(step, width)
            shares_ref[j, frame * step : (frame + 1) * step, :] = share.astype(BF16)


def weight_grad_kernel(place_ref, rows_ref, own_ref, other_ref, out_ref, sums_ref):
    n = rows_ref.shape[0]
    halves = sums_ref.shape[0]
    core = place_ref[1]
    for half in range(halves):
        for grads, at in ((own_ref, core), (other_ref, 1 - core)):
            total = None
            for frame in range(n):
                term = jnp.dot(
                    grads[frame * halves + half], rows_ref[frame], preferred_element_type=F32
                )
                total = term if total is None else total + term
            sums_ref[half, at] = total
    out_ref[...] = sums_ref[...].reshape(-1, sums_ref.shape[-1]).T.astype(BF16)


def attend_back_kernel(patches, place_ref, qkv_ref, *refs):
    shares, (out_ref, grads_ref) = refs[:-2], refs[-2:]
    width = shares[0].shape[1]
    grad_rows = shares[0][...].astype(F32)
    for share in shares[1:]:
        grad_rows = grad_rows + share[...].astype(F32)
    grad_rows = grad_rows.astype(BF16)
    score_scale = HEAD_DIM ** (-0.5)
    for at in range(0, width, HEAD_DIM):
        queries = qkv_ref[0, :, at : at + HEAD_DIM]
        key_rows = qkv_ref[1, :, at : at + HEAD_DIM]
        values = qkv_ref[2, :, at : at + HEAD_DIM]
        grad = grad_rows[:, at : at + HEAD_DIM]
        probability = probabilities(queries, key_rows, patches)
        prob_grad = lax.dot_general(
            grad, values, (((1,), (1,)), ((), ())), preferred_element_type=F32
        )
        row_dot = jnp.sum(probability * prob_grad, axis=-1, keepdims=True)
        score_grad = (probability * (prob_grad - row_dot)).astype(BF16)
        query_grad = jnp.dot(score_grad, key_rows, preferred_element_type=F32) * score_scale
        key_grad = (
            lax.dot_general(
                score_grad, queries, (((0,), (0,)), ((), ())), preferred_element_type=F32
            )
            * score_scale
        )
        value_grad = lax.dot_general(
            probability.astype(BF16), grad, (((0,), (0,)), ((), ())), preferred_element_type=F32
        )
        for part, value in enumerate((query_grad, key_grad, value_grad)):
            grads_ref[part, :, at : at + HEAD_DIM] = value.astype(BF16)
    n, step = out_ref.shape[0], out_ref.shape[2]
    for j in range(n):
        start = pl.multiple_of(lax.rem(place_ref[0] + j, n) * step, step)
        out_ref[j] = grads_ref[:, pl.ds(start, step), :]


def arrange_kernel(place_ref, *refs):
    parts, (out_ref, sums_ref) = refs[:-2], refs[-2:]
    n = len(parts)
    frames, kinds, patches, width = out_ref.shape
    group = patches // n
    for j, part in enumerate(parts):
        start = pl.multiple_of(lax.rem(place_ref[0] + (n - j), n) * group, group)
        for kind in range(kinds):
            rows = part[kind].astype(F32).reshape(frames, group, width)
            sums_ref[:, kind, pl.ds(start, group), :] = rows
    out_ref[...] = sums_ref[...].astype(BF16)


def whole(kernel, out_shape, place, *operands, scratch=(), flops=0):
    several = isinstance(out_shape, (list, tuple))
    moved = sum(o.size * o.dtype.itemsize for o in operands)
    return pl.pallas_call(
        kernel,
        out_shape=out_shape,
        in_specs=[pl.BlockSpec(memory_space=pltpu.SMEM)]
        + [pl.BlockSpec(memory_space=pltpu.VMEM)] * len(operands),
        out_specs=[pl.BlockSpec(memory_space=pltpu.VMEM)] * len(out_shape)
        if several
        else pl.BlockSpec(memory_space=pltpu.VMEM),
        scratch_shapes=list(scratch),
        compiler_params=pltpu.CompilerParams(vmem_limit_bytes=32 * 1024 * 1024),
        cost_estimate=pl.CostEstimate(flops=flops, bytes_accessed=2 * moved, transcendentals=0),
    )(place, *operands)


def shifted(array, by, axis):
    n = lax.axis_size(axis)
    return lax.ppermute(array, axis, [(i, (i + by) % n) for i in range(n)])


def copies(array, n):
    return jnp.broadcast_to(array[None], (n, *array.shape))


def local(residual, projections, out_weight, out_grad):
    n_frame, n_y = lax.axis_size("frame"), lax.axis_size("y")
    n_clip = lax.axis_size("x") * lax.axis_size("zl")
    frame, core = lax.axis_index("frame"), lax.axis_index("core")
    place = jnp.stack([frame, core]).astype(jnp.int32)
    _, steps, patches, kinds, inner = projections.shape
    width = out_grad.shape[-1]
    frames = steps * n_frame
    step = steps * (patches // n_frame)
    rows = step * n_frame
    tokens = steps * patches
    halves = n_y // n_frame
    product = 2 * n_frame * tokens * inner * width * halves

    there = [
        (f * n_y + y, (y // halves) * n_y + halves * f + y % halves)
        for f in range(n_frame)
        for y in range(n_y)
    ]
    back = [(b, a) for a, b in there]

    grad_moved = lax.ppermute(out_grad.reshape(tokens, width).T, ("frame", "y"), back)
    qkv_all = lax.all_gather(
        projections.reshape(projections.shape[1:]).transpose(0, 2, 1, 3), "frame", tiled=True
    )
    grad_own = lax.all_to_all(copies(grad_moved, n_y), "y", 0, 0, tiled=True)
    grad_other = lax.ppermute(grad_own, "core", SWAP)

    feature_rows, qkv = whole(
        attend_kernel,
        [
            jax.ShapeDtypeStruct((n_frame, tokens, inner), BF16),
            jax.ShapeDtypeStruct((kinds, rows, inner), BF16),
        ],
        place,
        qkv_all,
        scratch=[pltpu.VMEM((frames, patches, inner), F32)],
        flops=product,
    )

    weight_t = out_weight.T.reshape(halves, 2, width, inner)
    piece_shape = jax.ShapeDtypeStruct((n_y, width, tokens), BF16)
    pieces_other = whole(
        project_other_kernel, piece_shape, place, weight_t, feature_rows, flops=product
    )
    pieces_got = lax.ppermute(pieces_other, "core", SWAP)
    pieces = whole(
        project_own_kernel, piece_shape, place, weight_t, feature_rows, pieces_got, flops=product
    )
    pieces, grad_own, grad_other = lax.optimization_barrier((pieces, grad_own, grad_other))
    pieces = lax.all_to_all(pieces, "y", 0, 0, tiled=True)

    shares = whole(
        attended_grad_kernel,
        jax.ShapeDtypeStruct((n_frame, rows, inner), BF16),
        place,
        weight_t,
        grad_own,
        grad_other,
        scratch=[pltpu.VMEM((steps, patches, inner), F32)],
        flops=2 * product,
    )
    weight_part = whole(
        weight_grad_kernel,
        jax.ShapeDtypeStruct(out_weight.shape, BF16),
        place,
        feature_rows,
        grad_own,
        grad_other,
        scratch=[pltpu.VMEM((halves, 2, width, inner), F32)],
        flops=2 * product,
    )
    shares = [shares[0]] + [shifted(shares[j], j, "frame") for j in range(1, n_frame)]
    grads = whole(
        functools.partial(attend_back_kernel, patches // n_frame),
        jax.ShapeDtypeStruct((n_frame, kinds, step, inner), BF16),
        place,
        qkv,
        *shares,
        scratch=[pltpu.VMEM((kinds, rows, inner), BF16)],
    )

    weight_part, _, pieces = lax.optimization_barrier((weight_part, grads, pieces))
    weight_part = weight_part.reshape(n_clip, inner // n_clip, -1)
    weight_part = lax.all_to_all(weight_part, CLIP, 0, 0, tiled=True)
    projected = jnp.sum(pieces.astype(F32), axis=0).astype(BF16)
    grads = [grads[0]] + [shifted(grads[j], j, "frame") for j in range(1, n_frame)]

    weight_sum = jnp.sum(weight_part.astype(F32), axis=0).astype(BF16)
    weight_sum, _ = lax.optimization_barrier((weight_sum, grads))
    weight_grad = lax.all_to_all(copies(weight_sum, n_clip), CLIP, 0, 0, tiled=True)
    weight_grad = weight_grad.reshape(out_weight.shape)

    projected = lax.ppermute(projected, ("frame", "y"), there)
    projected = projected.T.reshape(residual.shape)
    block_out = (residual.astype(F32) + projected.astype(F32)).astype(BF16)
    qkv_grad = whole(
        arrange_kernel,
        jax.ShapeDtypeStruct((steps, kinds, patches, inner), BF16),
        place,
        *grads,
        scratch=[pltpu.VMEM((steps, kinds, patches, inner), F32)],
    )
    qkv_grad = qkv_grad.transpose(0, 2, 1, 3).reshape(projections.shape)
    return (block_out, qkv_grad, weight_grad)


def solution(mesh):
    n_clip, n_frame, n_head = mesh.devices.shape
    fine = Mesh(mesh.devices.reshape(n_clip // 2, 2, n_frame, n_head // 2, 2), AXES)
    head = ("y", "core")
    in_specs = (
        P(CLIP, "frame", None, head),
        P(CLIP, "frame", None, None, head),
        P(head, "frame"),
        P(CLIP, "frame", None, head),
    )
    out_specs = (
        P(CLIP, "frame", None, head),
        P(CLIP, "frame", None, None, head),
        P(head, "frame"),
    )
    return jax.shard_map(local, mesh=fine, in_specs=in_specs, out_specs=out_specs, check_vma=False)
```

time: 166 us -> 133 us (0.80)
  the two profiles are of different devices: /device:TPU:42 before, /device:TPU:34 now
where the time goes in v2:
time: 133 us; the launch traced here: 132 us
  starting transfers between devices  75.5 us (57%)
  blocking collectives  20.8 us (16%)
  waiting for transfers between devices  14.8 us (11%)
  Pallas kernels  13.5 us (10%)
  local copies, waits for them, and re-layouts  5.42 us (4%)
    ppermute x6, starting transfers between devices, shifted(): return lax.ppermute(array, axis, [(i, (i + by) % n) for i in range(n)])  25.3 us
    all_gather x1, blocking collectives, local(): lax.all_gather(projections.reshape(projections.shape[1:]).transpose(0, 2,...  20.8 us
    pallas_call x7, Pallas kernels, whole(): pl.pallas_call(kernel, out_shape=out_shape, in_specs=[pl.BlockSpec(memory...  13.5 us
    ppermute x1, starting transfers between devices, local(): lax.ppermute(out_grad.reshape(tokens, width).T, ('frame', 'y'), back)  10.5 us
    all_to_all x1, starting transfers between devices, local(): weight_part = lax.all_to_all(weight_part, CLIP, 0, 0, tiled=True)  8.94 us
    ppermute x1, waiting for transfers between devices, local(): projected = lax.ppermute(projected, ('frame', 'y'), there)  7.69 us
    all_to_all x1, starting transfers between devices, local(): grad_own = lax.all_to_all(copies(grad_moved, n_y), 'y', 0, 0, tiled=True)  7.34 us
    all_to_all x1, starting transfers between devices, local(): pieces = lax.all_to_all(pieces, 'y', 0, 0, tiled=True)  7.21 us
  transfers between devices with their start and end apart: 14, of which 5 were waited for; matrix products, arithmetic and copies ran while one was open for 1% of the time, Pallas kernels for 10%

profile of v2, /device:TPU:34, one launch (start us, length us, event | category | flops | bytes accessed | tf_op | source)
XLA Modules:
  0.0 131.9 jit_solution(18120334438650257378)
XLA Ops:
  0.6 1.0 copy.13
  1.6 10.5 %collective-permute-start.1 = (bf16[320,128]{1,0:T(8,128)(2,1)S(1)}, bf16[320,128]{1,0:T(8,128)(2,1)S(1)}, u32[]{:S(2)}, u32[]{:S(2)}) collective-permute-start(bf16[320,128]{1,0:T(8,128)(2,1)S(1)} %bitcast.42), channel_id=1, source_target_pairs={{0,0},{2,2},{16,4},{18,6},{32,8},{34,10},{48,12},{50,14},{4,16},{6... | collective-permute-start | bytes 245768 | tf_op jit(solution)/shard_map/ppermute | solution.py:219
  12.1 4.6 %collective-permute-done.1 = bf16[320,128]{1,0:T(8,128)(2,1)S(1)} collective-permute-done((bf16[320,128]{1,0:T(8,128)(2,1)S(1)}, bf16[320,128]{1,0:T(8,128)(2,1)S(1)}, u32[]{:S(2)}, u32[]{:S(2)}) %collective-permute-start.1) | collective-permute-done | bytes 81952 | tf_op jit(solution)/shard_map/ppermute | solution.py:219
  16.7 0.9 broadcast_in_dim.4
  17.7 7.3 %all-to-all-start = ((bf16[8,320,128]{2,1,0:T(8,128)(2,1)}), bf16[8,320,128]{2,1,0:T(8,128)(2,1)S(1)}, u32[]{:S(2)}, u32[]{:S(2)}) async-start(bf16[8,320,128]{2,1,0:T(8,128)(2,1)} %broadcast_in_dim.4), calls=%async_computation | async-start | bytes 1310720 | tf_op jit(solution)/shard_map/all_to_all | solution.py:223
  25.0 0.2 copy.12
  25.3 0.1 pad_add_fusion.place_ref
  25.3 0.6 copy-done.3
  25.9 20.8 %all_gather.3.all_ref = bf16[16,3,32,256]{3,2,1,0:T(8,128)(2,1)S(1)} all-gather(bf16[4,3,32,256]{3,2,1,0:T(8,128)(2,1)S(1)} %bitcast.40), channel_id=1, replica_groups=mesh['x'=4,'zl'=2,'frame'=4,'y'=8,'core'=2] {'frame'}, dimensions={0}, use_global_device_ids=true | all-gather | bytes 983040 | tf_op jit(solution)/shard_map/all_gather | solution.py:220
  46.8 4.2 %shard_map.67 = (bf16[4,128,256]{2,1,0:T(8,128)(2,1)S(1)}, bf16[3,128,256]{2,1,0:T(8,128)(2,1)S(1)}) custom-call(s32[2]{0:T(128)S(1)} %pad_add_fusion.place_ref, bf16[16,3,32,256]{3,2,1,0:T(8,128)(2,1)S(1)} %all_gather.3.all_ref), custom_call_target="tpu_custom_call" | custom-call | flops 167772160 | bytes 1572864 | tf_op jit(solution)/shard_map/pallas_call | solution.py:175
  51.0 0.0 copy-start
  51.0 0.9 shard_map.68
  51.9 1.9 %collective-permute-start = (bf16[8,320,128]{2,1,0:T(8,128)(2,1)S(1)}, bf16[8,320,128]{2,1,0:T(8,128)(2,1)S(1)}, u32[]{:S(2)}, u32[]{:S(2)}) collective-permute-start(bf16[8,320,128]{2,1,0:T(8,128)(2,1)S(1)} %shard_map.68), channel_id=1, source_target_pairs={{0,1},{1,0},{2,3},{3,2},{4,5},{5,4},{6,7},{7,6},{8,9},{9,8},{10,11... | collective-permute-start | bytes 1966088 | tf_op jit(solution)/shard_map/ppermute | solution.py:243
  53.8 0.0 all-to-all-done.own_ref
  53.8 2.4 %collective-permute-start.2 = (bf16[8,320,128]{2,1,0:T(8,128)(2,1)S(1)}, bf16[8,320,128]{2,1,0:T(8,128)(2,1)S(1)}, u32[]{:S(2)}, u32[]{:S(2)}) collective-permute-start(bf16[8,320,128]{2,1,0:T(8,128)(2,1)S(1)} %all-to-all-done.own_ref), channel_id=1, source_target_pairs={{0,1},{1,0},{2,3},{3,2},{4,5},{5,4},{6,7},{7,6},{8,9},{9,8},{10,11... | collective-permute-start | bytes 1966088 | tf_op jit(solution)/shard_map/ppermute | solution.py:224
  56.3 0.0 collective-permute-done.got_ref
  56.3 1.7 %shard_map.69 = bf16[8,320,128]{2,1,0:T(8,128)(2,1)} custom-call(s32[2]{0:T(128)S(1)} %pad_add_fusion.place_ref, bf16[2,2,320,256]{3,2,1,0:T(8,128)(2,1)S(1)} %bitcast.34, bf16[4,128,256]{2,1,0:T(8,128)(2,1)S(1)} %get-tuple-element.11.rows_ref, bf16[8,320,128]{2,1,0:T(8,128)(2,1)S(1)} %collective-permute-done.got_ref), custom_call_target="tpu_custom_call" | custom-call | flops 167772160 | bytes 3145728 | tf_op jit(solution)/shard_map/pallas_call | solution.py:175
  58.0 0.0 collective-permute-done.2.other_ref
  58.0 7.2 %all-to-all-start.1 = ((bf16[8,320,128]{2,1,0:T(8,128)(2,1)}), bf16[8,320,128]{2,1,0:T(8,128)(2,1)S(1)}, u32[]{:S(2)}, u32[]{:S(2)}) async-start(bf16[8,320,128]{2,1,0:T(8,128)(2,1)} %shard_map.69), calls=%async_computation.1 | async-start | bytes 1310720 | tf_op jit(solution)/shard_map/all_to_all | solution.py:248
  65.2 1.4 %shard_map.71 = bf16[4,128,256]{2,1,0:T(8,128)(2,1)S(1)} custom-call(s32[2]{0:T(128)S(1)} %pad_add_fusion.place_ref, bf16[2,2,320,256]{3,2,1,0:T(8,128)(2,1)S(1)} %bitcast.35, bf16[8,320,128]{2,1,0:T(8,128)(2,1)S(1)} %all-to-all-done.own_ref, bf16[8,320,128]{2,1,0:T(8,128)(2,1)S(1)} %collective-permute-done.2.other_ref), custom_call_target="tpu_custom_call" | custom-call | flops 335544320 | bytes 3932160 | tf_op jit(solution)/shard_map/pallas_call | solution.py:175
  66.6 3.7 %collective-permute-start.3 = (bf16[128,256]{1,0:T(8,128)(2,1)S(1)}, bf16[128,256]{1,0:T(8,128)(2,1)S(1)}, u32[]{:S(2)}, u32[]{:S(2)}) collective-permute-start(bf16[128,256]{1,0:T(8,128)(2,1)S(1)} %get-tuple-element.21), channel_id=1, source_target_pairs={{0,16},{16,32},{32,48},{48,0},{1,17},{17,33},{33,49},{49,1},{2,18}... | collective-permute-start | bytes 196616 | tf_op jit(solution)/shard_map/ppermute | solution.py:191
  70.4 4.5 %collective-permute-start.4 = (bf16[128,256]{1,0:T(8,128)(2,1)S(1)}, bf16[128,256]{1,0:T(8,128)(2,1)S(1)}, u32[]{:S(2)}, u32[]{:S(2)}) collective-permute-start(bf16[128,256]{1,0:T(8,128)(2,1)S(1)} %get-tuple-element.20), channel_id=1, source_target_pairs={{0,32},{16,48},{32,0},{48,16},{1,33},{17,49},{33,1},{49,17},{2,34}... | collective-permute-start | bytes 196616 | tf_op jit(solution)/shard_map/ppermute | solution.py:191
  74.8 0.0 copy-start.1
  74.8 4.5 %collective-permute-start.5 = (bf16[128,256]{1,0:T(8,128)(2,1)S(1)}, bf16[128,256]{1,0:T(8,128)(2,1)S(1)}, u32[]{:S(2)}, u32[]{:S(2)}) collective-permute-start(bf16[128,256]{1,0:T(8,128)(2,1)S(1)} %get-tuple-element.19), channel_id=1, source_target_pairs={{0,48},{16,0},{32,16},{48,32},{1,49},{17,1},{33,17},{49,33},{2,50}... | collective-permute-start | bytes 196616 | tf_op jit(solution)/shard_map/ppermute | solution.py:191
  79.3 2.5 %shard_map.70 = bf16[256,1280]{1,0:T(8,128)(2,1)} custom-call(s32[2]{0:T(128)S(1)} %pad_add_fusion.place_ref, bf16[4,128,256]{2,1,0:T(8,128)(2,1)S(1)} %get-tuple-element.11.rows_ref, bf16[8,320,128]{2,1,0:T(8,128)(2,1)S(1)} %all-to-all-done.own_ref, bf16[8,320,128]{2,1,0:T(8,128)(2,1)S(1)} %collective-permute-done.2.other_ref), custom_call_target="tpu_custom_call" | custom-call | flops 335544320 | bytes 3145728 | tf_op jit(solution)/shard_map/pallas_call | solution.py:175
  81.8 0.0 collective-permute-done.3.refs_1_
  81.8 0.0 collective-permute-done.4.refs_2_
  81.8 0.4 collective-permute-done.5.refs_3_
  82.2 1.6 %shard_map.72 = bf16[4,3,32,256]{3,2,1,0:T(8,128)(2,1)S(1)} custom-call(s32[2]{0:T(128)S(1)} %pad_add_fusion.place_ref, bf16[3,128,256]{2,1,0:T(8,128)(2,1)S(1)} %copy-done.1, bf16[128,256]{1,0:T(8,128)(2,1)S(1)} %get-tuple-element.22.refs_0_, bf16[128,256]{1,0:T(8,128)(2,1)S(1)} %collective-permute-done.3.refs_1_, ...), custom_call_target="tpu_custom_call" | custom-call | bytes 917504 | tf_op jit(solution)/shard_map/pallas_call | solution.py:175
  83.8 0.0 all-to-all-done.1
  83.8 8.9 %all-to-all-start.2 = ((bf16[8,32,1280]{2,1,0:T(8,128)(2,1)}), bf16[8,32,1280]{2,1,0:T(8,128)(2,1)S(1)}, u32[]{:S(2)}, u32[]{:S(2)}) async-start(bf16[8,32,1280]{2,1,0:T(8,128)(2,1)} %bitcast.20), calls=%async_computation.2 | async-start | bytes 1310720 | tf_op jit(solution)/shard_map/all_to_all | solution.py:282
  92.8 3.2 %collective-permute-start.7 = (bf16[3,32,256]{2,1,0:T(8,128)(2,1)S(1)}, bf16[3,32,256]{2,1,0:T(8,128)(2,1)S(1)}, u32[]{:S(2)}, u32[]{:S(2)}) collective-permute-start(bf16[3,32,256]{2,1,0:T(8,128)(2,1)S(1)} %get-tuple-element.25), channel_id=1, source_target_pairs={{0,16},{16,32},{32,48},{48,0},{1,17},{17,33},{33,49},{49,1},{2,18}... | collective-permute-start | bytes 147464 | tf_op jit(solution)/shard_map/ppermute | solution.py:191
  95.9 4.8 %collective-permute-start.8 = (bf16[3,32,256]{2,1,0:T(8,128)(2,1)S(1)}, bf16[3,32,256]{2,1,0:T(8,128)(2,1)S(1)}, u32[]{:S(2)}, u32[]{:S(2)}) collective-permute-start(bf16[3,32,256]{2,1,0:T(8,128)(2,1)S(1)} %get-tuple-element.24), channel_id=1, source_target_pairs={{0,32},{16,48},{32,0},{48,16},{1,33},{17,49},{33,1},{49,17},{2,34}... | collective-permute-start | bytes 147464 | tf_op jit(solution)/shard_map/ppermute | solution.py:191
  100.7 4.7 %collective-permute-start.9 = (bf16[3,32,256]{2,1,0:T(8,128)(2,1)S(1)}, bf16[3,32,256]{2,1,0:T(8,128)(2,1)S(1)}, u32[]{:S(2)}, u32[]{:S(2)}) collective-permute-start(bf16[3,32,256]{2,1,0:T(8,128)(2,1)S(1)} %get-tuple-element.23), channel_id=1, source_target_pairs={{0,48},{16,0},{32,16},{48,32},{1,49},{17,1},{33,17},{49,33},{2,50}... | collective-permute-start | bytes 147464 | tf_op jit(solution)/shard_map/ppermute | solution.py:191
  105.5 0.1 reduce_sum.25
  105.6 0.5 collective-permute-done.8.refs_2_
  106.1 1.5 %collective-permute-done.9.refs_3_ = bf16[3,32,256]{2,1,0:T(8,128)(2,1)S(1)} collective-permute-done((bf16[3,32,256]{2,1,0:T(8,128)(2,1)S(1)}, bf16[3,32,256]{2,1,0:T(8,128)(2,1)S(1)}, u32[]{:S(2)}, u32[]{:S(2)}) %collective-permute-start.9) | collective-permute-done | bytes 49184 | tf_op jit(solution)/shard_map/ppermute | solution.py:191
  107.6 0.9 broadcast_in_dim.5
  108.5 5.7 %all-to-all-start.3 = ((bf16[8,32,1280]{2,1,0:T(8,128)(2,1)}), bf16[8,32,1280]{2,1,0:T(8,128)(2,1)S(1)}, u32[]{:S(2)}, u32[]{:S(2)}) async-start(bf16[8,32,1280]{2,1,0:T(8,128)(2,1)} %broadcast_in_dim.5), calls=%async_computation.3 | async-start | bytes 1310720 | tf_op jit(solution)/shard_map/all_to_all | solution.py:288
  114.2 0.1 reduce_sum.24
  114.3 6.2 %collective-permute-start.6 = (bf16[320,128]{1,0:T(8,128)(2,1)S(1)}, bf16[320,128]{1,0:T(8,128)(2,1)S(1)}, u32[]{:S(2)}, u32[]{:S(2)}) collective-permute-start(bf16[320,128]{1,0:T(8,128)(2,1)S(1)} %reduce_sum.24), channel_id=1, source_target_pairs={{0,0},{2,2},{4,16},{6,18},{8,32},{10,34},{12,48},{14,50},{16,4},{1... | collective-permute-start | bytes 245768 | tf_op jit(solution)/shard_map/ppermute | solution.py:291
  120.5 1.3 shard_map.73
  121.8 7.7 %collective-permute-done.6 = bf16[320,128]{1,0:T(8,128)(2,1)S(1)} collective-permute-done((bf16[320,128]{1,0:T(8,128)(2,1)S(1)}, bf16[320,128]{1,0:T(8,128)(2,1)S(1)}, u32[]{:S(2)}, u32[]{:S(2)}) %collective-permute-start.6) | collective-permute-done | bytes 81952 | tf_op jit(solution)/shard_map/ppermute | solution.py:291
  129.5 0.0 copy-start.4
  129.5 0.1 copy.14
  129.6 0.8 copy-done.4
  130.4 0.7 add_convert_fusion
  131.0 0.8 copy.16
  (11 shorter events, 0.1 us)
Async XLA Ops:
  1.6 15.1 %collective-permute-start.1 = (bf16[320,128]{1,0:T(8,128)(2,1)S(1)}, bf16[320,128]{1,0:T(8,128)(2,1)S(1)}, u32[]{:S(2)}, u32[]{:S(2)}) collective-permute-start(bf16[320,128]{1,0:T(8,128)(2,1)S(1)} %bitcast.42), channel_id=1, source_target_pairs={{0,0},{2,2},{16,4},{18,6},{32,8},{34,10},{48,12},{50,14},{4,16},{6... | collective-permute-start | bytes 245768 | tf_op jit(solution)/shard_map/ppermute | solution.py:219
  17.7 7.3 %copy-start.2 = (bf16[256,1280]{1,0:T(8,128)(2,1)S(1)}, bf16[256,1280]{1,0:T(8,128)(2,1)}, u32[]{:S(2)}) copy-start(bf16[256,1280]{1,0:T(8,128)(2,1)} %param.6) | copy-start | bytes 1966084
  17.7 36.2 %all-to-all-start = ((bf16[8,320,128]{2,1,0:T(8,128)(2,1)}), bf16[8,320,128]{2,1,0:T(8,128)(2,1)S(1)}, u32[]{:S(2)}, u32[]{:S(2)}) async-start(bf16[8,320,128]{2,1,0:T(8,128)(2,1)} %broadcast_in_dim.4), calls=%async_computation | async-start | bytes 1310720 | tf_op jit(solution)/shard_map/all_to_all | solution.py:223
  25.0 0.9 copy-start.3
  51.0 0.9 copy-start
  51.9 4.4 %collective-permute-start = (bf16[8,320,128]{2,1,0:T(8,128)(2,1)S(1)}, bf16[8,320,128]{2,1,0:T(8,128)(2,1)S(1)}, u32[]{:S(2)}, u32[]{:S(2)}) collective-permute-start(bf16[8,320,128]{2,1,0:T(8,128)(2,1)S(1)} %shard_map.68), channel_id=1, source_target_pairs={{0,1},{1,0},{2,3},{3,2},{4,5},{5,4},{6,7},{7,6},{8,9},{9,8},{10,11... | collective-permute-start | bytes 1966088 | tf_op jit(solution)/shard_map/ppermute | solution.py:243
  53.8 4.2 %collective-permute-start.2 = (bf16[8,320,128]{2,1,0:T(8,128)(2,1)S(1)}, bf16[8,320,128]{2,1,0:T(8,128)(2,1)S(1)}, u32[]{:S(2)}, u32[]{:S(2)}) collective-permute-start(bf16[8,320,128]{2,1,0:T(8,128)(2,1)S(1)} %all-to-all-done.own_ref), channel_id=1, source_target_pairs={{0,1},{1,0},{2,3},{3,2},{4,5},{5,4},{6,7},{7,6},{8,9},{9,8},{10,11... | collective-permute-start | bytes 1966088 | tf_op jit(solution)/shard_map/ppermute | solution.py:224
  58.0 25.8 %all-to-all-start.1 = ((bf16[8,320,128]{2,1,0:T(8,128)(2,1)}), bf16[8,320,128]{2,1,0:T(8,128)(2,1)S(1)}, u32[]{:S(2)}, u32[]{:S(2)}) async-start(bf16[8,320,128]{2,1,0:T(8,128)(2,1)} %shard_map.69), calls=%async_computation.1 | async-start | bytes 1310720 | tf_op jit(solution)/shard_map/all_to_all | solution.py:248
  66.6 15.1 %collective-permute-start.3 = (bf16[128,256]{1,0:T(8,128)(2,1)S(1)}, bf16[128,256]{1,0:T(8,128)(2,1)S(1)}, u32[]{:S(2)}, u32[]{:S(2)}) collective-permute-start(bf16[128,256]{1,0:T(8,128)(2,1)S(1)} %get-tuple-element.21), channel_id=1, source_target_pairs={{0,16},{16,32},{32,48},{48,0},{1,17},{17,33},{33,49},{49,1},{2,18}... | collective-permute-start | bytes 196616 | tf_op jit(solution)/shard_map/ppermute | solution.py:191
  70.4 11.4 %collective-permute-start.4 = (bf16[128,256]{1,0:T(8,128)(2,1)S(1)}, bf16[128,256]{1,0:T(8,128)(2,1)S(1)}, u32[]{:S(2)}, u32[]{:S(2)}) collective-permute-start(bf16[128,256]{1,0:T(8,128)(2,1)S(1)} %get-tuple-element.20), channel_id=1, source_target_pairs={{0,32},{16,48},{32,0},{48,16},{1,33},{17,49},{33,1},{49,17},{2,34}... | collective-permute-start | bytes 196616 | tf_op jit(solution)/shard_map/ppermute | solution.py:191
  74.8 7.4 %copy-start.1 = (bf16[3,128,256]{2,1,0:T(8,128)(2,1)S(1)}, bf16[3,128,256]{2,1,0:T(8,128)(2,1)}, u32[]{:S(2)}) copy-start(bf16[3,128,256]{2,1,0:T(8,128)(2,1)} %copy-done) | copy-start | bytes 589828
  74.8 7.4 %collective-permute-start.5 = (bf16[128,256]{1,0:T(8,128)(2,1)S(1)}, bf16[128,256]{1,0:T(8,128)(2,1)S(1)}, u32[]{:S(2)}, u32[]{:S(2)}) collective-permute-start(bf16[128,256]{1,0:T(8,128)(2,1)S(1)} %get-tuple-element.19), channel_id=1, source_target_pairs={{0,48},{16,0},{32,16},{48,32},{1,49},{17,1},{33,17},{49,33},{2,50}... | collective-permute-start | bytes 196616 | tf_op jit(solution)/shard_map/ppermute | solution.py:191
  83.8 21.7 %all-to-all-start.2 = ((bf16[8,32,1280]{2,1,0:T(8,128)(2,1)}), bf16[8,32,1280]{2,1,0:T(8,128)(2,1)S(1)}, u32[]{:S(2)}, u32[]{:S(2)}) async-start(bf16[8,32,1280]{2,1,0:T(8,128)(2,1)} %bitcast.20), calls=%async_computation.2 | async-start | bytes 1310720 | tf_op jit(solution)/shard_map/all_to_all | solution.py:282
  92.8 12.8 %collective-permute-start.7 = (bf16[3,32,256]{2,1,0:T(8,128)(2,1)S(1)}, bf16[3,32,256]{2,1,0:T(8,128)(2,1)S(1)}, u32[]{:S(2)}, u32[]{:S(2)}) collective-permute-start(bf16[3,32,256]{2,1,0:T(8,128)(2,1)S(1)} %get-tuple-element.25), channel_id=1, source_target_pairs={{0,16},{16,32},{32,48},{48,0},{1,17},{17,33},{33,49},{49,1},{2,18}... | collective-permute-start | bytes 147464 | tf_op jit(solution)/shard_map/ppermute | solution.py:191
  95.9 10.2 %collective-permute-start.8 = (bf16[3,32,256]{2,1,0:T(8,128)(2,1)S(1)}, bf16[3,32,256]{2,1,0:T(8,128)(2,1)S(1)}, u32[]{:S(2)}, u32[]{:S(2)}) collective-permute-start(bf16[3,32,256]{2,1,0:T(8,128)(2,1)S(1)} %get-tuple-element.24), channel_id=1, source_target_pairs={{0,32},{16,48},{32,0},{48,16},{1,33},{17,49},{33,1},{49,17},{2,34}... | collective-permute-start | bytes 147464 | tf_op jit(solution)/shard_map/ppermute | solution.py:191
  100.7 6.9 %collective-permute-start.9 = (bf16[3,32,256]{2,1,0:T(8,128)(2,1)S(1)}, bf16[3,32,256]{2,1,0:T(8,128)(2,1)S(1)}, u32[]{:S(2)}, u32[]{:S(2)}) collective-permute-start(bf16[3,32,256]{2,1,0:T(8,128)(2,1)S(1)} %get-tuple-element.23), channel_id=1, source_target_pairs={{0,48},{16,0},{32,16},{48,32},{1,49},{17,1},{33,17},{49,33},{2,50}... | collective-permute-start | bytes 147464 | tf_op jit(solution)/shard_map/ppermute | solution.py:191
  108.5 22.5 %all-to-all-start.3 = ((bf16[8,32,1280]{2,1,0:T(8,128)(2,1)}), bf16[8,32,1280]{2,1,0:T(8,128)(2,1)S(1)}, u32[]{:S(2)}, u32[]{:S(2)}) async-start(bf16[8,32,1280]{2,1,0:T(8,128)(2,1)} %broadcast_in_dim.5), calls=%async_computation.3 | async-start | bytes 1310720 | tf_op jit(solution)/shard_map/all_to_all | solution.py:288
  114.3 15.2 %collective-permute-start.6 = (bf16[320,128]{1,0:T(8,128)(2,1)S(1)}, bf16[320,128]{1,0:T(8,128)(2,1)S(1)}, u32[]{:S(2)}, u32[]{:S(2)}) collective-permute-start(bf16[320,128]{1,0:T(8,128)(2,1)S(1)} %reduce_sum.24), channel_id=1, source_target_pairs={{0,0},{2,2},{4,16},{6,18},{8,32},{10,34},{12,48},{14,50},{16,4},{1... | collective-permute-start | bytes 245768 | tf_op jit(solution)/shard_map/ppermute | solution.py:291
  129.5 0.9 copy-start.4

commit v3 on v2

v3 whole, which is shorter than its diff:
```python
import jax
import jax.numpy as jnp
from jax import lax
from jax.experimental import pallas as pl
from jax.experimental.pallas import tpu as pltpu
from jax.sharding import Mesh, PartitionSpec as P

HEAD_DIM = 128
AXES = ("x", "zl", "frame", "y", "core")
CLIP = ("x", "zl")
SWAP = ((0, 1), (1, 0))
F32 = jnp.float32
BF16 = jnp.bfloat16


def probabilities(queries, key_rows, patches):
    rows = queries.shape[0]
    scores = lax.dot_general(
        queries, key_rows, (((1,), (1,)), ((), ())), preferred_element_type=F32
    ) * (HEAD_DIM ** (-0.5))
    at = lax.broadcasted_iota(jnp.int32, (rows, rows), 0)
    to = lax.broadcasted_iota(jnp.int32, (rows, rows), 1)
    allowed = (at % patches == to % patches) & (at >= to)
    scores = jnp.where(allowed, scores, -jnp.inf)
    shifted = jnp.exp(scores - jnp.max(scores, axis=-1, keepdims=True))
    return shifted / jnp.sum(shifted, axis=-1, keepdims=True)


def block_of(part):
    return part.reshape(-1, part.shape[-1]).astype(BF16)


def attend_kernel(all_ref, rows_ref, sums_ref):
    n, tokens = rows_ref.shape[0], rows_ref.shape[1]
    frames, kinds, patches, width = all_ref.shape
    group = patches // n
    for at in range(0, width, HEAD_DIM):
        features = slice(at, at + HEAD_DIM)
        parts = [all_ref[:, kind, :, features].astype(F32) for kind in range(kinds)]
        for start in range(0, patches, group):
            span = slice(start, start + group)
            queries, key_rows, values = (block_of(part[:, span]) for part in parts)
            weights = probabilities(queries, key_rows, group).astype(BF16)
            attended = jnp.dot(weights, values, preferred_element_type=F32)
            sums_ref[:, span, features] = attended.reshape(frames, group, HEAD_DIM)
    rows_ref[...] = sums_ref[...].reshape(n, tokens, width).astype(BF16)


def slot(place_ref, frame, n):
    return lax.rem(2 * place_ref[0] + n // 2 + n - frame, n)


def project_block(weight, rows):
    flat = rows.reshape(-1, rows.shape[-1])
    return lax.dot_general(weight, flat, (((1,), (1,)), ((), ())), preferred_element_type=F32)


def project_other_kernel(place_ref, weight_ref, rows_ref, pieces_ref):
    n, tokens = rows_ref.shape[0], rows_ref.shape[1]
    halves = weight_ref.shape[0]
    for half in range(halves):
        block = project_block(weight_ref[half, 1 - place_ref[1]], rows_ref[...]).astype(BF16)
        for frame in range(n):
            pieces_ref[slot(place_ref, frame, n) * halves + half] = block[:, frame * tokens : (frame + 1) * tokens]


def project_own_kernel(place_ref, weight_ref, rows_ref, got_ref, pieces_ref):
    n, tokens = rows_ref.shape[0], rows_ref.shape[1]
    halves = weight_ref.shape[0]
    for half in range(halves):
        block = project_block(weight_ref[half, place_ref[1]], rows_ref[...])
        for frame in range(n):
            at = slot(place_ref, frame, n) * halves + half
            piece = block[:, frame * tokens : (frame + 1) * tokens] + got_ref[at].astype(F32)
            pieces_ref[at] = piece.astype(BF16)


def attended_grad_kernel(place_ref, weight_ref, own_ref, other_ref, out_ref):
    n, halves = out_ref.shape[0], weight_ref.shape[0]
    core = place_ref[1]
    for frame in range(n):
        total = None
        for half in range(halves):
            for grads, at in ((own_ref, core), (other_ref, 1 - core)):
                term = lax.dot_general(
                    grads[slot(place_ref, frame, n) * halves + half],
                    weight_ref[half, at],
                    (((0,), (0,)), ((), ())),
                    preferred_element_type=F32,
                )
                total = term if total is None else total + term
        out_ref[frame] = total.astype(BF16)


def weight_grad_kernel(place_ref, rows_ref, own_ref, other_ref, out_ref, sums_ref):
    n = rows_ref.shape[0]
    halves = sums_ref.shape[0]
    core = place_ref[1]
    for half in range(halves):
        for grads, at in ((own_ref, core), (other_ref, 1 - core)):
            total = None
            for frame in range(n):
                term = jnp.dot(
                    grads[slot(place_ref, frame, n) * halves + half], rows_ref[frame], preferred_element_type=F32
                )
                total = term if total is None else total + term
            sums_ref[half, at] = total
    out_ref[...] = sums_ref[...].reshape(-1, sums_ref.shape[-1]).T.astype(BF16)


def sum_kernel(parts_ref, out_ref):
    total = parts_ref[0].astype(F32)
    for at in range(1, parts_ref.shape[0]):
        total = total + parts_ref[at].astype(F32)
    out_ref[...] = total.astype(BF16)


def attend_back_kernel(group, place_ref, all_ref, near_ref, far_ref, out_ref, grads_ref, sums_ref):
    frames, kinds, patches, width = all_ref.shape
    steps = out_ref.shape[0]
    total = near_ref[...].astype(F32) + far_ref[...].astype(F32)
    grads_ref[...] = total.reshape(frames, patches, width)
    score_scale = HEAD_DIM ** (-0.5)
    for at in range(0, width, HEAD_DIM):
        features = slice(at, at + HEAD_DIM)
        parts = [all_ref[:, kind, :, features].astype(F32) for kind in range(kinds)]
        for start in range(0, patches, group):
            span = slice(start, start + group)
            queries, key_rows, values = (block_of(part[:, span]) for part in parts)
            grad = block_of(grads_ref[:, span, features])
            probability = probabilities(queries, key_rows, group)
            prob_grad = lax.dot_general(
                grad, values, (((1,), (1,)), ((), ())), preferred_element_type=F32
            )
            row_dot = jnp.sum(probability * prob_grad, axis=-1, keepdims=True)
            score_grad = (probability * (prob_grad - row_dot)).astype(BF16)
            query_grad = jnp.dot(score_grad, key_rows, preferred_element_type=F32) * score_scale
            key_grad = (
                lax.dot_general(
                    score_grad, queries, (((0,), (0,)), ((), ())), preferred_element_type=F32
                )
                * score_scale
            )
            value_grad = lax.dot_general(
                probability.astype(BF16), grad, (((0,), (0,)), ((), ())), preferred_element_type=F32
            )
            for kind, value in enumerate((query_grad, key_grad, value_grad)):
                sums_ref[:, kind, span, features] = value.reshape(frames, group, HEAD_DIM)
    for step in range(steps):
        out_ref[step] = sums_ref[place_ref[0] * steps + step].astype(BF16)


def whole(kernel, out_shape, place, *operands, scratch=(), flops=0):
    several = isinstance(out_shape, (list, tuple))
    moved = sum(o.size * o.dtype.itemsize for o in operands)
    return pl.pallas_call(
        kernel,
        out_shape=out_shape,
        in_specs=[pl.BlockSpec(memory_space=pltpu.SMEM)]
        + [pl.BlockSpec(memory_space=pltpu.VMEM)] * len(operands),
        out_specs=[pl.BlockSpec(memory_space=pltpu.VMEM)] * len(out_shape)
        if several
        else pl.BlockSpec(memory_space=pltpu.VMEM),
        scratch_shapes=list(scratch),
        compiler_params=pltpu.CompilerParams(vmem_limit_bytes=32 * 1024 * 1024),
        cost_estimate=pl.CostEstimate(flops=flops, bytes_accessed=2 * moved, transcendentals=0),
    )(place, *operands)


def shifted(array, by, axis):
    n = lax.axis_size(axis)
    return lax.ppermute(array, axis, [(i, (i + by) % n) for i in range(n)])


def copies(array, n):
    return jnp.broadcast_to(array[None], (n, *array.shape))


def local(residual, projections, out_weight, out_grad):
    n_frame, n_y = lax.axis_size("frame"), lax.axis_size("y")
    n_clip = lax.axis_size("x") * lax.axis_size("zl")
    frame, core = lax.axis_index("frame"), lax.axis_index("core")
    place = jnp.stack([frame, core]).astype(jnp.int32)
    _, steps, patches, kinds, inner = projections.shape
    width = out_grad.shape[-1]
    frames = steps * n_frame
    tokens = steps * patches
    halves = n_y // n_frame
    product = 2 * n_frame * tokens * inner * width * halves

    there = [
        (
            f * n_y + y,
            (2 * f + n_frame // 2 - y // halves) % n_frame * n_y + halves * f + y % halves,
        )
        for f in range(n_frame)
        for y in range(n_y)
    ]
    back = [(b, a) for a, b in there]

    grad_moved = lax.ppermute(out_grad.reshape(tokens, width).T, ("frame", "y"), back)
    qkv_all = lax.all_gather(
        projections.reshape(projections.shape[1:]).transpose(0, 2, 1, 3), "frame", tiled=True
    )
    grad_own = lax.all_to_all(copies(grad_moved, n_y), "y", 0, 0, tiled=True)
    grad_other = lax.ppermute(grad_own, "core", SWAP)

    feature_rows = pl.pallas_call(
        attend_kernel,
        out_shape=jax.ShapeDtypeStruct((n_frame, tokens, inner), BF16),
        scratch_shapes=[pltpu.VMEM((frames, patches, inner), F32)],
        compiler_params=pltpu.CompilerParams(vmem_limit_bytes=32 * 1024 * 1024),
        cost_estimate=pl.CostEstimate(flops=product, bytes_accessed=2**22, transcendentals=0),
    )(qkv_all)

    weight_t = out_weight.T.reshape(halves, 2, width, inner)
    piece_shape = jax.ShapeDtypeStruct((n_y, width, tokens), BF16)
    pieces_other = whole(
        project_other_kernel, piece_shape, place, weight_t, feature_rows, flops=product
    )
    pieces_got = lax.ppermute(pieces_other, "core", SWAP)
    pieces = whole(
        project_own_kernel, piece_shape, place, weight_t, feature_rows, pieces_got, flops=product
    )
    pieces, grad_own, grad_other = lax.optimization_barrier((pieces, grad_own, grad_other))
    pieces = lax.all_to_all(pieces, "y", 0, 0, tiled=True)

    share = whole(
        attended_grad_kernel,
        jax.ShapeDtypeStruct((n_frame, tokens, inner), BF16),
        place,
        weight_t,
        grad_own,
        grad_other,
        flops=2 * product,
    )
    weight_part = whole(
        weight_grad_kernel,
        jax.ShapeDtypeStruct(out_weight.shape, BF16),
        place,
        feature_rows,
        grad_own,
        grad_other,
        scratch=[pltpu.VMEM((halves, 2, width, inner), F32)],
        flops=2 * product,
    )
    near = lax.ppermute(share, "frame", [(i, i ^ 1) for i in range(n_frame)])
    weight_part, near = lax.optimization_barrier((weight_part, near))
    near = (share.astype(F32) + near.astype(F32)).astype(BF16)
    far = lax.ppermute(near, "frame", [(i, n_frame - 1 - i) for i in range(n_frame)])

    weight_part, _, pieces = lax.optimization_barrier((weight_part, near, pieces))
    weight_part = weight_part.reshape(n_clip, inner // n_clip, -1)
    weight_part = lax.all_to_all(weight_part, CLIP, 0, 0, tiled=True)
    projected = pl.pallas_call(
        sum_kernel,
        out_shape=jax.ShapeDtypeStruct(pieces.shape[1:], BF16),
        cost_estimate=pl.CostEstimate(flops=product, bytes_accessed=2**20, transcendentals=0),
    )(pieces)
    projected = lax.ppermute(projected, ("frame", "y"), there)

    weight_sum = jnp.sum(weight_part.astype(F32), axis=0).astype(BF16)
    _, near, projected = lax.optimization_barrier((weight_sum, near, projected))
    weight_grad = lax.all_to_all(copies(weight_sum, n_clip), CLIP, 0, 0, tiled=True)
    weight_grad = weight_grad.reshape(out_weight.shape)

    projected = projected.T.reshape(residual.shape)
    block_out = (residual.astype(F32) + projected.astype(F32)).astype(BF16)
    qkv_grad = whole(
        lambda *refs: attend_back_kernel(patches // n_frame, *refs),
        jax.ShapeDtypeStruct((steps, kinds, patches, inner), BF16),
        place,
        qkv_all,
        near,
        far,
        scratch=[
            pltpu.VMEM((frames, patches, inner), F32),
            pltpu.VMEM((frames, kinds, patches, inner), F32),
        ],
        flops=400 * product,
    )
    qkv_grad = qkv_grad.transpose(0, 2, 1, 3).reshape(projections.shape)
    return (block_out, qkv_grad, weight_grad)


def solution(mesh):
    n_clip, n_frame, n_head = mesh.devices.shape
    fine = Mesh(mesh.devices.reshape(n_clip // 2, 2, n_frame, n_head // 2, 2), AXES)
    head = ("y", "core")
    in_specs = (
        P(CLIP, "frame", None, head),
        P(CLIP, "frame", None, None, head),
        P(head, "frame"),
        P(CLIP, "frame", None, head),
    )
    out_specs = (
        P(CLIP, "frame", None, head),
        P(CLIP, "frame", None, None, head),
        P(head, "frame"),
    )
    return jax.shard_map(local, mesh=fine, in_specs=in_specs, out_specs=out_specs, check_vma=False)
```

time: 133 us -> 122 us (0.917)
  the two profiles are of different devices: /device:TPU:34 before, /device:TPU:2 now
where the time goes in v3:
time: 122 us; the launch traced here: 121 us
  starting transfers between devices  53.5 us (44%)
  blocking collectives  23.4 us (19%)
  waiting for transfers between devices  20 us (16%)
  Pallas kernels  16.5 us (14%)
  local copies, waits for them, and re-layouts  6.31 us (5%)
    all_gather x1, blocking collectives, local(): lax.all_gather(projections.reshape(projections.shape[1:]).transpose(0, 2,...  23.4 us
    pallas_call x5, Pallas kernels, whole(): pl.pallas_call(kernel, out_shape=out_shape, in_specs=[pl.BlockSpec(memory...  12 us
    ppermute x1, waiting for transfers between devices, local(): near = lax.ppermute(share, 'frame', [(i, i ^ 1) for i in range(n_frame)])  9.41 us
    ppermute x1, starting transfers between devices, local(): lax.ppermute(out_grad.reshape(tokens, width).T, ('frame', 'y'), back)  7.73 us
    all_to_all x1, starting transfers between devices, local(): grad_own = lax.all_to_all(copies(grad_moved, n_y), 'y', 0, 0, tiled=True)  7.39 us
    all_to_all x1, starting transfers between devices, local(): pieces = lax.all_to_all(pieces, 'y', 0, 0, tiled=True)  7.23 us
    all_to_all x1, starting transfers between devices, local(): lax.all_to_all(copies(weight_sum, n_clip), CLIP, 0, 0, tiled=True)  6.78 us
    ppermute x1, waiting for transfers between devices, local(): lax.ppermute(out_grad.reshape(tokens, width).T, ('frame', 'y'), back)  5.61 us
  transfers between devices with their start and end apart: 10, of which 5 were waited for; matrix products, arithmetic and copies ran while one was open for 2% of the time, Pallas kernels for 14%

profile of v3, /device:TPU:2, one launch (start us, length us, event | category | flops | bytes accessed | tf_op | source)
XLA Modules:
  0.0 121.4 jit_solution(3939307947817332611)
XLA Ops:
  0.6 1.0 copy.14
  1.6 7.7 %collective-permute-start.1 = (bf16[320,128]{1,0:T(8,128)(2,1)S(1)}, bf16[320,128]{1,0:T(8,128)(2,1)S(1)}, u32[]{:S(2)}, u32[]{:S(2)}) collective-permute-start(bf16[320,128]{1,0:T(8,128)(2,1)S(1)} %bitcast.25), channel_id=1, source_target_pairs={{32,0},{34,2},{16,4},{18,6},{0,8},{2,10},{48,12},{50,14},{4,16},{6... | collective-permute-start | bytes 245768 | tf_op jit(solution)/shard_map/ppermute | solution.py:201
  9.4 5.6 %collective-permute-done.1 = bf16[320,128]{1,0:T(8,128)(2,1)S(1)} collective-permute-done((bf16[320,128]{1,0:T(8,128)(2,1)S(1)}, bf16[320,128]{1,0:T(8,128)(2,1)S(1)}, u32[]{:S(2)}, u32[]{:S(2)}) %collective-permute-start.1) | collective-permute-done | bytes 81952 | tf_op jit(solution)/shard_map/ppermute | solution.py:201
  15.0 1.0 broadcast_in_dim.4
  15.9 0.0 copy-start.1
  15.9 7.4 %all-to-all-start = ((bf16[8,320,128]{2,1,0:T(8,128)(2,1)}), bf16[8,320,128]{2,1,0:T(8,128)(2,1)S(1)}, u32[]{:S(2)}, u32[]{:S(2)}) async-start(bf16[8,320,128]{2,1,0:T(8,128)(2,1)} %broadcast_in_dim.4), calls=%async_computation | async-start | bytes 1310720 | tf_op jit(solution)/shard_map/all_to_all | solution.py:205
  23.3 0.0 copy-done.1
  23.3 0.0 copy-start.2
  23.4 0.2 copy.13
  23.6 0.7 copy-done.2
  24.3 23.4 %all_gather.3.all_ref.refs_1_ = bf16[16,3,32,256]{3,2,1,0:T(8,128)(2,1)S(1)} all-gather(bf16[4,3,32,256]{3,2,1,0:T(8,128)(2,1)S(1)} %bitcast.23), channel_id=1, replica_groups=mesh['x'=4,'zl'=2,'frame'=4,'y'=8,'core'=2] {'frame'}, dimensions={0}, use_global_device_ids=true | all-gather | bytes 983040 | tf_op jit(solution)/shard_map/all_gather | solution.py:202
  47.7 2.7 %shard_map.67.rows_ref = bf16[4,128,256]{2,1,0:T(8,128)(2,1)S(1)} custom-call(bf16[16,3,32,256]{3,2,1,0:T(8,128)(2,1)S(1)} %all_gather.3.all_ref.refs_1_), custom_call_target="tpu_custom_call" | custom-call | flops 167772160 | bytes 4194304 | tf_op jit(solution)/shard_map/pallas_call | solution.py:208
  50.4 0.1 pad_add_fusion.place_ref.refs_0_
  50.4 1.7 %shard_map.68 = bf16[8,320,128]{2,1,0:T(8,128)(2,1)} custom-call(s32[2]{0:T(128)S(1)} %pad_add_fusion.place_ref.refs_0_, bf16[2,2,320,256]{3,2,1,0:T(8,128)(2,1)S(1)} %bitcast.17, bf16[4,128,256]{2,1,0:T(8,128)(2,1)S(1)} %shard_map.67.rows_ref), custom_call_target="tpu_custom_call" | custom-call | flops 167772160 | bytes 1835008 | tf_op jit(solution)/shard_map/pallas_call | solution.py:156
  52.2 1.9 %collective-permute-start = (bf16[8,320,128]{2,1,0:T(8,128)(2,1)}, bf16[8,320,128]{2,1,0:T(8,128)(2,1)}, u32[]{:S(2)}, u32[]{:S(2)}) collective-permute-start(bf16[8,320,128]{2,1,0:T(8,128)(2,1)} %shard_map.68), channel_id=1, source_target_pairs={{0,1},{1,0},{2,3},{3,2},{4,5},{5,4},{6,7},{7,6},{8,9},{9,8},{10,11... | collective-permute-start | bytes 1966088 | tf_op jit(solution)/shard_map/ppermute | solution.py:221
  54.1 0.0 all-to-all-done.own_ref
  54.1 2.4 %collective-permute-start.2 = (bf16[8,320,128]{2,1,0:T(8,128)(2,1)S(1)}, bf16[8,320,128]{2,1,0:T(8,128)(2,1)S(1)}, u32[]{:S(2)}, u32[]{:S(2)}) collective-permute-start(bf16[8,320,128]{2,1,0:T(8,128)(2,1)S(1)} %all-to-all-done.own_ref), channel_id=1, source_target_pairs={{0,1},{1,0},{2,3},{3,2},{4,5},{5,4},{6,7},{7,6},{8,9},{9,8},{10,11... | collective-permute-start | bytes 1966088 | tf_op jit(solution)/shard_map/ppermute | solution.py:206
  56.5 0.0 collective-permute-done.got_ref
  56.5 1.5 %shard_map.69 = bf16[8,320,128]{2,1,0:T(8,128)(2,1)S(1)} custom-call(s32[2]{0:T(128)S(1)} %pad_add_fusion.place_ref.refs_0_, bf16[2,2,320,256]{3,2,1,0:T(8,128)(2,1)S(1)} %bitcast.18, bf16[4,128,256]{2,1,0:T(8,128)(2,1)S(1)} %shard_map.67.rows_ref, bf16[8,320,128]{2,1,0:T(8,128)(2,1)} %collective-permute-done.got_ref), custom_call_target="tpu_custom_call" | custom-call | flops 167772160 | bytes 3145728 | tf_op jit(solution)/shard_map/pallas_call | solution.py:156
  58.0 0.0 copy-start
  58.0 0.8 copy-done
  58.8 0.0 collective-permute-done.2.other_ref
  58.8 7.2 %all-to-all-start.1 = ((bf16[8,320,128]{2,1,0:T(8,128)(2,1)}), bf16[8,320,128]{2,1,0:T(8,128)(2,1)}, u32[]{:S(2)}, u32[]{:S(2)}) async-start(bf16[8,320,128]{2,1,0:T(8,128)(2,1)} %copy-done), calls=%async_computation.1 | async-start | bytes 1310720 | tf_op jit(solution)/shard_map/all_to_all | solution.py:226
  66.1 1.3 %shard_map.71 = bf16[4,128,256]{2,1,0:T(8,128)(2,1)S(1)} custom-call(s32[2]{0:T(128)S(1)} %pad_add_fusion.place_ref.refs_0_, bf16[2,2,320,256]{3,2,1,0:T(8,128)(2,1)S(1)} %bitcast.19, bf16[8,320,128]{2,1,0:T(8,128)(2,1)S(1)} %all-to-all-done.own_ref, bf16[8,320,128]{2,1,0:T(8,128)(2,1)S(1)} %collective-permute-done.2.other_ref), custom_call_target="tpu_custom_call" | custom-call | flops 335544320 | bytes 3932160 | tf_op jit(solution)/shard_map/pallas_call | solution.py:156
  67.4 4.8 %collective-permute-start.3 = (bf16[4,128,256]{2,1,0:T(8,128)(2,1)S(1)}, bf16[4,128,256]{2,1,0:T(8,128)(2,1)S(1)}, u32[]{:S(2)}, u32[]{:S(2)}) collective-permute-start(bf16[4,128,256]{2,1,0:T(8,128)(2,1)S(1)} %shard_map.71), channel_id=1, source_target_pairs={{0,16},{16,0},{32,48},{48,32},{1,17},{17,1},{33,49},{49,33},{2,18}... | collective-permute-start | bytes 786440 | tf_op jit(solution)/shard_map/ppermute | solution.py:247
  72.2 2.5 %shard_map.70 = bf16[256,1280]{1,0:T(8,128)(2,1)} custom-call(s32[2]{0:T(128)S(1)} %pad_add_fusion.place_ref.refs_0_, bf16[4,128,256]{2,1,0:T(8,128)(2,1)S(1)} %shard_map.67.rows_ref, bf16[8,320,128]{2,1,0:T(8,128)(2,1)S(1)} %all-to-all-done.own_ref, bf16[8,320,128]{2,1,0:T(8,128)(2,1)S(1)} %collective-permute-done.2.other_ref), custom_call_target="tpu_custom_call" | custom-call | flops 335544320 | bytes 3145728 | tf_op jit(solution)/shard_map/pallas_call | solution.py:156
  74.6 9.4 %collective-permute-done.3 = bf16[4,128,256]{2,1,0:T(8,128)(2,1)S(1)} collective-permute-done((bf16[4,128,256]{2,1,0:T(8,128)(2,1)S(1)}, bf16[4,128,256]{2,1,0:T(8,128)(2,1)S(1)}, u32[]{:S(2)}, u32[]{:S(2)}) %collective-permute-start.3) | collective-permute-done | bytes 262176 | tf_op jit(solution)/shard_map/ppermute | solution.py:247
  84.1 0.1 add_convert_fusion.refs_2_
  84.1 2.6 %all-to-all-done.1.parts_ref = bf16[8,320,128]{2,1,0:T(8,128)(2,1)} async-done(((bf16[8,320,128]{2,1,0:T(8,128)(2,1)}), bf16[8,320,128]{2,1,0:T(8,128)(2,1)}, u32[]{:S(2)}, u32[]{:S(2)}) %all-to-all-start.1) | async-done | bytes 655392 | tf_op jit(solution)/shard_map/all_to_all | solution.py:226
  86.8 4.9 %all-to-all-start.2 = ((bf16[8,32,1280]{2,1,0:T(8,128)(2,1)}), bf16[8,32,1280]{2,1,0:T(8,128)(2,1)S(1)}, u32[]{:S(2)}, u32[]{:S(2)}) async-start(bf16[8,32,1280]{2,1,0:T(8,128)(2,1)} %bitcast.8), calls=%async_computation.2 | async-start | bytes 1310720 | tf_op jit(solution)/shard_map/all_to_all | solution.py:254
  91.7 5.3 %collective-permute-start.5 = (bf16[4,128,256]{2,1,0:T(8,128)(2,1)S(1)}, bf16[4,128,256]{2,1,0:T(8,128)(2,1)S(1)}, u32[]{:S(2)}, u32[]{:S(2)}) collective-permute-start(bf16[4,128,256]{2,1,0:T(8,128)(2,1)S(1)} %add_convert_fusion.refs_2_), channel_id=1, source_target_pairs={{0,48},{16,32},{32,16},{48,0},{1,49},{17,33},{33,17},{49,1},{2,50}... | collective-permute-start | bytes 786440 | tf_op jit(solution)/shard_map/ppermute | solution.py:250
  97.0 1.8 %shard_map.72 = bf16[320,128]{1,0:T(8,128)(2,1)} custom-call(bf16[8,320,128]{2,1,0:T(8,128)(2,1)} %all-to-all-done.1.parts_ref), custom_call_target="tpu_custom_call" | custom-call | flops 167772160 | bytes 1048576 | tf_op jit(solution)/shard_map/pallas_call | solution.py:255
  98.8 5.1 %collective-permute-start.4 = (bf16[320,128]{1,0:T(8,128)(2,1)}, bf16[320,128]{1,0:T(8,128)(2,1)S(1)}, u32[]{:S(2)}, u32[]{:S(2)}) collective-permute-start(bf16[320,128]{1,0:T(8,128)(2,1)} %shard_map.72), channel_id=1, source_target_pairs={{0,32},{2,34},{4,16},{6,18},{8,0},{10,2},{12,48},{14,50},{16,4},{1... | collective-permute-start | bytes 245768 | tf_op jit(solution)/shard_map/ppermute | solution.py:260
  103.9 1.6 %all-to-all-done.2 = bf16[8,32,1280]{2,1,0:T(8,128)(2,1)S(1)} async-done(((bf16[8,32,1280]{2,1,0:T(8,128)(2,1)}), bf16[8,32,1280]{2,1,0:T(8,128)(2,1)S(1)}, u32[]{:S(2)}, u32[]{:S(2)}) %all-to-all-start.2) | async-done | bytes 655392 | tf_op jit(solution)/shard_map/all_to_all | solution.py:254
  105.4 0.1 reduce_sum.12
  105.5 0.9 broadcast_in_dim.5
  106.4 6.8 %all-to-all-start.3 = ((bf16[8,32,1280]{2,1,0:T(8,128)(2,1)}), bf16[8,32,1280]{2,1,0:T(8,128)(2,1)S(1)}, u32[]{:S(2)}, u32[]{:S(2)}) async-start(bf16[8,32,1280]{2,1,0:T(8,128)(2,1)} %broadcast_in_dim.5), calls=%async_computation.3 | async-start | bytes 1310720 | tf_op jit(solution)/shard_map/all_to_all | solution.py:264
  113.2 0.0 collective-permute-done.4
  113.2 0.0 collective-permute-done.5.refs_3_
  113.2 5.0 %shard_map.73 = bf16[4,3,32,256]{3,2,1,0:T(8,128)(2,1)} custom-call(s32[2]{0:T(128)S(1)} %pad_add_fusion.place_ref.refs_0_, bf16[16,3,32,256]{3,2,1,0:T(8,128)(2,1)S(1)} %all_gather.3.all_ref.refs_1_, bf16[4,128,256]{2,1,0:T(8,128)(2,1)S(1)} %add_convert_fusion.refs_2_, bf16[4,128,256]{2,1,0:T(8,128)(2,1)S(1)} %collective-permute-done.5.refs_3_), custom_call_target="tpu_custom_call" | custom-call | flops 67108864000 | bytes 2621440 | tf_op jit(solution)/shard_map/pallas_call | solution.py:156
  118.2 0.0 copy-start.3
  118.2 0.1 copy.15
  118.4 0.8 copy-done.3
  119.1 0.7 add_convert_fusion.1
  119.8 0.8 all-to-all-done.3
  120.5 0.8 copy.17
  (1 shorter events, 0.0 us)
Async XLA Ops:
  1.6 13.4 %collective-permute-start.1 = (bf16[320,128]{1,0:T(8,128)(2,1)S(1)}, bf16[320,128]{1,0:T(8,128)(2,1)S(1)}, u32[]{:S(2)}, u32[]{:S(2)}) collective-permute-start(bf16[320,128]{1,0:T(8,128)(2,1)S(1)} %bitcast.25), channel_id=1, source_target_pairs={{32,0},{34,2},{16,4},{18,6},{0,8},{2,10},{48,12},{50,14},{4,16},{6... | collective-permute-start | bytes 245768 | tf_op jit(solution)/shard_map/ppermute | solution.py:201
  15.9 7.4 %copy-start.1 = (bf16[256,1280]{1,0:T(8,128)(2,1)S(1)}, bf16[256,1280]{1,0:T(8,128)(2,1)}, u32[]{:S(2)}) copy-start(bf16[256,1280]{1,0:T(8,128)(2,1)} %param.6) | copy-start | bytes 1966084
  15.9 38.2 %all-to-all-start = ((bf16[8,320,128]{2,1,0:T(8,128)(2,1)}), bf16[8,320,128]{2,1,0:T(8,128)(2,1)S(1)}, u32[]{:S(2)}, u32[]{:S(2)}) async-start(bf16[8,320,128]{2,1,0:T(8,128)(2,1)} %broadcast_in_dim.4), calls=%async_computation | async-start | bytes 1310720 | tf_op jit(solution)/shard_map/all_to_all | solution.py:205
  23.3 0.9 copy-start.2
  52.2 4.3 %collective-permute-start = (bf16[8,320,128]{2,1,0:T(8,128)(2,1)}, bf16[8,320,128]{2,1,0:T(8,128)(2,1)}, u32[]{:S(2)}, u32[]{:S(2)}) collective-permute-start(bf16[8,320,128]{2,1,0:T(8,128)(2,1)} %shard_map.68), channel_id=1, source_target_pairs={{0,1},{1,0},{2,3},{3,2},{4,5},{5,4},{6,7},{7,6},{8,9},{9,8},{10,11... | collective-permute-start | bytes 1966088 | tf_op jit(solution)/shard_map/ppermute | solution.py:221
  54.1 4.7 %collective-permute-start.2 = (bf16[8,320,128]{2,1,0:T(8,128)(2,1)S(1)}, bf16[8,320,128]{2,1,0:T(8,128)(2,1)S(1)}, u32[]{:S(2)}, u32[]{:S(2)}) collective-permute-start(bf16[8,320,128]{2,1,0:T(8,128)(2,1)S(1)} %all-to-all-done.own_ref), channel_id=1, source_target_pairs={{0,1},{1,0},{2,3},{3,2},{4,5},{5,4},{6,7},{7,6},{8,9},{9,8},{10,11... | collective-permute-start | bytes 1966088 | tf_op jit(solution)/shard_map/ppermute | solution.py:206
  58.0 0.8 copy-start
  58.8 27.9 %all-to-all-start.1 = ((bf16[8,320,128]{2,1,0:T(8,128)(2,1)}), bf16[8,320,128]{2,1,0:T(8,128)(2,1)}, u32[]{:S(2)}, u32[]{:S(2)}) async-start(bf16[8,320,128]{2,1,0:T(8,128)(2,1)} %copy-done), calls=%async_computation.1 | async-start | bytes 1310720 | tf_op jit(solution)/shard_map/all_to_all | solution.py:226
  67.4 16.7 %collective-permute-start.3 = (bf16[4,128,256]{2,1,0:T(8,128)(2,1)S(1)}, bf16[4,128,256]{2,1,0:T(8,128)(2,1)S(1)}, u32[]{:S(2)}, u32[]{:S(2)}) collective-permute-start(bf16[4,128,256]{2,1,0:T(8,128)(2,1)S(1)} %shard_map.71), channel_id=1, source_target_pairs={{0,16},{16,0},{32,48},{48,32},{1,17},{17,1},{33,49},{49,33},{2,18}... | collective-permute-start | bytes 786440 | tf_op jit(solution)/shard_map/ppermute | solution.py:247
  86.8 18.7 %all-to-all-start.2 = ((bf16[8,32,1280]{2,1,0:T(8,128)(2,1)}), bf16[8,32,1280]{2,1,0:T(8,128)(2,1)S(1)}, u32[]{:S(2)}, u32[]{:S(2)}) async-start(bf16[8,32,1280]{2,1,0:T(8,128)(2,1)} %bitcast.8), calls=%async_computation.2 | async-start | bytes 1310720 | tf_op jit(solution)/shard_map/all_to_all | solution.py:254
  91.7 21.5 %collective-permute-start.5 = (bf16[4,128,256]{2,1,0:T(8,128)(2,1)S(1)}, bf16[4,128,256]{2,1,0:T(8,128)(2,1)S(1)}, u32[]{:S(2)}, u32[]{:S(2)}) collective-permute-start(bf16[4,128,256]{2,1,0:T(8,128)(2,1)S(1)} %add_convert_fusion.refs_2_), channel_id=1, source_target_pairs={{0,48},{16,32},{32,16},{48,0},{1,49},{17,33},{33,17},{49,1},{2,50}... | collective-permute-start | bytes 786440 | tf_op jit(solution)/shard_map/ppermute | solution.py:250
  98.8 14.4 %collective-permute-start.4 = (bf16[320,128]{1,0:T(8,128)(2,1)}, bf16[320,128]{1,0:T(8,128)(2,1)S(1)}, u32[]{:S(2)}, u32[]{:S(2)}) collective-permute-start(bf16[320,128]{1,0:T(8,128)(2,1)} %shard_map.72), channel_id=1, source_target_pairs={{0,32},{2,34},{4,16},{6,18},{8,0},{10,2},{12,48},{14,50},{16,4},{1... | collective-permute-start | bytes 245768 | tf_op jit(solution)/shard_map/ppermute | solution.py:260
  106.4 14.1 %all-to-all-start.3 = ((bf16[8,32,1280]{2,1,0:T(8,128)(2,1)}), bf16[8,32,1280]{2,1,0:T(8,128)(2,1)S(1)}, u32[]{:S(2)}, u32[]{:S(2)}) async-start(bf16[8,32,1280]{2,1,0:T(8,128)(2,1)} %broadcast_in_dim.5), calls=%async_computation.3 | async-start | bytes 1310720 | tf_op jit(solution)/shard_map/all_to_all | solution.py:264
  118.2 0.9 copy-start.3

commit v4 on v3

--- a/solution.py
+++ b/solution.py
@@ -162,7 +162,7 @@
         if several
         else pl.BlockSpec(memory_space=pltpu.VMEM),
         scratch_shapes=list(scratch),
-        compiler_params=pltpu.CompilerParams(vmem_limit_bytes=32 * 1024 * 1024),
+        compiler_params=pltpu.CompilerParams(vmem_limit_bytes=16 * 1024 * 1024),
         cost_estimate=pl.CostEstimate(flops=flops, bytes_accessed=2 * moved, transcendentals=0),
     )(place, *operands)
 
@@ -202,14 +202,14 @@
     qkv_all = lax.all_gather(
         projections.reshape(projections.shape[1:]).transpose(0, 2, 1, 3), "frame", tiled=True
     )
+    grad_moved, qkv_all = lax.optimization_barrier((grad_moved, qkv_all))
     grad_own = lax.all_to_all(copies(grad_moved, n_y), "y", 0, 0, tiled=True)
-    grad_other = lax.ppermute(grad_own, "core", SWAP)
 
     feature_rows = pl.pallas_call(
         attend_kernel,
         out_shape=jax.ShapeDtypeStruct((n_frame, tokens, inner), BF16),
         scratch_shapes=[pltpu.VMEM((frames, patches, inner), F32)],
-        compiler_params=pltpu.CompilerParams(vmem_limit_bytes=32 * 1024 * 1024),
+        compiler_params=pltpu.CompilerParams(vmem_limit_bytes=16 * 1024 * 1024),
         cost_estimate=pl.CostEstimate(flops=product, bytes_accessed=2**22, transcendentals=0),
     )(qkv_all)
 
@@ -222,8 +222,9 @@
     pieces = whole(
         project_own_kernel, piece_shape, place, weight_t, feature_rows, pieces_got, flops=product
     )
-    pieces, grad_own, grad_other = lax.optimization_barrier((pieces, grad_own, grad_other))
+    pieces, grad_own = lax.optimization_barrier((pieces, grad_own))
     pieces = lax.all_to_all(pieces, "y", 0, 0, tiled=True)
+    grad_other = lax.ppermute(grad_own, "core", SWAP)
 
     share = whole(
         attended_grad_kernel,
@@ -245,27 +246,25 @@
         flops=2 * product,
     )
     near = lax.ppermute(share, "frame", [(i, i ^ 1) for i in range(n_frame)])
-    weight_part, near = lax.optimization_barrier((weight_part, near))
-    near = (share.astype(F32) + near.astype(F32)).astype(BF16)
-    far = lax.ppermute(near, "frame", [(i, n_frame - 1 - i) for i in range(n_frame)])
-
-    weight_part, _, pieces = lax.optimization_barrier((weight_part, near, pieces))
+    weight_part, _, pieces = lax.optimization_barrier((weight_part, share, pieces))
     weight_part = weight_part.reshape(n_clip, inner // n_clip, -1)
     weight_part = lax.all_to_all(weight_part, CLIP, 0, 0, tiled=True)
     projected = pl.pallas_call(
         sum_kernel,
         out_shape=jax.ShapeDtypeStruct(pieces.shape[1:], BF16),
-        cost_estimate=pl.CostEstimate(flops=product, bytes_accessed=2**20, transcendentals=0),
+        compiler_params=pltpu.CompilerParams(vmem_limit_bytes=16 * 1024 * 1024),
+        cost_estimate=pl.CostEstimate(flops=400 * product, bytes_accessed=2**20, transcendentals=0),
     )(pieces)
+    projected, near = lax.optimization_barrier((projected, near))
     projected = lax.ppermute(projected, ("frame", "y"), there)
+    near = (share.astype(F32) + near.astype(F32)).astype(BF16)
+    far = lax.ppermute(near, "frame", [(i, n_frame - 1 - i) for i in range(n_frame)])
 
     weight_sum = jnp.sum(weight_part.astype(F32), axis=0).astype(BF16)
-    _, near, projected = lax.optimization_barrier((weight_sum, near, projected))
+    _, near = lax.optimization_barrier((weight_sum, near))
     weight_grad = lax.all_to_all(copies(weight_sum, n_clip), CLIP, 0, 0, tiled=True)
     weight_grad = weight_grad.reshape(out_weight.shape)
 
-    projected = projected.T.reshape(residual.shape)
-    block_out = (residual.astype(F32) + projected.astype(F32)).astype(BF16)
     qkv_grad = whole(
         lambda *refs: attend_back_kernel(patches // n_frame, *refs),
         jax.ShapeDtypeStruct((steps, kinds, patches, inner), BF16),
@@ -279,6 +278,9 @@
         ],
         flops=400 * product,
     )
+    projected, qkv_grad = lax.optimization_barrier((projected, qkv_grad))
+    projected = projected.T.reshape(residual.shape)
+    block_out = (residual.astype(F32) + projected.astype(F32)).astype(BF16)
     qkv_grad = qkv_grad.transpose(0, 2, 1, 3).reshape(projections.shape)
     return (block_out, qkv_grad, weight_grad)
 

time: 122 us -> 116 us (0.951)
  the two profiles are of different devices: /device:TPU:2 before, /device:TPU:8 now
where the time goes in v4:
time: 116 us; the launch traced here: 115 us
  starting transfers between devices  49.7 us (43%)
  blocking collectives  23.5 us (20%)
  waiting for transfers between devices  21.5 us (19%)
  Pallas kernels  14.2 us (12%)
  local copies, waits for them, and re-layouts  4.79 us (4%)
    all_gather x1, blocking collectives, local(): lax.all_gather(projections.reshape(projections.shape[1:]).transpose(0, 2,...  23.5 us
    pallas_call x5, Pallas kernels, whole(): pl.pallas_call(kernel, out_shape=out_shape, in_specs=[pl.BlockSpec(memory...  11.4 us
    all_to_all x1, starting transfers between devices, local(): grad_own = lax.all_to_all(copies(grad_moved, n_y), 'y', 0, 0, tiled=True)  8.85 us
    all_to_all x1, waiting for transfers between devices, local(): grad_own = lax.all_to_all(copies(grad_moved, n_y), 'y', 0, 0, tiled=True)  7.32 us
    ppermute x1, starting transfers between devices, local(): projected = lax.ppermute(projected, ('frame', 'y'), there)  7.2 us
    all_to_all x1, starting transfers between devices, local(): weight_part = lax.all_to_all(weight_part, CLIP, 0, 0, tiled=True)  7 us
    ppermute x1, starting transfers between devices, local(): lax.ppermute(out_grad.reshape(tokens, width).T, ('frame', 'y'), back)  6.83 us
    all_to_all x1, waiting for transfers between devices, local(): pieces = lax.all_to_all(pieces, 'y', 0, 0, tiled=True)  5.8 us
  transfers between devices with their start and end apart: 10, of which 6 were waited for; matrix products, arithmetic and copies ran while one was open for 2% of the time, Pallas kernels for 12%

profile of v4, /device:TPU:8, one launch (start us, length us, event | category | flops | bytes accessed | tf_op | source)
XLA Modules:
  0.0 115.4 jit_solution(505880213986526670)
XLA Ops:
  0.6 1.0 copy.13
  1.6 6.8 %collective-permute-start = (bf16[320,128]{1,0:T(8,128)(2,1)S(1)}, bf16[320,128]{1,0:T(8,128)(2,1)S(1)}, u32[]{:S(2)}, u32[]{:S(2)}) collective-permute-start(bf16[320,128]{1,0:T(8,128)(2,1)S(1)} %bitcast.25), channel_id=1, source_target_pairs={{32,0},{34,2},{16,4},{18,6},{0,8},{2,10},{48,12},{50,14},{4,16},{6... | collective-permute-start | bytes 245768 | tf_op jit(solution)/shard_map/ppermute | solution.py:201
  8.5 23.5 %all_gather.3.all_ref.refs_1_ = bf16[16,3,32,256]{3,2,1,0:T(8,128)(2,1)S(1)} all-gather(bf16[4,3,32,256]{3,2,1,0:T(8,128)(2,1)} %bitcast.23), channel_id=1, replica_groups=mesh['x'=4,'zl'=2,'frame'=4,'y'=8,'core'=2] {'frame'}, dimensions={0}, use_global_device_ids=true | all-gather | bytes 983040 | tf_op jit(solution)/shard_map/all_gather | solution.py:202
  32.0 0.0 collective-permute-done
  32.0 0.9 broadcast_in_dim.4
  32.9 0.0 copy-start
  33.0 8.9 %all-to-all-start = ((bf16[8,320,128]{2,1,0:T(8,128)(2,1)}), bf16[8,320,128]{2,1,0:T(8,128)(2,1)S(1)}, u32[]{:S(2)}, u32[]{:S(2)}) async-start(bf16[8,320,128]{2,1,0:T(8,128)(2,1)} %broadcast_in_dim.4), calls=%async_computation | async-start | bytes 1310720 | tf_op jit(solution)/shard_map/all_to_all | solution.py:206
  41.8 0.0 copy-done
  41.8 0.2 copy.14
  42.0 0.1 pad_add_fusion.place_ref.refs_0_
  42.1 2.7 %shard_map.67.rows_ref = bf16[4,128,256]{2,1,0:T(8,128)(2,1)S(1)} custom-call(bf16[16,3,32,256]{3,2,1,0:T(8,128)(2,1)S(1)} %all_gather.3.all_ref.refs_1_), custom_call_target="tpu_custom_call" | custom-call | flops 167772160 | bytes 4194304 | tf_op jit(solution)/shard_map/pallas_call | solution.py:208
  44.8 0.9 shard_map.68
  45.7 1.9 %collective-permute-start.1 = (bf16[8,320,128]{2,1,0:T(8,128)(2,1)S(1)}, bf16[8,320,128]{2,1,0:T(8,128)(2,1)S(1)}, u32[]{:S(2)}, u32[]{:S(2)}) collective-permute-start(bf16[8,320,128]{2,1,0:T(8,128)(2,1)S(1)} %shard_map.68), channel_id=1, source_target_pairs={{0,1},{1,0},{2,3},{3,2},{4,5},{5,4},{6,7},{7,6},{8,9},{9,8},{10,11... | collective-permute-start | bytes 1966088 | tf_op jit(solution)/shard_map/ppermute | solution.py:221
  47.7 2.1 %collective-permute-done.1.got_ref = bf16[8,320,128]{2,1,0:T(8,128)(2,1)S(1)} collective-permute-done((bf16[8,320,128]{2,1,0:T(8,128)(2,1)S(1)}, bf16[8,320,128]{2,1,0:T(8,128)(2,1)S(1)}, u32[]{:S(2)}, u32[]{:S(2)}) %collective-permute-start.1) | collective-permute-done | bytes 655392 | tf_op jit(solution)/shard_map/ppermute | solution.py:221
  49.7 1.7 %shard_map.69 = bf16[8,320,128]{2,1,0:T(8,128)(2,1)} custom-call(s32[2]{0:T(128)S(1)} %pad_add_fusion.place_ref.refs_0_, bf16[2,2,320,256]{3,2,1,0:T(8,128)(2,1)S(1)} %bitcast.18, bf16[4,128,256]{2,1,0:T(8,128)(2,1)S(1)} %shard_map.67.rows_ref, bf16[8,320,128]{2,1,0:T(8,128)(2,1)S(1)} %collective-permute-done.1.got_ref), custom_call_target="tpu_custom_call" | custom-call | flops 167772160 | bytes 3145728 | tf_op jit(solution)/shard_map/pallas_call | solution.py:156
  51.5 7.3 %all-to-all-done.own_ref = bf16[8,320,128]{2,1,0:T(8,128)(2,1)S(1)} async-done(((bf16[8,320,128]{2,1,0:T(8,128)(2,1)}), bf16[8,320,128]{2,1,0:T(8,128)(2,1)S(1)}, u32[]{:S(2)}, u32[]{:S(2)}) %all-to-all-start) | async-done | bytes 655392 | tf_op jit(solution)/shard_map/all_to_all | solution.py:206
  58.8 5.0 %all-to-all-start.1 = ((bf16[8,320,128]{2,1,0:T(8,128)(2,1)}), bf16[8,320,128]{2,1,0:T(8,128)(2,1)S(1)}, u32[]{:S(2)}, u32[]{:S(2)}) async-start(bf16[8,320,128]{2,1,0:T(8,128)(2,1)} %shard_map.69), calls=%async_computation.1 | async-start | bytes 1310720 | tf_op jit(solution)/shard_map/all_to_all | solution.py:226
  63.7 1.9 %collective-permute-start.2 = (bf16[8,320,128]{2,1,0:T(8,128)(2,1)S(1)}, bf16[8,320,128]{2,1,0:T(8,128)(2,1)S(1)}, u32[]{:S(2)}, u32[]{:S(2)}) collective-permute-start(bf16[8,320,128]{2,1,0:T(8,128)(2,1)S(1)} %all-to-all-done.own_ref), channel_id=1, source_target_pairs={{0,1},{1,0},{2,3},{3,2},{4,5},{5,4},{6,7},{7,6},{8,9},{9,8},{10,11... | collective-permute-start | bytes 1966088 | tf_op jit(solution)/shard_map/ppermute | solution.py:227
  65.6 2.1 %collective-permute-done.2.other_ref = bf16[8,320,128]{2,1,0:T(8,128)(2,1)S(1)} collective-permute-done((bf16[8,320,128]{2,1,0:T(8,128)(2,1)S(1)}, bf16[8,320,128]{2,1,0:T(8,128)(2,1)S(1)}, u32[]{:S(2)}, u32[]{:S(2)}) %collective-permute-start.2) | collective-permute-done | bytes 655392 | tf_op jit(solution)/shard_map/ppermute | solution.py:227
  67.7 1.3 %shard_map.71 = bf16[4,128,256]{2,1,0:T(8,128)(2,1)S(1)} custom-call(s32[2]{0:T(128)S(1)} %pad_add_fusion.place_ref.refs_0_, bf16[2,2,320,256]{3,2,1,0:T(8,128)(2,1)S(1)} %bitcast.19, bf16[8,320,128]{2,1,0:T(8,128)(2,1)S(1)} %all-to-all-done.own_ref, bf16[8,320,128]{2,1,0:T(8,128)(2,1)S(1)} %collective-permute-done.2.other_ref), custom_call_target="tpu_custom_call" | custom-call | flops 335544320 | bytes 3932160 | tf_op jit(solution)/shard_map/pallas_call | solution.py:156
  69.0 2.9 %collective-permute-start.3 = (bf16[4,128,256]{2,1,0:T(8,128)(2,1)S(1)}, bf16[4,128,256]{2,1,0:T(8,128)(2,1)S(1)}, u32[]{:S(2)}, u32[]{:S(2)}) collective-permute-start(bf16[4,128,256]{2,1,0:T(8,128)(2,1)S(1)} %shard_map.71), channel_id=1, source_target_pairs={{0,16},{16,0},{32,48},{48,32},{1,17},{17,1},{33,49},{49,33},{2,18}... | collective-permute-start | bytes 786440 | tf_op jit(solution)/shard_map/ppermute | solution.py:248
  72.0 2.5 %shard_map.70 = bf16[256,1280]{1,0:T(8,128)(2,1)} custom-call(s32[2]{0:T(128)S(1)} %pad_add_fusion.place_ref.refs_0_, bf16[4,128,256]{2,1,0:T(8,128)(2,1)S(1)} %shard_map.67.rows_ref, bf16[8,320,128]{2,1,0:T(8,128)(2,1)S(1)} %all-to-all-done.own_ref, bf16[8,320,128]{2,1,0:T(8,128)(2,1)S(1)} %collective-permute-done.2.other_ref), custom_call_target="tpu_custom_call" | custom-call | flops 335544320 | bytes 3145728 | tf_op jit(solution)/shard_map/pallas_call | solution.py:156
  74.4 5.8 %all-to-all-done.1.parts_ref = bf16[8,320,128]{2,1,0:T(8,128)(2,1)S(1)} async-done(((bf16[8,320,128]{2,1,0:T(8,128)(2,1)}), bf16[8,320,128]{2,1,0:T(8,128)(2,1)S(1)}, u32[]{:S(2)}, u32[]{:S(2)}) %all-to-all-start.1) | async-done | bytes 655392 | tf_op jit(solution)/shard_map/all_to_all | solution.py:226
  80.2 7.0 %all-to-all-start.2 = ((bf16[8,32,1280]{2,1,0:T(8,128)(2,1)}), bf16[8,32,1280]{2,1,0:T(8,128)(2,1)S(1)}, u32[]{:S(2)}, u32[]{:S(2)}) async-start(bf16[8,32,1280]{2,1,0:T(8,128)(2,1)} %bitcast.8), calls=%async_computation.2 | async-start | bytes 1310720 | tf_op jit(solution)/shard_map/all_to_all | solution.py:251
  87.2 0.1 shard_map.72
  87.3 0.0 collective-permute-done.3
  87.3 0.1 add_convert_fusion.refs_2_
  87.4 2.7 %collective-permute-start.5 = (bf16[4,128,256]{2,1,0:T(8,128)(2,1)S(1)}, bf16[4,128,256]{2,1,0:T(8,128)(2,1)S(1)}, u32[]{:S(2)}, u32[]{:S(2)}) collective-permute-start(bf16[4,128,256]{2,1,0:T(8,128)(2,1)S(1)} %add_convert_fusion.refs_2_), channel_id=1, source_target_pairs={{0,48},{16,32},{32,16},{48,0},{1,49},{17,33},{33,17},{49,1},{2,50}... | collective-permute-start | bytes 786440 | tf_op jit(solution)/shard_map/ppermute | solution.py:261
  90.1 7.2 %collective-permute-start.4 = (bf16[320,128]{1,0:T(8,128)(2,1)S(1)}, bf16[320,128]{1,0:T(8,128)(2,1)S(1)}, u32[]{:S(2)}, u32[]{:S(2)}) collective-permute-start(bf16[320,128]{1,0:T(8,128)(2,1)S(1)} %shard_map.72), channel_id=1, source_target_pairs={{0,32},{2,34},{4,16},{6,18},{8,0},{10,2},{12,48},{14,50},{16,4},{1... | collective-permute-start | bytes 245768 | tf_op jit(solution)/shard_map/ppermute | solution.py:259
  97.4 1.5 %all-to-all-done.2 = bf16[8,32,1280]{2,1,0:T(8,128)(2,1)S(1)} async-done(((bf16[8,32,1280]{2,1,0:T(8,128)(2,1)}), bf16[8,32,1280]{2,1,0:T(8,128)(2,1)S(1)}, u32[]{:S(2)}, u32[]{:S(2)}) %all-to-all-start.2) | async-done | bytes 655392 | tf_op jit(solution)/shard_map/all_to_all | solution.py:251
  98.8 0.1 reduce_sum.12
  98.9 0.9 broadcast_in_dim.5
  99.8 5.4 %all-to-all-start.3 = ((bf16[8,32,1280]{2,1,0:T(8,128)(2,1)}), bf16[8,32,1280]{2,1,0:T(8,128)(2,1)S(1)}, u32[]{:S(2)}, u32[]{:S(2)}) async-start(bf16[8,32,1280]{2,1,0:T(8,128)(2,1)} %broadcast_in_dim.5), calls=%async_computation.3 | async-start | bytes 1310720 | tf_op jit(solution)/shard_map/all_to_all | solution.py:265
  105.2 0.0 collective-permute-done.5.refs_3_
  105.2 5.0 %shard_map.73 = bf16[4,3,32,256]{3,2,1,0:T(8,128)(2,1)} custom-call(s32[2]{0:T(128)S(1)} %pad_add_fusion.place_ref.refs_0_, bf16[16,3,32,256]{3,2,1,0:T(8,128)(2,1)S(1)} %all_gather.3.all_ref.refs_1_, bf16[4,128,256]{2,1,0:T(8,128)(2,1)S(1)} %add_convert_fusion.refs_2_, bf16[4,128,256]{2,1,0:T(8,128)(2,1)S(1)} %collective-permute-done.5.refs_3_), custom_call_target="tpu_custom_call" | custom-call | flops 67108864000 | bytes 2621440 | tf_op jit(solution)/shard_map/pallas_call | solution.py:156
  110.2 0.0 collective-permute-done.4
  110.2 0.0 copy-start.1
  110.2 0.1 copy.15
  110.3 0.8 copy-done.1
  111.1 0.7 add_convert_fusion.1
  111.7 2.8 %all-to-all-done.3 = bf16[8,32,1280]{2,1,0:T(8,128)(2,1)S(1)} async-done(((bf16[8,32,1280]{2,1,0:T(8,128)(2,1)}), bf16[8,32,1280]{2,1,0:T(8,128)(2,1)S(1)}, u32[]{:S(2)}, u32[]{:S(2)}) %all-to-all-start.3) | async-done | bytes 655392 | tf_op jit(solution)/shard_map/all_to_all | solution.py:265
  114.6 0.8 copy.17
  (1 shorter events, 0.0 us)
Async XLA Ops:
  1.6 30.4 %collective-permute-start = (bf16[320,128]{1,0:T(8,128)(2,1)S(1)}, bf16[320,128]{1,0:T(8,128)(2,1)S(1)}, u32[]{:S(2)}, u32[]{:S(2)}) collective-permute-start(bf16[320,128]{1,0:T(8,128)(2,1)S(1)} %bitcast.25), channel_id=1, source_target_pairs={{32,0},{34,2},{16,4},{18,6},{0,8},{2,10},{48,12},{50,14},{4,16},{6... | collective-permute-start | bytes 245768 | tf_op jit(solution)/shard_map/ppermute | solution.py:201
  32.9 8.9 %copy-start = (bf16[256,1280]{1,0:T(8,128)(2,1)S(1)}, bf16[256,1280]{1,0:T(8,128)(2,1)}, u32[]{:S(2)}) copy-start(bf16[256,1280]{1,0:T(8,128)(2,1)} %param.6) | copy-start | bytes 1966084
  33.0 25.8 %all-to-all-start = ((bf16[8,320,128]{2,1,0:T(8,128)(2,1)}), bf16[8,320,128]{2,1,0:T(8,128)(2,1)S(1)}, u32[]{:S(2)}, u32[]{:S(2)}) async-start(bf16[8,320,128]{2,1,0:T(8,128)(2,1)} %broadcast_in_dim.4), calls=%async_computation | async-start | bytes 1310720 | tf_op jit(solution)/shard_map/all_to_all | solution.py:206
  45.7 4.0 %collective-permute-start.1 = (bf16[8,320,128]{2,1,0:T(8,128)(2,1)S(1)}, bf16[8,320,128]{2,1,0:T(8,128)(2,1)S(1)}, u32[]{:S(2)}, u32[]{:S(2)}) collective-permute-start(bf16[8,320,128]{2,1,0:T(8,128)(2,1)S(1)} %shard_map.68), channel_id=1, source_target_pairs={{0,1},{1,0},{2,3},{3,2},{4,5},{5,4},{6,7},{7,6},{8,9},{9,8},{10,11... | collective-permute-start | bytes 1966088 | tf_op jit(solution)/shard_map/ppermute | solution.py:221
  58.8 21.5 %all-to-all-start.1 = ((bf16[8,320,128]{2,1,0:T(8,128)(2,1)}), bf16[8,320,128]{2,1,0:T(8,128)(2,1)S(1)}, u32[]{:S(2)}, u32[]{:S(2)}) async-start(bf16[8,320,128]{2,1,0:T(8,128)(2,1)} %shard_map.69), calls=%async_computation.1 | async-start | bytes 1310720 | tf_op jit(solution)/shard_map/all_to_all | solution.py:226
  63.7 4.0 %collective-permute-start.2 = (bf16[8,320,128]{2,1,0:T(8,128)(2,1)S(1)}, bf16[8,320,128]{2,1,0:T(8,128)(2,1)S(1)}, u32[]{:S(2)}, u32[]{:S(2)}) collective-permute-start(bf16[8,320,128]{2,1,0:T(8,128)(2,1)S(1)} %all-to-all-done.own_ref), channel_id=1, source_target_pairs={{0,1},{1,0},{2,3},{3,2},{4,5},{5,4},{6,7},{7,6},{8,9},{9,8},{10,11... | collective-permute-start | bytes 1966088 | tf_op jit(solution)/shard_map/ppermute | solution.py:227
  69.0 18.3 %collective-permute-start.3 = (bf16[4,128,256]{2,1,0:T(8,128)(2,1)S(1)}, bf16[4,128,256]{2,1,0:T(8,128)(2,1)S(1)}, u32[]{:S(2)}, u32[]{:S(2)}) collective-permute-start(bf16[4,128,256]{2,1,0:T(8,128)(2,1)S(1)} %shard_map.71), channel_id=1, source_target_pairs={{0,16},{16,0},{32,48},{48,32},{1,17},{17,1},{33,49},{49,33},{2,18}... | collective-permute-start | bytes 786440 | tf_op jit(solution)/shard_map/ppermute | solution.py:248
  80.2 18.6 %all-to-all-start.2 = ((bf16[8,32,1280]{2,1,0:T(8,128)(2,1)}), bf16[8,32,1280]{2,1,0:T(8,128)(2,1)S(1)}, u32[]{:S(2)}, u32[]{:S(2)}) async-start(bf16[8,32,1280]{2,1,0:T(8,128)(2,1)} %bitcast.8), calls=%async_computation.2 | async-start | bytes 1310720 | tf_op jit(solution)/shard_map/all_to_all | solution.py:251
  87.4 17.7 %collective-permute-start.5 = (bf16[4,128,256]{2,1,0:T(8,128)(2,1)S(1)}, bf16[4,128,256]{2,1,0:T(8,128)(2,1)S(1)}, u32[]{:S(2)}, u32[]{:S(2)}) collective-permute-start(bf16[4,128,256]{2,1,0:T(8,128)(2,1)S(1)} %add_convert_fusion.refs_2_), channel_id=1, source_target_pairs={{0,48},{16,32},{32,16},{48,0},{1,49},{17,33},{33,17},{49,1},{2,50}... | collective-permute-start | bytes 786440 | tf_op jit(solution)/shard_map/ppermute | solution.py:261
  90.1 20.0 %collective-permute-start.4 = (bf16[320,128]{1,0:T(8,128)(2,1)S(1)}, bf16[320,128]{1,0:T(8,128)(2,1)S(1)}, u32[]{:S(2)}, u32[]{:S(2)}) collective-permute-start(bf16[320,128]{1,0:T(8,128)(2,1)S(1)} %shard_map.72), channel_id=1, source_target_pairs={{0,32},{2,34},{4,16},{6,18},{8,0},{10,2},{12,48},{14,50},{16,4},{1... | collective-permute-start | bytes 245768 | tf_op jit(solution)/shard_map/ppermute | solution.py:259
  99.8 14.7 %all-to-all-start.3 = ((bf16[8,32,1280]{2,1,0:T(8,128)(2,1)}), bf16[8,32,1280]{2,1,0:T(8,128)(2,1)S(1)}, u32[]{:S(2)}, u32[]{:S(2)}) async-start(bf16[8,32,1280]{2,1,0:T(8,128)(2,1)} %broadcast_in_dim.5), calls=%async_computation.3 | async-start | bytes 1310720 | tf_op jit(solution)/shard_map/all_to_all | solution.py:265
  110.2 0.9 copy-start.1

commit v5 on v4

--- a/solution.py
+++ b/solution.py
@@ -106,6 +106,10 @@
                 total = term if total is None else total + term
             sums_ref[half, at] = total
     out_ref[...] = sums_ref[...].reshape(-1, sums_ref.shape[-1]).T.astype(BF16)
+
+
+def add_kernel(one_ref, two_ref, out_ref):
+    out_ref[...] = (one_ref[...].astype(F32) + two_ref[...].astype(F32)).astype(BF16)
 
 
 def sum_kernel(parts_ref, out_ref):
@@ -257,7 +261,12 @@
     )(pieces)
     projected, near = lax.optimization_barrier((projected, near))
     projected = lax.ppermute(projected, ("frame", "y"), there)
-    near = (share.astype(F32) + near.astype(F32)).astype(BF16)
+    near = pl.pallas_call(
+        add_kernel,
+        out_shape=jax.ShapeDtypeStruct(share.shape, BF16),
+        compiler_params=pltpu.CompilerParams(vmem_limit_bytes=16 * 1024 * 1024),
+        cost_estimate=pl.CostEstimate(flops=0, bytes_accessed=2**20, transcendentals=0),
+    )(share, near)
     far = lax.ppermute(near, "frame", [(i, n_frame - 1 - i) for i in range(n_frame)])
 
     weight_sum = jnp.sum(weight_part.astype(F32), axis=0).astype(BF16)

time: 116 us -> 116 us (level)
  no operation moved by 1% of the time
where the time goes in v5:
time: 116 us; the launch traced here: 115 us
  starting transfers between devices  49.7 us (43%)
  blocking collectives  23.5 us (20%)
  waiting for transfers between devices  21.6 us (19%)
  Pallas kernels  14.3 us (12%)
  local copies, waits for them, and re-layouts  4.79 us (4%)
    all_gather x1, blocking collectives, local(): lax.all_gather(projections.reshape(projections.shape[1:]).transpose(0, 2,...  23.5 us
    pallas_call x5, Pallas kernels, whole(): pl.pallas_call(kernel, out_shape=out_shape, in_specs=[pl.BlockSpec(memory...  11.4 us
    all_to_all x1, starting transfers between devices, local(): grad_own = lax.all_to_all(copies(grad_moved, n_y), 'y', 0, 0, tiled=True)  8.85 us
    all_to_all x1, waiting for transfers between devices, local(): grad_own = lax.all_to_all(copies(grad_moved, n_y), 'y', 0, 0, tiled=True)  7.32 us
    ppermute x1, starting transfers between devices, local(): projected = lax.ppermute(projected, ('frame', 'y'), there)  7.2 us
    all_to_all x1, starting transfers between devices, local(): weight_part = lax.all_to_all(weight_part, CLIP, 0, 0, tiled=True)  7 us
    ppermute x1, starting transfers between devices, local(): lax.ppermute(out_grad.reshape(tokens, width).T, ('frame', 'y'), back)  6.83 us
    all_to_all x1, waiting for transfers between devices, local(): pieces = lax.all_to_all(pieces, 'y', 0, 0, tiled=True)  5.8 us
  transfers between devices with their start and end apart: 10, of which 6 were waited for; matrix products, arithmetic and copies ran while one was open for 2% of the time, Pallas kernels for 12%

profile of v5, /device:TPU:8, one launch (start us, length us, event | category | flops | bytes accessed | tf_op | source)
XLA Modules:
  0.0 115.4 jit_solution(5592767191358931118)
XLA Ops:
  0.6 1.0 copy.13
  1.6 6.8 %collective-permute-start = (bf16[320,128]{1,0:T(8,128)(2,1)S(1)}, bf16[320,128]{1,0:T(8,128)(2,1)S(1)}, u32[]{:S(2)}, u32[]{:S(2)}) collective-permute-start(bf16[320,128]{1,0:T(8,128)(2,1)S(1)} %bitcast.25), channel_id=1, source_target_pairs={{32,0},{34,2},{16,4},{18,6},{0,8},{2,10},{48,12},{50,14},{4,16},{6... | collective-permute-start | bytes 245768 | tf_op jit(solution)/shard_map/ppermute | solution.py:205
  8.5 23.5 %all_gather.3.all_ref.refs_1_ = bf16[16,3,32,256]{3,2,1,0:T(8,128)(2,1)S(1)} all-gather(bf16[4,3,32,256]{3,2,1,0:T(8,128)(2,1)} %bitcast.23), channel_id=1, replica_groups=mesh['x'=4,'zl'=2,'frame'=4,'y'=8,'core'=2] {'frame'}, dimensions={0}, use_global_device_ids=true | all-gather | bytes 983040 | tf_op jit(solution)/shard_map/all_gather | solution.py:206
  32.0 0.0 collective-permute-done
  32.0 0.9 broadcast_in_dim.4
  32.9 0.0 copy-start
  33.0 8.9 %all-to-all-start = ((bf16[8,320,128]{2,1,0:T(8,128)(2,1)}), bf16[8,320,128]{2,1,0:T(8,128)(2,1)S(1)}, u32[]{:S(2)}, u32[]{:S(2)}) async-start(bf16[8,320,128]{2,1,0:T(8,128)(2,1)} %broadcast_in_dim.4), calls=%async_computation | async-start | bytes 1310720 | tf_op jit(solution)/shard_map/all_to_all | solution.py:210
  41.8 0.0 copy-done
  41.8 0.2 copy.14
  42.0 0.1 pad_add_fusion.place_ref.refs_0_
  42.1 2.7 %shard_map.67.rows_ref = bf16[4,128,256]{2,1,0:T(8,128)(2,1)S(1)} custom-call(bf16[16,3,32,256]{3,2,1,0:T(8,128)(2,1)S(1)} %all_gather.3.all_ref.refs_1_), custom_call_target="tpu_custom_call" | custom-call | flops 167772160 | bytes 4194304 | tf_op jit(solution)/shard_map/pallas_call | solution.py:212
  44.8 0.9 shard_map.68
  45.7 1.9 %collective-permute-start.1 = (bf16[8,320,128]{2,1,0:T(8,128)(2,1)S(1)}, bf16[8,320,128]{2,1,0:T(8,128)(2,1)S(1)}, u32[]{:S(2)}, u32[]{:S(2)}) collective-permute-start(bf16[8,320,128]{2,1,0:T(8,128)(2,1)S(1)} %shard_map.68), channel_id=1, source_target_pairs={{0,1},{1,0},{2,3},{3,2},{4,5},{5,4},{6,7},{7,6},{8,9},{9,8},{10,11... | collective-permute-start | bytes 1966088 | tf_op jit(solution)/shard_map/ppermute | solution.py:225
  47.7 2.1 %collective-permute-done.1.got_ref = bf16[8,320,128]{2,1,0:T(8,128)(2,1)S(1)} collective-permute-done((bf16[8,320,128]{2,1,0:T(8,128)(2,1)S(1)}, bf16[8,320,128]{2,1,0:T(8,128)(2,1)S(1)}, u32[]{:S(2)}, u32[]{:S(2)}) %collective-permute-start.1) | collective-permute-done | bytes 655392 | tf_op jit(solution)/shard_map/ppermute | solution.py:225
  49.7 1.7 %shard_map.69 = bf16[8,320,128]{2,1,0:T(8,128)(2,1)} custom-call(s32[2]{0:T(128)S(1)} %pad_add_fusion.place_ref.refs_0_, bf16[2,2,320,256]{3,2,1,0:T(8,128)(2,1)S(1)} %bitcast.18, bf16[4,128,256]{2,1,0:T(8,128)(2,1)S(1)} %shard_map.67.rows_ref, bf16[8,320,128]{2,1,0:T(8,128)(2,1)S(1)} %collective-permute-done.1.got_ref), custom_call_target="tpu_custom_call" | custom-call | flops 167772160 | bytes 3145728 | tf_op jit(solution)/shard_map/pallas_call | solution.py:160
  51.5 7.3 %all-to-all-done.own_ref = bf16[8,320,128]{2,1,0:T(8,128)(2,1)S(1)} async-done(((bf16[8,320,128]{2,1,0:T(8,128)(2,1)}), bf16[8,320,128]{2,1,0:T(8,128)(2,1)S(1)}, u32[]{:S(2)}, u32[]{:S(2)}) %all-to-all-start) | async-done | bytes 655392 | tf_op jit(solution)/shard_map/all_to_all | solution.py:210
  58.8 5.0 %all-to-all-start.1 = ((bf16[8,320,128]{2,1,0:T(8,128)(2,1)}), bf16[8,320,128]{2,1,0:T(8,128)(2,1)S(1)}, u32[]{:S(2)}, u32[]{:S(2)}) async-start(bf16[8,320,128]{2,1,0:T(8,128)(2,1)} %shard_map.69), calls=%async_computation.1 | async-start | bytes 1310720 | tf_op jit(solution)/shard_map/all_to_all | solution.py:230
  63.7 1.9 %collective-permute-start.2 = (bf16[8,320,128]{2,1,0:T(8,128)(2,1)S(1)}, bf16[8,320,128]{2,1,0:T(8,128)(2,1)S(1)}, u32[]{:S(2)}, u32[]{:S(2)}) collective-permute-start(bf16[8,320,128]{2,1,0:T(8,128)(2,1)S(1)} %all-to-all-done.own_ref), channel_id=1, source_target_pairs={{0,1},{1,0},{2,3},{3,2},{4,5},{5,4},{6,7},{7,6},{8,9},{9,8},{10,11... | collective-permute-start | bytes 1966088 | tf_op jit(solution)/shard_map/ppermute | solution.py:231
  65.6 2.1 %collective-permute-done.2.other_ref = bf16[8,320,128]{2,1,0:T(8,128)(2,1)S(1)} collective-permute-done((bf16[8,320,128]{2,1,0:T(8,128)(2,1)S(1)}, bf16[8,320,128]{2,1,0:T(8,128)(2,1)S(1)}, u32[]{:S(2)}, u32[]{:S(2)}) %collective-permute-start.2) | collective-permute-done | bytes 655392 | tf_op jit(solution)/shard_map/ppermute | solution.py:231
  67.7 1.3 %shard_map.71.one_ref = bf16[4,128,256]{2,1,0:T(8,128)(2,1)S(1)} custom-call(s32[2]{0:T(128)S(1)} %pad_add_fusion.place_ref.refs_0_, bf16[2,2,320,256]{3,2,1,0:T(8,128)(2,1)S(1)} %bitcast.19, bf16[8,320,128]{2,1,0:T(8,128)(2,1)S(1)} %all-to-all-done.own_ref, bf16[8,320,128]{2,1,0:T(8,128)(2,1)S(1)} %collective-permute-done.2.other_ref), custom_call_target="tpu_custom_call" | custom-call | flops 335544320 | bytes 3932160 | tf_op jit(solution)/shard_map/pallas_call | solution.py:160
  69.0 2.9 %collective-permute-start.3 = (bf16[4,128,256]{2,1,0:T(8,128)(2,1)S(1)}, bf16[4,128,256]{2,1,0:T(8,128)(2,1)S(1)}, u32[]{:S(2)}, u32[]{:S(2)}) collective-permute-start(bf16[4,128,256]{2,1,0:T(8,128)(2,1)S(1)} %shard_map.71.one_ref), channel_id=1, source_target_pairs={{0,16},{16,0},{32,48},{48,32},{1,17},{17,1},{33,49},{49,33},{2,18}... | collective-permute-start | bytes 786440 | tf_op jit(solution)/shard_map/ppermute | solution.py:252
  72.0 2.5 %shard_map.70 = bf16[256,1280]{1,0:T(8,128)(2,1)} custom-call(s32[2]{0:T(128)S(1)} %pad_add_fusion.place_ref.refs_0_, bf16[4,128,256]{2,1,0:T(8,128)(2,1)S(1)} %shard_map.67.rows_ref, bf16[8,320,128]{2,1,0:T(8,128)(2,1)S(1)} %all-to-all-done.own_ref, bf16[8,320,128]{2,1,0:T(8,128)(2,1)S(1)} %collective-permute-done.2.other_ref), custom_call_target="tpu_custom_call" | custom-call | flops 335544320 | bytes 3145728 | tf_op jit(solution)/shard_map/pallas_call | solution.py:160
  74.4 5.8 %all-to-all-done.1.parts_ref = bf16[8,320,128]{2,1,0:T(8,128)(2,1)S(1)} async-done(((bf16[8,320,128]{2,1,0:T(8,128)(2,1)}), bf16[8,320,128]{2,1,0:T(8,128)(2,1)S(1)}, u32[]{:S(2)}, u32[]{:S(2)}) %all-to-all-start.1) | async-done | bytes 655392 | tf_op jit(solution)/shard_map/all_to_all | solution.py:230
  80.2 7.0 %all-to-all-start.2 = ((bf16[8,32,1280]{2,1,0:T(8,128)(2,1)}), bf16[8,32,1280]{2,1,0:T(8,128)(2,1)S(1)}, u32[]{:S(2)}, u32[]{:S(2)}) async-start(bf16[8,32,1280]{2,1,0:T(8,128)(2,1)} %bitcast.8), calls=%async_computation.2 | async-start | bytes 1310720 | tf_op jit(solution)/shard_map/all_to_all | solution.py:255
  87.2 0.1 shard_map.72
  87.3 0.0 collective-permute-done.3.two_ref
  87.3 0.1 shard_map.73.refs_2_
  87.4 2.7 %collective-permute-start.5 = (bf16[4,128,256]{2,1,0:T(8,128)(2,1)S(1)}, bf16[4,128,256]{2,1,0:T(8,128)(2,1)S(1)}, u32[]{:S(2)}, u32[]{:S(2)}) collective-permute-start(bf16[4,128,256]{2,1,0:T(8,128)(2,1)S(1)} %shard_map.73.refs_2_), channel_id=1, source_target_pairs={{0,48},{16,32},{32,16},{48,0},{1,49},{17,33},{33,17},{49,1},{2,50}... | collective-permute-start | bytes 786440 | tf_op jit(solution)/shard_map/ppermute | solution.py:270
  90.1 7.2 %collective-permute-start.4 = (bf16[320,128]{1,0:T(8,128)(2,1)S(1)}, bf16[320,128]{1,0:T(8,128)(2,1)S(1)}, u32[]{:S(2)}, u32[]{:S(2)}) collective-permute-start(bf16[320,128]{1,0:T(8,128)(2,1)S(1)} %shard_map.72), channel_id=1, source_target_pairs={{0,32},{2,34},{4,16},{6,18},{8,0},{10,2},{12,48},{14,50},{16,4},{1... | collective-permute-start | bytes 245768 | tf_op jit(solution)/shard_map/ppermute | solution.py:263
  97.4 1.5 %all-to-all-done.2 = bf16[8,32,1280]{2,1,0:T(8,128)(2,1)S(1)} async-done(((bf16[8,32,1280]{2,1,0:T(8,128)(2,1)}), bf16[8,32,1280]{2,1,0:T(8,128)(2,1)S(1)}, u32[]{:S(2)}, u32[]{:S(2)}) %all-to-all-start.2) | async-done | bytes 655392 | tf_op jit(solution)/shard_map/all_to_all | solution.py:255
  98.8 0.1 reduce_sum.12
  98.9 0.9 broadcast_in_dim.5
  99.8 5.3 %all-to-all-start.3 = ((bf16[8,32,1280]{2,1,0:T(8,128)(2,1)}), bf16[8,32,1280]{2,1,0:T(8,128)(2,1)S(1)}, u32[]{:S(2)}, u32[]{:S(2)}) async-start(bf16[8,32,1280]{2,1,0:T(8,128)(2,1)} %broadcast_in_dim.5), calls=%async_computation.3 | async-start | bytes 1310720 | tf_op jit(solution)/shard_map/all_to_all | solution.py:274
  105.2 0.0 collective-permute-done.5.refs_3_
  105.2 5.0 %shard_map.74 = bf16[4,3,32,256]{3,2,1,0:T(8,128)(2,1)} custom-call(s32[2]{0:T(128)S(1)} %pad_add_fusion.place_ref.refs_0_, bf16[16,3,32,256]{3,2,1,0:T(8,128)(2,1)S(1)} %all_gather.3.all_ref.refs_1_, bf16[4,128,256]{2,1,0:T(8,128)(2,1)S(1)} %shard_map.73.refs_2_, bf16[4,128,256]{2,1,0:T(8,128)(2,1)S(1)} %collective-permute-done.5.refs_3_), custom_call_target="tpu_custom_call" | custom-call | flops 67108864000 | bytes 2621440 | tf_op jit(solution)/shard_map/pallas_call | solution.py:160
  110.2 0.0 collective-permute-done.4
  110.2 0.0 copy-start.1
  110.2 0.1 copy.15
  110.3 0.8 copy-done.1
  111.1 0.7 add_convert_fusion
  111.7 2.8 %all-to-all-done.3 = bf16[8,32,1280]{2,1,0:T(8,128)(2,1)S(1)} async-done(((bf16[8,32,1280]{2,1,0:T(8,128)(2,1)}), bf16[8,32,1280]{2,1,0:T(8,128)(2,1)S(1)}, u32[]{:S(2)}, u32[]{:S(2)}) %all-to-all-start.3) | async-done | bytes 655392 | tf_op jit(solution)/shard_map/all_to_all | solution.py:274
  114.6 0.8 copy.17
  (1 shorter events, 0.0 us)
Async XLA Ops:
  1.6 30.4 %collective-permute-start = (bf16[320,128]{1,0:T(8,128)(2,1)S(1)}, bf16[320,128]{1,0:T(8,128)(2,1)S(1)}, u32[]{:S(2)}, u32[]{:S(2)}) collective-permute-start(bf16[320,128]{1,0:T(8,128)(2,1)S(1)} %bitcast.25), channel_id=1, source_target_pairs={{32,0},{34,2},{16,4},{18,6},{0,8},{2,10},{48,12},{50,14},{4,16},{6... | collective-permute-start | bytes 245768 | tf_op jit(solution)/shard_map/ppermute | solution.py:205
  32.9 8.9 %copy-start = (bf16[256,1280]{1,0:T(8,128)(2,1)S(1)}, bf16[256,1280]{1,0:T(8,128)(2,1)}, u32[]{:S(2)}) copy-start(bf16[256,1280]{1,0:T(8,128)(2,1)} %param.6) | copy-start | bytes 1966084
  33.0 25.8 %all-to-all-start = ((bf16[8,320,128]{2,1,0:T(8,128)(2,1)}), bf16[8,320,128]{2,1,0:T(8,128)(2,1)S(1)}, u32[]{:S(2)}, u32[]{:S(2)}) async-start(bf16[8,320,128]{2,1,0:T(8,128)(2,1)} %broadcast_in_dim.4), calls=%async_computation | async-start | bytes 1310720 | tf_op jit(solution)/shard_map/all_to_all | solution.py:210
  45.7 4.0 %collective-permute-start.1 = (bf16[8,320,128]{2,1,0:T(8,128)(2,1)S(1)}, bf16[8,320,128]{2,1,0:T(8,128)(2,1)S(1)}, u32[]{:S(2)}, u32[]{:S(2)}) collective-permute-start(bf16[8,320,128]{2,1,0:T(8,128)(2,1)S(1)} %shard_map.68), channel_id=1, source_target_pairs={{0,1},{1,0},{2,3},{3,2},{4,5},{5,4},{6,7},{7,6},{8,9},{9,8},{10,11... | collective-permute-start | bytes 1966088 | tf_op jit(solution)/shard_map/ppermute | solution.py:225
  58.8 21.5 %all-to-all-start.1 = ((bf16[8,320,128]{2,1,0:T(8,128)(2,1)}), bf16[8,320,128]{2,1,0:T(8,128)(2,1)S(1)}, u32[]{:S(2)}, u32[]{:S(2)}) async-start(bf16[8,320,128]{2,1,0:T(8,128)(2,1)} %shard_map.69), calls=%async_computation.1 | async-start | bytes 1310720 | tf_op jit(solution)/shard_map/all_to_all | solution.py:230
  63.7 4.0 %collective-permute-start.2 = (bf16[8,320,128]{2,1,0:T(8,128)(2,1)S(1)}, bf16[8,320,128]{2,1,0:T(8,128)(2,1)S(1)}, u32[]{:S(2)}, u32[]{:S(2)}) collective-permute-start(bf16[8,320,128]{2,1,0:T(8,128)(2,1)S(1)} %all-to-all-done.own_ref), channel_id=1, source_target_pairs={{0,1},{1,0},{2,3},{3,2},{4,5},{5,4},{6,7},{7,6},{8,9},{9,8},{10,11... | collective-permute-start | bytes 1966088 | tf_op jit(solution)/shard_map/ppermute | solution.py:231
  69.0 18.3 %collective-permute-start.3 = (bf16[4,128,256]{2,1,0:T(8,128)(2,1)S(1)}, bf16[4,128,256]{2,1,0:T(8,128)(2,1)S(1)}, u32[]{:S(2)}, u32[]{:S(2)}) collective-permute-start(bf16[4,128,256]{2,1,0:T(8,128)(2,1)S(1)} %shard_map.71.one_ref), channel_id=1, source_target_pairs={{0,16},{16,0},{32,48},{48,32},{1,17},{17,1},{33,49},{49,33},{2,18}... | collective-permute-start | bytes 786440 | tf_op jit(solution)/shard_map/ppermute | solution.py:252
  80.2 18.6 %all-to-all-start.2 = ((bf16[8,32,1280]{2,1,0:T(8,128)(2,1)}), bf16[8,32,1280]{2,1,0:T(8,128)(2,1)S(1)}, u32[]{:S(2)}, u32[]{:S(2)}) async-start(bf16[8,32,1280]{2,1,0:T(8,128)(2,1)} %bitcast.8), calls=%async_computation.2 | async-start | bytes 1310720 | tf_op jit(solution)/shard_map/all_to_all | solution.py:255
  87.4 17.7 %collective-permute-start.5 = (bf16[4,128,256]{2,1,0:T(8,128)(2,1)S(1)}, bf16[4,128,256]{2,1,0:T(8,128)(2,1)S(1)}, u32[]{:S(2)}, u32[]{:S(2)}) collective-permute-start(bf16[4,128,256]{2,1,0:T(8,128)(2,1)S(1)} %shard_map.73.refs_2_), channel_id=1, source_target_pairs={{0,48},{16,32},{32,16},{48,0},{1,49},{17,33},{33,17},{49,1},{2,50}... | collective-permute-start | bytes 786440 | tf_op jit(solution)/shard_map/ppermute | solution.py:270
  90.1 20.0 %collective-permute-start.4 = (bf16[320,128]{1,0:T(8,128)(2,1)S(1)}, bf16[320,128]{1,0:T(8,128)(2,1)S(1)}, u32[]{:S(2)}, u32[]{:S(2)}) collective-permute-start(bf16[320,128]{1,0:T(8,128)(2,1)S(1)} %shard_map.72), channel_id=1, source_target_pairs={{0,32},{2,34},{4,16},{6,18},{8,0},{10,2},{12,48},{14,50},{16,4},{1... | collective-permute-start | bytes 245768 | tf_op jit(solution)/shard_map/ppermute | solution.py:263
  99.8 14.7 %all-to-all-start.3 = ((bf16[8,32,1280]{2,1,0:T(8,128)(2,1)}), bf16[8,32,1280]{2,1,0:T(8,128)(2,1)S(1)}, u32[]{:S(2)}, u32[]{:S(2)}) async-start(bf16[8,32,1280]{2,1,0:T(8,128)(2,1)} %broadcast_in_dim.5), calls=%async_computation.3 | async-start | bytes 1310720 | tf_op jit(solution)/shard_map/all_to_all | solution.py:274
  110.2 0.9 copy-start.1

commit v6 on v5

--- a/solution.py
+++ b/solution.py
@@ -48,6 +48,10 @@
 
 def slot(place_ref, frame, n):
     return lax.rem(2 * place_ref[0] + n // 2 + n - frame, n)
+
+
+def turn_kernel(array_ref, out_ref):
+    out_ref[...] = array_ref[...].T
 
 
 def project_block(weight, rows):
@@ -202,7 +206,12 @@
     ]
     back = [(b, a) for a, b in there]
 
-    grad_moved = lax.ppermute(out_grad.reshape(tokens, width).T, ("frame", "y"), back)
+    grad_t = pl.pallas_call(
+        turn_kernel,
+        out_shape=jax.ShapeDtypeStruct((width, tokens), BF16),
+        cost_estimate=pl.CostEstimate(flops=0, bytes_accessed=2**17, transcendentals=0),
+    )(out_grad.reshape(tokens, width))
+    grad_moved = lax.ppermute(grad_t, ("frame", "y"), back)
     qkv_all = lax.all_gather(
         projections.reshape(projections.shape[1:]).transpose(0, 2, 1, 3), "frame", tiled=True
     )

time: 116 us -> 120 us (1.034)
  starting transfers between devices: 49.7 us -> 52.4 us
  Pallas kernels: 14.3 us -> 15.9 us
  waiting for transfers between devices: 21.6 us -> 23.1 us
    all_to_all x1, waiting for transfers between devices: 1.49 us -> 4.37 us  [local(): weight_part = lax.all_to_all(weight_part, CLIP, 0, 0, tiled=True)]
    all_to_all x1, starting transfers between devices: 7 us -> 8.82 us  [local(): weight_part = lax.all_to_all(weight_part, CLIP, 0, 0, tiled=True)]
    pallas_call x0 -> x1, Pallas kernels: none -> 1.61 us  [local(): pl.pallas_call(turn_kernel, out_shape=jax.ShapeDtypeStruct((width, tokens...]
    all_to_all x1, waiting for transfers between devices: 5.8 us -> 4.52 us  [local(): pieces = lax.all_to_all(pieces, 'y', 0, 0, tiled=True)]
    ppermute x1, starting transfers between devices: 2.92 us -> 4.17 us  [local(): near = lax.ppermute(share, 'frame', [(i, i ^ 1) for i in range(n_frame)])]
where the time goes in v6:
time: 120 us
  starting transfers between devices  52.4 us (44%)
  waiting for transfers between devices  23.1 us (19%)
  blocking collectives  23 us (19%)
  Pallas kernels  15.9 us (13%)
  local copies, waits for them, and re-layouts  3.78 us (3%)
    all_gather x1, blocking collectives, local(): lax.all_gather(projections.reshape(projections.shape[1:]).transpose(0, 2,...  23 us
    pallas_call x5, Pallas kernels, whole(): pl.pallas_call(kernel, out_shape=out_shape, in_specs=[pl.BlockSpec(memory...  11.4 us
    all_to_all x1, starting transfers between devices, local(): grad_own = lax.all_to_all(copies(grad_moved, n_y), 'y', 0, 0, tiled=True)  9.09 us
    all_to_all x1, starting transfers between devices, local(): weight_part = lax.all_to_all(weight_part, CLIP, 0, 0, tiled=True)  8.82 us
    all_to_all x1, waiting for transfers between devices, local(): grad_own = lax.all_to_all(copies(grad_moved, n_y), 'y', 0, 0, tiled=True)  7.25 us
    ppermute x1, starting transfers between devices, local(): grad_moved = lax.ppermute(grad_t, ('frame', 'y'), back)  6.82 us
    ppermute x1, starting transfers between devices, local(): projected = lax.ppermute(projected, ('frame', 'y'), there)  6.44 us
    all_to_all x1, starting transfers between devices, local(): lax.all_to_all(copies(weight_sum, n_clip), CLIP, 0, 0, tiled=True)  5.2 us
  transfers between devices with their start and end apart: 10, of which 6 were waited for; matrix products, arithmetic and copies ran while one was open for 2% of the time, Pallas kernels for 12%

profile of v6, /device:TPU:8, one launch (start us, length us, event | category | flops | bytes accessed | tf_op | source)
XLA Modules:
  0.0 119.7 jit_solution(14988539226932259840)
XLA Ops:
  0.6 1.6 %shard_map.67 = bf16[320,128]{1,0:T(8,128)(2,1)} custom-call(bf16[128,320]{1,0:T(8,128)(2,1)} %bitcast.23), custom_call_target="tpu_custom_call" | custom-call | bytes 131072 | tf_op jit(solution)/shard_map/pallas_call | solution.py:209
  2.2 6.8 %collective-permute-start = (bf16[320,128]{1,0:T(8,128)(2,1)}, bf16[320,128]{1,0:T(8,128)(2,1)S(1)}, u32[]{:S(2)}, u32[]{:S(2)}) collective-permute-start(bf16[320,128]{1,0:T(8,128)(2,1)} %shard_map.67), channel_id=1, source_target_pairs={{32,0},{34,2},{16,4},{18,6},{0,8},{2,10},{48,12},{50,14},{4,16},{6... | collective-permute-start | bytes 245768 | tf_op jit(solution)/shard_map/ppermute | solution.py:214
  9.1 23.0 %all_gather.3.all_ref.refs_1_ = bf16[16,3,32,256]{3,2,1,0:T(8,128)(2,1)S(1)} all-gather(bf16[4,3,32,256]{3,2,1,0:T(8,128)(2,1)} %bitcast.22), channel_id=1, replica_groups=mesh['x'=4,'zl'=2,'frame'=4,'y'=8,'core'=2] {'frame'}, dimensions={0}, use_global_device_ids=true | all-gather | bytes 983040 | tf_op jit(solution)/shard_map/all_gather | solution.py:215
  32.1 0.0 collective-permute-done
  32.1 0.9 broadcast_in_dim.4
  33.0 0.0 copy-start
  33.0 9.1 %all-to-all-start = ((bf16[8,320,128]{2,1,0:T(8,128)(2,1)}), bf16[8,320,128]{2,1,0:T(8,128)(2,1)S(1)}, u32[]{:S(2)}, u32[]{:S(2)}) async-start(bf16[8,320,128]{2,1,0:T(8,128)(2,1)} %broadcast_in_dim.4), calls=%async_computation | async-start | bytes 1310720 | tf_op jit(solution)/shard_map/all_to_all | solution.py:219
  42.1 0.0 copy-done
  42.1 0.2 copy.11
  42.4 0.1 pad_add_fusion.place_ref.refs_0_
  42.4 2.7 %shard_map.68.rows_ref = bf16[4,128,256]{2,1,0:T(8,128)(2,1)S(1)} custom-call(bf16[16,3,32,256]{3,2,1,0:T(8,128)(2,1)S(1)} %all_gather.3.all_ref.refs_1_), custom_call_target="tpu_custom_call" | custom-call | flops 167772160 | bytes 4194304 | tf_op jit(solution)/shard_map/pallas_call | solution.py:221
  45.1 0.9 shard_map.69
  46.0 1.9 %collective-permute-start.1 = (bf16[8,320,128]{2,1,0:T(8,128)(2,1)S(1)}, bf16[8,320,128]{2,1,0:T(8,128)(2,1)S(1)}, u32[]{:S(2)}, u32[]{:S(2)}) collective-permute-start(bf16[8,320,128]{2,1,0:T(8,128)(2,1)S(1)} %shard_map.69), channel_id=1, source_target_pairs={{0,1},{1,0},{2,3},{3,2},{4,5},{5,4},{6,7},{7,6},{8,9},{9,8},{10,11... | collective-permute-start | bytes 1966088 | tf_op jit(solution)/shard_map/ppermute | solution.py:234
  48.0 2.1 %collective-permute-done.1.got_ref = bf16[8,320,128]{2,1,0:T(8,128)(2,1)S(1)} collective-permute-done((bf16[8,320,128]{2,1,0:T(8,128)(2,1)S(1)}, bf16[8,320,128]{2,1,0:T(8,128)(2,1)S(1)}, u32[]{:S(2)}, u32[]{:S(2)}) %collective-permute-start.1) | collective-permute-done | bytes 655392 | tf_op jit(solution)/shard_map/ppermute | solution.py:234
  50.0 1.7 %shard_map.70 = bf16[8,320,128]{2,1,0:T(8,128)(2,1)} custom-call(s32[2]{0:T(128)S(1)} %pad_add_fusion.place_ref.refs_0_, bf16[2,2,320,256]{3,2,1,0:T(8,128)(2,1)S(1)} %bitcast.17, bf16[4,128,256]{2,1,0:T(8,128)(2,1)S(1)} %shard_map.68.rows_ref, bf16[8,320,128]{2,1,0:T(8,128)(2,1)S(1)} %collective-permute-done.1.got_ref), custom_call_target="tpu_custom_call" | custom-call | flops 167772160 | bytes 3145728 | tf_op jit(solution)/shard_map/pallas_call | solution.py:164
  51.8 7.2 %all-to-all-done.own_ref = bf16[8,320,128]{2,1,0:T(8,128)(2,1)S(1)} async-done(((bf16[8,320,128]{2,1,0:T(8,128)(2,1)}), bf16[8,320,128]{2,1,0:T(8,128)(2,1)S(1)}, u32[]{:S(2)}, u32[]{:S(2)}) %all-to-all-start) | async-done | bytes 655392 | tf_op jit(solution)/shard_map/all_to_all | solution.py:219
  59.0 5.0 %all-to-all-start.1 = ((bf16[8,320,128]{2,1,0:T(8,128)(2,1)}), bf16[8,320,128]{2,1,0:T(8,128)(2,1)S(1)}, u32[]{:S(2)}, u32[]{:S(2)}) async-start(bf16[8,320,128]{2,1,0:T(8,128)(2,1)} %shard_map.70), calls=%async_computation.1 | async-start | bytes 1310720 | tf_op jit(solution)/shard_map/all_to_all | solution.py:239
  64.0 1.9 %collective-permute-start.2 = (bf16[8,320,128]{2,1,0:T(8,128)(2,1)S(1)}, bf16[8,320,128]{2,1,0:T(8,128)(2,1)S(1)}, u32[]{:S(2)}, u32[]{:S(2)}) collective-permute-start(bf16[8,320,128]{2,1,0:T(8,128)(2,1)S(1)} %all-to-all-done.own_ref), channel_id=1, source_target_pairs={{0,1},{1,0},{2,3},{3,2},{4,5},{5,4},{6,7},{7,6},{8,9},{9,8},{10,11... | collective-permute-start | bytes 1966088 | tf_op jit(solution)/shard_map/ppermute | solution.py:240
  65.9 2.1 %collective-permute-done.2.other_ref = bf16[8,320,128]{2,1,0:T(8,128)(2,1)S(1)} collective-permute-done((bf16[8,320,128]{2,1,0:T(8,128)(2,1)S(1)}, bf16[8,320,128]{2,1,0:T(8,128)(2,1)S(1)}, u32[]{:S(2)}, u32[]{:S(2)}) %collective-permute-start.2) | collective-permute-done | bytes 655392 | tf_op jit(solution)/shard_map/ppermute | solution.py:240
  68.0 1.3 %shard_map.72.one_ref = bf16[4,128,256]{2,1,0:T(8,128)(2,1)S(1)} custom-call(s32[2]{0:T(128)S(1)} %pad_add_fusion.place_ref.refs_0_, bf16[2,2,320,256]{3,2,1,0:T(8,128)(2,1)S(1)} %bitcast.18, bf16[8,320,128]{2,1,0:T(8,128)(2,1)S(1)} %all-to-all-done.own_ref, bf16[8,320,128]{2,1,0:T(8,128)(2,1)S(1)} %collective-permute-done.2.other_ref), custom_call_target="tpu_custom_call" | custom-call | flops 335544320 | bytes 3932160 | tf_op jit(solution)/shard_map/pallas_call | solution.py:164
  69.3 4.2 %collective-permute-start.3 = (bf16[4,128,256]{2,1,0:T(8,128)(2,1)S(1)}, bf16[4,128,256]{2,1,0:T(8,128)(2,1)S(1)}, u32[]{:S(2)}, u32[]{:S(2)}) collective-permute-start(bf16[4,128,256]{2,1,0:T(8,128)(2,1)S(1)} %shard_map.72.one_ref), channel_id=1, source_target_pairs={{0,16},{16,0},{32,48},{48,32},{1,17},{17,1},{33,49},{49,33},{2,18}... | collective-permute-start | bytes 786440 | tf_op jit(solution)/shard_map/ppermute | solution.py:261
  73.5 2.5 %shard_map.71 = bf16[256,1280]{1,0:T(8,128)(2,1)} custom-call(s32[2]{0:T(128)S(1)} %pad_add_fusion.place_ref.refs_0_, bf16[4,128,256]{2,1,0:T(8,128)(2,1)S(1)} %shard_map.68.rows_ref, bf16[8,320,128]{2,1,0:T(8,128)(2,1)S(1)} %all-to-all-done.own_ref, bf16[8,320,128]{2,1,0:T(8,128)(2,1)S(1)} %collective-permute-done.2.other_ref), custom_call_target="tpu_custom_call" | custom-call | flops 335544320 | bytes 3145728 | tf_op jit(solution)/shard_map/pallas_call | solution.py:164
  75.9 4.5 %all-to-all-done.1.parts_ref = bf16[8,320,128]{2,1,0:T(8,128)(2,1)S(1)} async-done(((bf16[8,320,128]{2,1,0:T(8,128)(2,1)}), bf16[8,320,128]{2,1,0:T(8,128)(2,1)S(1)}, u32[]{:S(2)}, u32[]{:S(2)}) %all-to-all-start.1) | async-done | bytes 655392 | tf_op jit(solution)/shard_map/all_to_all | solution.py:239
  80.5 8.8 %all-to-all-start.2 = ((bf16[8,32,1280]{2,1,0:T(8,128)(2,1)}), bf16[8,32,1280]{2,1,0:T(8,128)(2,1)S(1)}, u32[]{:S(2)}, u32[]{:S(2)}) async-start(bf16[8,32,1280]{2,1,0:T(8,128)(2,1)} %bitcast.7), calls=%async_computation.2 | async-start | bytes 1310720 | tf_op jit(solution)/shard_map/all_to_all | solution.py:264
  89.3 0.1 shard_map.73
  89.4 0.0 collective-permute-done.3.two_ref
  89.4 0.1 shard_map.74.refs_2_
  89.4 3.1 %collective-permute-start.5 = (bf16[4,128,256]{2,1,0:T(8,128)(2,1)S(1)}, bf16[4,128,256]{2,1,0:T(8,128)(2,1)S(1)}, u32[]{:S(2)}, u32[]{:S(2)}) collective-permute-start(bf16[4,128,256]{2,1,0:T(8,128)(2,1)S(1)} %shard_map.74.refs_2_), channel_id=1, source_target_pairs={{0,48},{16,32},{32,16},{48,0},{1,49},{17,33},{33,17},{49,1},{2,50}... | collective-permute-start | bytes 786440 | tf_op jit(solution)/shard_map/ppermute | solution.py:279
  92.5 6.4 %collective-permute-start.4 = (bf16[320,128]{1,0:T(8,128)(2,1)S(1)}, bf16[320,128]{1,0:T(8,128)(2,1)S(1)}, u32[]{:S(2)}, u32[]{:S(2)}) collective-permute-start(bf16[320,128]{1,0:T(8,128)(2,1)S(1)} %shard_map.73), channel_id=1, source_target_pairs={{0,32},{2,34},{4,16},{6,18},{8,0},{10,2},{12,48},{14,50},{16,4},{1... | collective-permute-start | bytes 245768 | tf_op jit(solution)/shard_map/ppermute | solution.py:272
  99.0 4.4 %all-to-all-done.2 = bf16[8,32,1280]{2,1,0:T(8,128)(2,1)S(1)} async-done(((bf16[8,32,1280]{2,1,0:T(8,128)(2,1)}), bf16[8,32,1280]{2,1,0:T(8,128)(2,1)S(1)}, u32[]{:S(2)}, u32[]{:S(2)}) %all-to-all-start.2) | async-done | bytes 655392 | tf_op jit(solution)/shard_map/all_to_all | solution.py:264
  103.3 0.1 reduce_sum.12
  103.4 0.9 broadcast_in_dim.5
  104.3 5.2 %all-to-all-start.3 = ((bf16[8,32,1280]{2,1,0:T(8,128)(2,1)}), bf16[8,32,1280]{2,1,0:T(8,128)(2,1)S(1)}, u32[]{:S(2)}, u32[]{:S(2)}) async-start(bf16[8,32,1280]{2,1,0:T(8,128)(2,1)} %broadcast_in_dim.5), calls=%async_computation.3 | async-start | bytes 1310720 | tf_op jit(solution)/shard_map/all_to_all | solution.py:283
  109.5 0.0 collective-permute-done.5.refs_3_
  109.5 5.0 %shard_map.75 = bf16[4,3,32,256]{3,2,1,0:T(8,128)(2,1)} custom-call(s32[2]{0:T(128)S(1)} %pad_add_fusion.place_ref.refs_0_, bf16[16,3,32,256]{3,2,1,0:T(8,128)(2,1)S(1)} %all_gather.3.all_ref.refs_1_, bf16[4,128,256]{2,1,0:T(8,128)(2,1)S(1)} %shard_map.74.refs_2_, bf16[4,128,256]{2,1,0:T(8,128)(2,1)S(1)} %collective-permute-done.5.refs_3_), custom_call_target="tpu_custom_call" | custom-call | flops 67108864000 | bytes 2621440 | tf_op jit(solution)/shard_map/pallas_call | solution.py:164
  114.5 0.0 collective-permute-done.4
  114.5 0.0 copy-start.1
  114.5 0.1 copy.12
  114.7 0.8 copy-done.1
  115.4 0.7 add_convert_fusion
  116.1 2.8 %all-to-all-done.3 = bf16[8,32,1280]{2,1,0:T(8,128)(2,1)S(1)} async-done(((bf16[8,32,1280]{2,1,0:T(8,128)(2,1)}), bf16[8,32,1280]{2,1,0:T(8,128)(2,1)S(1)}, u32[]{:S(2)}, u32[]{:S(2)}) %all-to-all-start.3) | async-done | bytes 655392 | tf_op jit(solution)/shard_map/all_to_all | solution.py:283
  118.9 0.8 copy.14
  (1 shorter events, 0.0 us)
Async XLA Ops:
  2.2 29.8 %collective-permute-start = (bf16[320,128]{1,0:T(8,128)(2,1)}, bf16[320,128]{1,0:T(8,128)(2,1)S(1)}, u32[]{:S(2)}, u32[]{:S(2)}) collective-permute-start(bf16[320,128]{1,0:T(8,128)(2,1)} %shard_map.67), channel_id=1, source_target_pairs={{32,0},{34,2},{16,4},{18,6},{0,8},{2,10},{48,12},{50,14},{4,16},{6... | collective-permute-start | bytes 245768 | tf_op jit(solution)/shard_map/ppermute | solution.py:214
  33.0 9.1 %copy-start = (bf16[256,1280]{1,0:T(8,128)(2,1)S(1)}, bf16[256,1280]{1,0:T(8,128)(2,1)}, u32[]{:S(2)}) copy-start(bf16[256,1280]{1,0:T(8,128)(2,1)} %param.6) | copy-start | bytes 1966084
  33.0 26.0 %all-to-all-start = ((bf16[8,320,128]{2,1,0:T(8,128)(2,1)}), bf16[8,320,128]{2,1,0:T(8,128)(2,1)S(1)}, u32[]{:S(2)}, u32[]{:S(2)}) async-start(bf16[8,320,128]{2,1,0:T(8,128)(2,1)} %broadcast_in_dim.4), calls=%async_computation | async-start | bytes 1310720 | tf_op jit(solution)/shard_map/all_to_all | solution.py:219
  46.0 4.0 %collective-permute-start.1 = (bf16[8,320,128]{2,1,0:T(8,128)(2,1)S(1)}, bf16[8,320,128]{2,1,0:T(8,128)(2,1)S(1)}, u32[]{:S(2)}, u32[]{:S(2)}) collective-permute-start(bf16[8,320,128]{2,1,0:T(8,128)(2,1)S(1)} %shard_map.69), channel_id=1, source_target_pairs={{0,1},{1,0},{2,3},{3,2},{4,5},{5,4},{6,7},{7,6},{8,9},{9,8},{10,11... | collective-permute-start | bytes 1966088 | tf_op jit(solution)/shard_map/ppermute | solution.py:234
  59.0 21.4 %all-to-all-start.1 = ((bf16[8,320,128]{2,1,0:T(8,128)(2,1)}), bf16[8,320,128]{2,1,0:T(8,128)(2,1)S(1)}, u32[]{:S(2)}, u32[]{:S(2)}) async-start(bf16[8,320,128]{2,1,0:T(8,128)(2,1)} %shard_map.70), calls=%async_computation.1 | async-start | bytes 1310720 | tf_op jit(solution)/shard_map/all_to_all | solution.py:239
  64.0 4.0 %collective-permute-start.2 = (bf16[8,320,128]{2,1,0:T(8,128)(2,1)S(1)}, bf16[8,320,128]{2,1,0:T(8,128)(2,1)S(1)}, u32[]{:S(2)}, u32[]{:S(2)}) collective-permute-start(bf16[8,320,128]{2,1,0:T(8,128)(2,1)S(1)} %all-to-all-done.own_ref), channel_id=1, source_target_pairs={{0,1},{1,0},{2,3},{3,2},{4,5},{5,4},{6,7},{7,6},{8,9},{9,8},{10,11... | collective-permute-start | bytes 1966088 | tf_op jit(solution)/shard_map/ppermute | solution.py:240
  69.3 20.1 %collective-permute-start.3 = (bf16[4,128,256]{2,1,0:T(8,128)(2,1)S(1)}, bf16[4,128,256]{2,1,0:T(8,128)(2,1)S(1)}, u32[]{:S(2)}, u32[]{:S(2)}) collective-permute-start(bf16[4,128,256]{2,1,0:T(8,128)(2,1)S(1)} %shard_map.72.one_ref), channel_id=1, source_target_pairs={{0,16},{16,0},{32,48},{48,32},{1,17},{17,1},{33,49},{49,33},{2,18}... | collective-permute-start | bytes 786440 | tf_op jit(solution)/shard_map/ppermute | solution.py:261
  80.5 22.9 %all-to-all-start.2 = ((bf16[8,32,1280]{2,1,0:T(8,128)(2,1)}), bf16[8,32,1280]{2,1,0:T(8,128)(2,1)S(1)}, u32[]{:S(2)}, u32[]{:S(2)}) async-start(bf16[8,32,1280]{2,1,0:T(8,128)(2,1)} %bitcast.7), calls=%async_computation.2 | async-start | bytes 1310720 | tf_op jit(solution)/shard_map/all_to_all | solution.py:264
  89.4 20.1 %collective-permute-start.5 = (bf16[4,128,256]{2,1,0:T(8,128)(2,1)S(1)}, bf16[4,128,256]{2,1,0:T(8,128)(2,1)S(1)}, u32[]{:S(2)}, u32[]{:S(2)}) collective-permute-start(bf16[4,128,256]{2,1,0:T(8,128)(2,1)S(1)} %shard_map.74.refs_2_), channel_id=1, source_target_pairs={{0,48},{16,32},{32,16},{48,0},{1,49},{17,33},{33,17},{49,1},{2,50}... | collective-permute-start | bytes 786440 | tf_op jit(solution)/shard_map/ppermute | solution.py:279
  92.5 22.0 %collective-permute-start.4 = (bf16[320,128]{1,0:T(8,128)(2,1)S(1)}, bf16[320,128]{1,0:T(8,128)(2,1)S(1)}, u32[]{:S(2)}, u32[]{:S(2)}) collective-permute-start(bf16[320,128]{1,0:T(8,128)(2,1)S(1)} %shard_map.73), channel_id=1, source_target_pairs={{0,32},{2,34},{4,16},{6,18},{8,0},{10,2},{12,48},{14,50},{16,4},{1... | collective-permute-start | bytes 245768 | tf_op jit(solution)/shard_map/ppermute | solution.py:272
  104.3 14.6 %all-to-all-start.3 = ((bf16[8,32,1280]{2,1,0:T(8,128)(2,1)}), bf16[8,32,1280]{2,1,0:T(8,128)(2,1)S(1)}, u32[]{:S(2)}, u32[]{:S(2)}) async-start(bf16[8,32,1280]{2,1,0:T(8,128)(2,1)} %broadcast_in_dim.5), calls=%async_computation.3 | async-start | bytes 1310720 | tf_op jit(solution)/shard_map/all_to_all | solution.py:283
  114.5 0.9 copy-start.1

commit v7 on v5

--- a/solution.py
+++ b/solution.py
@@ -75,20 +75,32 @@
             pieces_ref[at] = piece.astype(BF16)
 
 
-def attended_grad_kernel(place_ref, weight_ref, own_ref, other_ref, out_ref):
+def share_own_kernel(place_ref, weight_ref, own_ref, out_ref):
     n, halves = out_ref.shape[0], weight_ref.shape[0]
-    core = place_ref[1]
     for frame in range(n):
         total = None
         for half in range(halves):
-            for grads, at in ((own_ref, core), (other_ref, 1 - core)):
-                term = lax.dot_general(
-                    grads[slot(place_ref, frame, n) * halves + half],
-                    weight_ref[half, at],
-                    (((0,), (0,)), ((), ())),
-                    preferred_element_type=F32,
-                )
-                total = term if total is None else total + term
+            term = lax.dot_general(
+                own_ref[slot(place_ref, frame, n) * halves + half],
+                weight_ref[half, place_ref[1]],
+                (((0,), (0,)), ((), ())),
+                preferred_element_type=F32,
+            )
+            total = term if total is None else total + term
+        out_ref[frame] = total
+
+
+def share_other_kernel(place_ref, weight_ref, other_ref, first_ref, out_ref):
+    n, halves = out_ref.shape[0], weight_ref.shape[0]
+    for frame in range(n):
+        total = first_ref[frame]
+        for half in range(halves):
+            total = total + lax.dot_general(
+                other_ref[slot(place_ref, frame, n) * halves + half],
+                weight_ref[half, 1 - place_ref[1]],
+                (((0,), (0,)), ((), ())),
+                preferred_element_type=F32,
+            )
         out_ref[frame] = total.astype(BF16)
 
 
@@ -231,13 +243,21 @@
     grad_other = lax.ppermute(grad_own, "core", SWAP)
 
     share = whole(
-        attended_grad_kernel,
+        share_own_kernel,
+        jax.ShapeDtypeStruct((n_frame, tokens, inner), F32),
+        place,
+        weight_t,
+        grad_own,
+        flops=product,
+    )
+    share = whole(
+        share_other_kernel,
         jax.ShapeDtypeStruct((n_frame, tokens, inner), BF16),
         place,
         weight_t,
-        grad_own,
         grad_other,
-        flops=2 * product,
+        share,
+        flops=product,
     )
     weight_part = whole(
         weight_grad_kernel,

time: 116 us -> 116 us (level)
    pallas_call x5 -> x6, Pallas kernels: 11.4 us -> 12.2 us  [whole(): pl.pallas_call(kernel, out_shape=out_shape, in_specs=[pl.BlockSpec(memory...]
  transfers between devices with their start and end apart: 10 -> 10, of which waited for: 6 -> 6; matrix products, arithmetic and copies ran while one was open for 2% -> 2% of each run, Pallas kernels for 12% -> 13%
where the time goes in v7:
time: 116 us; the launch traced here: 115 us
  starting transfers between devices  49.3 us (42%)
  blocking collectives  23.5 us (20%)
  waiting for transfers between devices  21.1 us (18%)
  Pallas kernels  15 us (13%)
  local copies, waits for them, and re-layouts  4.79 us (4%)
    all_gather x1, blocking collectives, local(): lax.all_gather(projections.reshape(projections.shape[1:]).transpose(0, 2,...  23.5 us
    pallas_call x6, Pallas kernels, whole(): pl.pallas_call(kernel, out_shape=out_shape, in_specs=[pl.BlockSpec(memory...  12.2 us
    all_to_all x1, starting transfers between devices, local(): grad_own = lax.all_to_all(copies(grad_moved, n_y), 'y', 0, 0, tiled=True)  8.85 us
    all_to_all x1, waiting for transfers between devices, local(): grad_own = lax.all_to_all(copies(grad_moved, n_y), 'y', 0, 0, tiled=True)  7.32 us
    ppermute x1, starting transfers between devices, local(): projected = lax.ppermute(projected, ('frame', 'y'), there)  7.2 us
    all_to_all x1, starting transfers between devices, local(): weight_part = lax.all_to_all(weight_part, CLIP, 0, 0, tiled=True)  7 us
    ppermute x1, starting transfers between devices, local(): lax.ppermute(out_grad.reshape(tokens, width).T, ('frame', 'y'), back)  6.83 us
    all_to_all x1, waiting for transfers between devices, local(): pieces = lax.all_to_all(pieces, 'y', 0, 0, tiled=True)  6.07 us
  transfers between devices with their start and end apart: 10, of which 6 were waited for; matrix products, arithmetic and copies ran while one was open for 2% of the time, Pallas kernels for 13%

profile of v7, /device:TPU:8, one launch (start us, length us, event | category | flops | bytes accessed | tf_op | source)
XLA Modules:
  0.0 115.4 jit_solution(10745318743762478241)
XLA Ops:
  0.6 1.0 copy.13
  1.6 6.8 %collective-permute-start = (bf16[320,128]{1,0:T(8,128)(2,1)S(1)}, bf16[320,128]{1,0:T(8,128)(2,1)S(1)}, u32[]{:S(2)}, u32[]{:S(2)}) collective-permute-start(bf16[320,128]{1,0:T(8,128)(2,1)S(1)} %bitcast.26), channel_id=1, source_target_pairs={{32,0},{34,2},{16,4},{18,6},{0,8},{2,10},{48,12},{50,14},{4,16},{6... | collective-permute-start | bytes 245768 | tf_op jit(solution)/shard_map/ppermute | solution.py:217
  8.5 23.5 %all_gather.3.all_ref.refs_1_ = bf16[16,3,32,256]{3,2,1,0:T(8,128)(2,1)S(1)} all-gather(bf16[4,3,32,256]{3,2,1,0:T(8,128)(2,1)} %bitcast.24), channel_id=1, replica_groups=mesh['x'=4,'zl'=2,'frame'=4,'y'=8,'core'=2] {'frame'}, dimensions={0}, use_global_device_ids=true | all-gather | bytes 983040 | tf_op jit(solution)/shard_map/all_gather | solution.py:218
  32.0 0.0 collective-permute-done
  32.0 0.9 broadcast_in_dim.4
  32.9 0.0 copy-start
  33.0 8.9 %all-to-all-start = ((bf16[8,320,128]{2,1,0:T(8,128)(2,1)}), bf16[8,320,128]{2,1,0:T(8,128)(2,1)S(1)}, u32[]{:S(2)}, u32[]{:S(2)}) async-start(bf16[8,320,128]{2,1,0:T(8,128)(2,1)} %broadcast_in_dim.4), calls=%async_computation | async-start | bytes 1310720 | tf_op jit(solution)/shard_map/all_to_all | solution.py:222
  41.8 0.0 copy-done
  41.8 0.2 copy.14
  42.0 0.1 pad_add_fusion.place_ref.refs_0_
  42.1 2.7 %shard_map.67.rows_ref = bf16[4,128,256]{2,1,0:T(8,128)(2,1)S(1)} custom-call(bf16[16,3,32,256]{3,2,1,0:T(8,128)(2,1)S(1)} %all_gather.3.all_ref.refs_1_), custom_call_target="tpu_custom_call" | custom-call | flops 167772160 | bytes 4194304 | tf_op jit(solution)/shard_map/pallas_call | solution.py:224
  44.8 0.9 shard_map.68
  45.7 1.9 %collective-permute-start.1 = (bf16[8,320,128]{2,1,0:T(8,128)(2,1)S(1)}, bf16[8,320,128]{2,1,0:T(8,128)(2,1)S(1)}, u32[]{:S(2)}, u32[]{:S(2)}) collective-permute-start(bf16[8,320,128]{2,1,0:T(8,128)(2,1)S(1)} %shard_map.68), channel_id=1, source_target_pairs={{0,1},{1,0},{2,3},{3,2},{4,5},{5,4},{6,7},{7,6},{8,9},{9,8},{10,11... | collective-permute-start | bytes 1966088 | tf_op jit(solution)/shard_map/ppermute | solution.py:237
  47.7 2.1 %collective-permute-done.1.got_ref = bf16[8,320,128]{2,1,0:T(8,128)(2,1)S(1)} collective-permute-done((bf16[8,320,128]{2,1,0:T(8,128)(2,1)S(1)}, bf16[8,320,128]{2,1,0:T(8,128)(2,1)S(1)}, u32[]{:S(2)}, u32[]{:S(2)}) %collective-permute-start.1) | collective-permute-done | bytes 655392 | tf_op jit(solution)/shard_map/ppermute | solution.py:237
  49.7 1.7 %shard_map.69 = bf16[8,320,128]{2,1,0:T(8,128)(2,1)} custom-call(s32[2]{0:T(128)S(1)} %pad_add_fusion.place_ref.refs_0_, bf16[2,2,320,256]{3,2,1,0:T(8,128)(2,1)S(1)} %bitcast.18, bf16[4,128,256]{2,1,0:T(8,128)(2,1)S(1)} %shard_map.67.rows_ref, bf16[8,320,128]{2,1,0:T(8,128)(2,1)S(1)} %collective-permute-done.1.got_ref), custom_call_target="tpu_custom_call" | custom-call | flops 167772160 | bytes 3145728 | tf_op jit(solution)/shard_map/pallas_call | solution.py:172
  51.5 7.3 %all-to-all-done.own_ref = bf16[8,320,128]{2,1,0:T(8,128)(2,1)S(1)} async-done(((bf16[8,320,128]{2,1,0:T(8,128)(2,1)}), bf16[8,320,128]{2,1,0:T(8,128)(2,1)S(1)}, u32[]{:S(2)}, u32[]{:S(2)}) %all-to-all-start) | async-done | bytes 655392 | tf_op jit(solution)/shard_map/all_to_all | solution.py:222
  58.8 5.0 %all-to-all-start.1 = ((bf16[8,320,128]{2,1,0:T(8,128)(2,1)}), bf16[8,320,128]{2,1,0:T(8,128)(2,1)S(1)}, u32[]{:S(2)}, u32[]{:S(2)}) async-start(bf16[8,320,128]{2,1,0:T(8,128)(2,1)} %shard_map.69), calls=%async_computation.1 | async-start | bytes 1310720 | tf_op jit(solution)/shard_map/all_to_all | solution.py:242
  63.7 1.9 %collective-permute-start.2 = (bf16[8,320,128]{2,1,0:T(8,128)(2,1)S(1)}, bf16[8,320,128]{2,1,0:T(8,128)(2,1)S(1)}, u32[]{:S(2)}, u32[]{:S(2)}) collective-permute-start(bf16[8,320,128]{2,1,0:T(8,128)(2,1)S(1)} %all-to-all-done.own_ref), channel_id=1, source_target_pairs={{0,1},{1,0},{2,3},{3,2},{4,5},{5,4},{6,7},{7,6},{8,9},{9,8},{10,11... | collective-permute-start | bytes 1966088 | tf_op jit(solution)/shard_map/ppermute | solution.py:243
  65.6 1.0 shard_map.71.first_ref
  66.7 1.0 collective-permute-done.2.other_ref
  67.7 1.0 shard_map.72.one_ref
  68.8 2.9 %collective-permute-start.3 = (bf16[4,128,256]{2,1,0:T(8,128)(2,1)S(1)}, bf16[4,128,256]{2,1,0:T(8,128)(2,1)S(1)}, u32[]{:S(2)}, u32[]{:S(2)}) collective-permute-start(bf16[4,128,256]{2,1,0:T(8,128)(2,1)S(1)} %shard_map.72.one_ref), channel_id=1, source_target_pairs={{0,16},{16,0},{32,48},{48,32},{1,17},{17,1},{33,49},{49,33},{2,18}... | collective-permute-start | bytes 786440 | tf_op jit(solution)/shard_map/ppermute | solution.py:272
  71.7 2.5 %shard_map.70 = bf16[256,1280]{1,0:T(8,128)(2,1)} custom-call(s32[2]{0:T(128)S(1)} %pad_add_fusion.place_ref.refs_0_, bf16[4,128,256]{2,1,0:T(8,128)(2,1)S(1)} %shard_map.67.rows_ref, bf16[8,320,128]{2,1,0:T(8,128)(2,1)S(1)} %all-to-all-done.own_ref, bf16[8,320,128]{2,1,0:T(8,128)(2,1)S(1)} %collective-permute-done.2.other_ref), custom_call_target="tpu_custom_call" | custom-call | flops 335544320 | bytes 3145728 | tf_op jit(solution)/shard_map/pallas_call | solution.py:172
  74.2 6.1 %all-to-all-done.1.parts_ref = bf16[8,320,128]{2,1,0:T(8,128)(2,1)S(1)} async-done(((bf16[8,320,128]{2,1,0:T(8,128)(2,1)}), bf16[8,320,128]{2,1,0:T(8,128)(2,1)S(1)}, u32[]{:S(2)}, u32[]{:S(2)}) %all-to-all-start.1) | async-done | bytes 655392 | tf_op jit(solution)/shard_map/all_to_all | solution.py:242
  80.2 7.0 %all-to-all-start.2 = ((bf16[8,32,1280]{2,1,0:T(8,128)(2,1)}), bf16[8,32,1280]{2,1,0:T(8,128)(2,1)S(1)}, u32[]{:S(2)}, u32[]{:S(2)}) async-start(bf16[8,32,1280]{2,1,0:T(8,128)(2,1)} %bitcast.8), calls=%async_computation.2 | async-start | bytes 1310720 | tf_op jit(solution)/shard_map/all_to_all | solution.py:275
  87.2 0.1 shard_map.73
  87.3 0.0 collective-permute-done.3.two_ref
  87.3 0.1 shard_map.74.refs_2_
  87.4 2.7 %collective-permute-start.5 = (bf16[4,128,256]{2,1,0:T(8,128)(2,1)S(1)}, bf16[4,128,256]{2,1,0:T(8,128)(2,1)S(1)}, u32[]{:S(2)}, u32[]{:S(2)}) collective-permute-start(bf16[4,128,256]{2,1,0:T(8,128)(2,1)S(1)} %shard_map.74.refs_2_), channel_id=1, source_target_pairs={{0,48},{16,32},{32,16},{48,0},{1,49},{17,33},{33,17},{49,1},{2,50}... | collective-permute-start | bytes 786440 | tf_op jit(solution)/shard_map/ppermute | solution.py:290
  90.1 7.2 %collective-permute-start.4 = (bf16[320,128]{1,0:T(8,128)(2,1)S(1)}, bf16[320,128]{1,0:T(8,128)(2,1)S(1)}, u32[]{:S(2)}, u32[]{:S(2)}) collective-permute-start(bf16[320,128]{1,0:T(8,128)(2,1)S(1)} %shard_map.73), channel_id=1, source_target_pairs={{0,32},{2,34},{4,16},{6,18},{8,0},{10,2},{12,48},{14,50},{16,4},{1... | collective-permute-start | bytes 245768 | tf_op jit(solution)/shard_map/ppermute | solution.py:283
  97.4 1.8 %all-to-all-done.2 = bf16[8,32,1280]{2,1,0:T(8,128)(2,1)S(1)} async-done(((bf16[8,32,1280]{2,1,0:T(8,128)(2,1)}), bf16[8,32,1280]{2,1,0:T(8,128)(2,1)S(1)}, u32[]{:S(2)}, u32[]{:S(2)}) %all-to-all-start.2) | async-done | bytes 655392 | tf_op jit(solution)/shard_map/all_to_all | solution.py:275
  99.2 0.1 reduce_sum.12
  99.3 0.9 broadcast_in_dim.5
  100.1 5.0 %all-to-all-start.3 = ((bf16[8,32,1280]{2,1,0:T(8,128)(2,1)}), bf16[8,32,1280]{2,1,0:T(8,128)(2,1)S(1)}, u32[]{:S(2)}, u32[]{:S(2)}) async-start(bf16[8,32,1280]{2,1,0:T(8,128)(2,1)} %broadcast_in_dim.5), calls=%async_computation.3 | async-start | bytes 1310720 | tf_op jit(solution)/shard_map/all_to_all | solution.py:294
  105.2 0.0 collective-permute-done.5.refs_3_
  105.2 5.0 %shard_map.75 = bf16[4,3,32,256]{3,2,1,0:T(8,128)(2,1)} custom-call(s32[2]{0:T(128)S(1)} %pad_add_fusion.place_ref.refs_0_, bf16[16,3,32,256]{3,2,1,0:T(8,128)(2,1)S(1)} %all_gather.3.all_ref.refs_1_, bf16[4,128,256]{2,1,0:T(8,128)(2,1)S(1)} %shard_map.74.refs_2_, bf16[4,128,256]{2,1,0:T(8,128)(2,1)S(1)} %collective-permute-done.5.refs_3_), custom_call_target="tpu_custom_call" | custom-call | flops 67108864000 | bytes 2621440 | tf_op jit(solution)/shard_map/pallas_call | solution.py:172
  110.2 0.0 collective-permute-done.4
  110.2 0.0 copy-start.1
  110.2 0.1 copy.15
  110.3 0.8 copy-done.1
  111.1 0.7 add_convert_fusion
  111.7 2.8 %all-to-all-done.3 = bf16[8,32,1280]{2,1,0:T(8,128)(2,1)S(1)} async-done(((bf16[8,32,1280]{2,1,0:T(8,128)(2,1)}), bf16[8,32,1280]{2,1,0:T(8,128)(2,1)S(1)}, u32[]{:S(2)}, u32[]{:S(2)}) %all-to-all-start.3) | async-done | bytes 655392 | tf_op jit(solution)/shard_map/all_to_all | solution.py:294
  114.6 0.8 copy.17
  (1 shorter events, 0.0 us)
Async XLA Ops:
  1.6 30.4 %collective-permute-start = (bf16[320,128]{1,0:T(8,128)(2,1)S(1)}, bf16[320,128]{1,0:T(8,128)(2,1)S(1)}, u32[]{:S(2)}, u32[]{:S(2)}) collective-permute-start(bf16[320,128]{1,0:T(8,128)(2,1)S(1)} %bitcast.26), channel_id=1, source_target_pairs={{32,0},{34,2},{16,4},{18,6},{0,8},{2,10},{48,12},{50,14},{4,16},{6... | collective-permute-start | bytes 245768 | tf_op jit(solution)/shard_map/ppermute | solution.py:217
  32.9 8.9 %copy-start = (bf16[256,1280]{1,0:T(8,128)(2,1)S(1)}, bf16[256,1280]{1,0:T(8,128)(2,1)}, u32[]{:S(2)}) copy-start(bf16[256,1280]{1,0:T(8,128)(2,1)} %param.6) | copy-start | bytes 1966084
  33.0 25.8 %all-to-all-start = ((bf16[8,320,128]{2,1,0:T(8,128)(2,1)}), bf16[8,320,128]{2,1,0:T(8,128)(2,1)S(1)}, u32[]{:S(2)}, u32[]{:S(2)}) async-start(bf16[8,320,128]{2,1,0:T(8,128)(2,1)} %broadcast_in_dim.4), calls=%async_computation | async-start | bytes 1310720 | tf_op jit(solution)/shard_map/all_to_all | solution.py:222
  45.7 4.0 %collective-permute-start.1 = (bf16[8,320,128]{2,1,0:T(8,128)(2,1)S(1)}, bf16[8,320,128]{2,1,0:T(8,128)(2,1)S(1)}, u32[]{:S(2)}, u32[]{:S(2)}) collective-permute-start(bf16[8,320,128]{2,1,0:T(8,128)(2,1)S(1)} %shard_map.68), channel_id=1, source_target_pairs={{0,1},{1,0},{2,3},{3,2},{4,5},{5,4},{6,7},{7,6},{8,9},{9,8},{10,11... | collective-permute-start | bytes 1966088 | tf_op jit(solution)/shard_map/ppermute | solution.py:237
  58.8 21.5 %all-to-all-start.1 = ((bf16[8,320,128]{2,1,0:T(8,128)(2,1)}), bf16[8,320,128]{2,1,0:T(8,128)(2,1)S(1)}, u32[]{:S(2)}, u32[]{:S(2)}) async-start(bf16[8,320,128]{2,1,0:T(8,128)(2,1)} %shard_map.69), calls=%async_computation.1 | async-start | bytes 1310720 | tf_op jit(solution)/shard_map/all_to_all | solution.py:242
  63.7 4.0 %collective-permute-start.2 = (bf16[8,320,128]{2,1,0:T(8,128)(2,1)S(1)}, bf16[8,320,128]{2,1,0:T(8,128)(2,1)S(1)}, u32[]{:S(2)}, u32[]{:S(2)}) collective-permute-start(bf16[8,320,128]{2,1,0:T(8,128)(2,1)S(1)} %all-to-all-done.own_ref), channel_id=1, source_target_pairs={{0,1},{1,0},{2,3},{3,2},{4,5},{5,4},{6,7},{7,6},{8,9},{9,8},{10,11... | collective-permute-start | bytes 1966088 | tf_op jit(solution)/shard_map/ppermute | solution.py:243
  68.8 18.6 %collective-permute-start.3 = (bf16[4,128,256]{2,1,0:T(8,128)(2,1)S(1)}, bf16[4,128,256]{2,1,0:T(8,128)(2,1)S(1)}, u32[]{:S(2)}, u32[]{:S(2)}) collective-permute-start(bf16[4,128,256]{2,1,0:T(8,128)(2,1)S(1)} %shard_map.72.one_ref), channel_id=1, source_target_pairs={{0,16},{16,0},{32,48},{48,32},{1,17},{17,1},{33,49},{49,33},{2,18}... | collective-permute-start | bytes 786440 | tf_op jit(solution)/shard_map/ppermute | solution.py:272
  80.2 18.9 %all-to-all-start.2 = ((bf16[8,32,1280]{2,1,0:T(8,128)(2,1)}), bf16[8,32,1280]{2,1,0:T(8,128)(2,1)S(1)}, u32[]{:S(2)}, u32[]{:S(2)}) async-start(bf16[8,32,1280]{2,1,0:T(8,128)(2,1)} %bitcast.8), calls=%async_computation.2 | async-start | bytes 1310720 | tf_op jit(solution)/shard_map/all_to_all | solution.py:275
  87.4 17.7 %collective-permute-start.5 = (bf16[4,128,256]{2,1,0:T(8,128)(2,1)S(1)}, bf16[4,128,256]{2,1,0:T(8,128)(2,1)S(1)}, u32[]{:S(2)}, u32[]{:S(2)}) collective-permute-start(bf16[4,128,256]{2,1,0:T(8,128)(2,1)S(1)} %shard_map.74.refs_2_), channel_id=1, source_target_pairs={{0,48},{16,32},{32,16},{48,0},{1,49},{17,33},{33,17},{49,1},{2,50}... | collective-permute-start | bytes 786440 | tf_op jit(solution)/shard_map/ppermute | solution.py:290
  90.1 20.0 %collective-permute-start.4 = (bf16[320,128]{1,0:T(8,128)(2,1)S(1)}, bf16[320,128]{1,0:T(8,128)(2,1)S(1)}, u32[]{:S(2)}, u32[]{:S(2)}) collective-permute-start(bf16[320,128]{1,0:T(8,128)(2,1)S(1)} %shard_map.73), channel_id=1, source_target_pairs={{0,32},{2,34},{4,16},{6,18},{8,0},{10,2},{12,48},{14,50},{16,4},{1... | collective-permute-start | bytes 245768 | tf_op jit(solution)/shard_map/ppermute | solution.py:283
  100.1 14.4 %all-to-all-start.3 = ((bf16[8,32,1280]{2,1,0:T(8,128)(2,1)}), bf16[8,32,1280]{2,1,0:T(8,128)(2,1)S(1)}, u32[]{:S(2)}, u32[]{:S(2)}) async-start(bf16[8,32,1280]{2,1,0:T(8,128)(2,1)} %broadcast_in_dim.5), calls=%async_computation.3 | async-start | bytes 1310720 | tf_op jit(solution)/shard_map/all_to_all | solution.py:294
  110.2 0.9 copy-start.1
